TPU v7x, 512 devices: a whole 4x8x8 slice. The times are simulated.
512 devices in a mesh: depth: 32 (over z_lo, y), height: 2 (over z_hi), view: 8 (over x, core).
Axes of the slice: x: 4, y: 8, z: 8 (z_hi: 2, z_lo: 4; z = z_hi * 4 + z_lo), core: 2. Of those that a mesh axis runs over, the one named last changes fastest.
Arguments:
- camera_feats: bfloat16 [4096, 16, 128], P(('depth', 'height', 'view')), may hold values from -6 to 6
- footprint_slot_weights: bfloat16 [8, 128, 128], replicated, may hold values from -0.1875 to 0.1875
- tile_bricks: int32 [4096, 8], P(('depth', 'height', 'view')), may hold values from 0 to 7
- tile_rows: int32 [4096, 8], P(('depth', 'height', 'view')), may hold values from 0 to 7
- conv_first: bfloat16 [16, 16, 3, 3, 3], replicated, may hold values from -0.3125 to 0.3125
- conv_second: bfloat16 [16, 16, 3, 3, 3], replicated, may hold values from -0.3125 to 0.3125
- conv_third: bfloat16 [16, 16, 3, 3, 3], replicated, may hold values from -0.3125 to 0.3125
- bias_first: float32 [16], replicated, may hold values from -3 to 3
- bias_second: float32 [16], replicated, may hold values from -3 to 3
- out_grad: bfloat16 [256, 16, 16, 128], P(('depth', 'view'), 'height'), may hold values from -6 to 6
Outputs:
- field: bfloat16 [256, 16, 16, 128], P(('depth', 'view'), 'height')
- camera_tile_feature_gradient: float32 [4096, 16, 128], P(('depth', 'height', 'view'))
- weight_grads: float32 [3, 16, 16, 3, 3, 3], replicated
- bias_gradient_pair: float32 [2, 16], replicated
All inputs are finite; a program needn't handle non-finite values.
Results may differ from a plain program's by a relative error of at most 0.017.
Values may be sent and summed in bfloat16 or wider, within the bound.
No kernel may reach another device: no remote copies, remote signals or barrier semaphores. Data moves between devices by JAX's collectives and lax.ppermute only.
A program may use at most 64 MiB of HBM per device.

v0:
```python
import math

import jax
import jax.numpy as jnp
from jax import lax
from jax.sharding import PartitionSpec as P

C = 16
XB = 128
ZP = 1
CX = 128
CY = 8


conv_layout = ("NDHCW", "OIDHW", "NDHCW")
grad_layout = ("CDHNW", "IDHOW", "CNDHW")


def extended(block, sides, width):
    for axis, dim in sides:
        count = lax.axis_size(axis)
        forward = [(i, i + 1) for i in range(count - 1)]
        backward = [(target, source) for source, target in forward]
        low = lax.ppermute(
            lax.slice_in_dim(block, block.shape[dim] - width, None, axis=dim), axis, forward
        )
        high = lax.ppermute(lax.slice_in_dim(block, 0, width, axis=dim), axis, backward)
        block = jnp.concatenate([low, block, high], axis=dim)
    return block


def split_up(shard, dim, peers):
    before, after = (shard.shape[:dim], shard.shape[dim + 1 :])
    return jnp.moveaxis(shard.reshape(*before, peers, -1, *after), dim, 0)


def summed_on_arrival(shard, axis, dim):
    tiles = split_up(shard, dim, lax.axis_size(axis))
    arrived = lax.all_to_all(tiles, axis, split_axis=0, concat_axis=0, tiled=True)
    return arrived.astype(jnp.float32).sum(axis=0)


def together(arrays, axis):
    flat, at, gathered = (jnp.concatenate([a.reshape(-1) for a in arrays]), 0, [])
    subtotal = lax.psum(flat, axis)
    for a in arrays:
        gathered.append(subtotal[at : at + a.size].reshape(a.shape))
        at += a.size
    return tuple(gathered)


def copy_for_each(shard, axis):
    peers = lax.axis_size(axis)
    return lax.all_to_all(
        jnp.broadcast_to(shard[None], (peers, *shard.shape)), axis, 0, 0, tiled=True
    )


def in_order(tiles, dim):
    shape = list(tiles.shape[1:])
    shape[dim] *= tiles.shape[0]
    return jnp.moveaxis(tiles, 0, dim).reshape(shape)


def gathered_copies(shard, axis, dim):
    tiles = copy_for_each(shard, axis)
    return in_order(tiles, dim)


def with_rim(volume):
    padded = extended(volume, ((("depth", "view"), 0), ("height", 1)), 1)
    return jnp.pad(padded, ((0, 0), (0, 0), (0, 0), (1, 1)))


def conv_valid(padded, weight):
    result = lax.conv_general_dilated(
        padded[None],
        weight,
        (1, 1, 1),
        ((0, 0), (0, 0), (0, 0)),
        dimension_numbers=conv_layout,
        preferred_element_type=jnp.float32,
    )
    return result[0]


def flip_swap(weight):
    return jnp.transpose(jnp.flip(weight, (2, 3, 4)), (1, 0, 2, 3, 4))


def weight_grad(grad_out, padded):
    return lax.conv_general_dilated(
        padded[None],
        grad_out[None],
        (1, 1, 1),
        ((0, 0), (0, 0), (0, 0)),
        dimension_numbers=grad_layout,
        preferred_element_type=jnp.float32,
    )


def silu_grad(values):
    sigma = jax.nn.sigmoid(values)
    return sigma * (1.0 + values * (1.0 - sigma))


def body(
    camera_feats,
    footprint_slot_weights,
    tile_bricks,
    tile_rows,
    conv_first,
    conv_second,
    conv_third,
    bias_first,
    bias_second,
    out_grad,
):
    views = lax.axis_size("view")
    block_count = CX // XB
    plane_rows = tile_bricks * (ZP * CY) + tile_rows // block_count
    blocks = tile_rows % block_count
    partial_value = jnp.zeros((views * ZP * CY, C, block_count, XB), jnp.float32)
    contrib = jnp.einsum(
        "tcp,kxp->tkcx", camera_feats, footprint_slot_weights, preferred_element_type=jnp.float32
    )
    partial_value = partial_value.at[plane_rows, :, blocks, :].add(contrib)
    partial_value = partial_value.reshape(views * ZP, CY, C, CX)
    lifted = summed_on_arrival(partial_value.astype(jnp.bfloat16), "view", 0).astype(jnp.bfloat16)
    lifted_pad = with_rim(lifted)
    pre_first = conv_valid(lifted_pad, conv_first) + bias_first[None, None, :, None]
    act_first = jax.nn.silu(pre_first).astype(jnp.bfloat16)
    leading_padding = with_rim(act_first)
    pre_second = conv_valid(leading_padding, conv_second) + bias_second[None, None, :, None]
    act_second = (jax.nn.silu(pre_second) + act_first.astype(jnp.float32)).astype(jnp.bfloat16)
    second_pad = with_rim(act_second)
    field_local = conv_valid(second_pad, conv_third).astype(jnp.bfloat16)
    voxels = ZP * CY * CX * lax.axis_size("depth") * lax.axis_size("height") * views
    scale = 1.0 / math.sqrt(voxels)
    padded_gradient_border = with_rim(out_grad)
    third_term = weight_grad(out_grad, second_pad)
    up_second = conv_valid(padded_gradient_border, flip_swap(conv_third))
    slope_second = up_second * silu_grad(pre_second)
    back_second = slope_second.astype(jnp.bfloat16)
    back_second_pad = with_rim(back_second)
    second_term = weight_grad(back_second, leading_padding)
    bias_later_layer = jnp.sum(slope_second, axis=(0, 1, 3))
    up_first = up_second + conv_valid(back_second_pad, flip_swap(conv_second))
    slope_first = up_first * silu_grad(pre_first)
    back_first = slope_first.astype(jnp.bfloat16)
    back_first_pad = with_rim(back_first)
    leading_summand = weight_grad(back_first, lifted_pad)
    first_bias = jnp.sum(slope_first, axis=(0, 1, 3))
    leading_summand, second_term, third_term, first_bias, bias_later_layer = together(
        (leading_summand, second_term, third_term, first_bias, bias_later_layer),
        ("depth", "height", "view"),
    )
    lift_grad = conv_valid(back_first_pad, flip_swap(conv_first)).astype(jnp.bfloat16)
    region_grad = gathered_copies(lift_grad, "view", 0)
    grid = region_grad.reshape(views * ZP * CY, C, block_count, XB)
    chosen_table_entries = grid[plane_rows, :, blocks, :]
    camera_tile_feature_gradient = jnp.einsum(
        "tkcx,kxp->tcp",
        chosen_table_entries,
        footprint_slot_weights,
        preferred_element_type=jnp.float32,
    )
    weight_grads = jnp.stack([leading_summand, second_term, third_term]) * scale
    bias_gradient_pair = jnp.stack([first_bias, bias_later_layer]) * scale
    return (field_local, camera_tile_feature_gradient, weight_grads, bias_gradient_pair)


def solution(mesh):
    in_specs = (
        P(("depth", "height", "view"), None, None),
        P(),
        P(("depth", "height", "view"), None),
        P(("depth", "height", "view"), None),
        P(),
        P(),
        P(),
        P(),
        P(),
        P(("depth", "view"), "height", None, None),
    )
    out_specs = (
        P(("depth", "view"), "height", None, None),
        P(("depth", "height", "view"), None, None),
        P(),
        P(),
    )
    return jax.shard_map(body, mesh=mesh, in_specs=in_specs, out_specs=out_specs, check_vma=False)
```

profile of v0, /device:TPU:1, one launch (start us, length us, event | category | flops | bytes accessed | tf_op | source)
XLA Modules:
  0.0 508.1 jit_solution(10279451132535471395)
XLA Ops:
  7.2 4.6 collective-permute-start.12
  11.8 5.6 %collective-permute-start.13 = (bf16[1,8,16,128]{3,2,1,0:T(8,128)(2,1)}, bf16[1,8,16,128]{3,2,1,0:T(8,128)(2,1)S(1)}, u32[]{:S(2)}, u32[]{:S(2)}) collective-permute-start(bf16[1,8,16,128]{3,2,1,0:T(8,128)(2,1)} %param.19), channel_id=1, source_target_pairs={{1,0},{2,1},{3,2},{4,3},{5,4},{6,5},{7,6},{16,7},{17,16},{18,17},{... | collective-permute-start | bytes 98312 | tf_op jit(solution)/shard_map/ppermute | solution.py:27
  19.3 2.9 scatter_fusion
  22.9 3.4 all-to-all-start
  27.7 8.5 %collective-permute-start.14 = (bf16[3,1,16,128]{3,2,1,0:T(8,128)(2,1)S(1)}, bf16[3,1,16,128]{3,2,1,0:T(8,128)(2,1)S(1)}, u32[]{:S(2)}, u32[]{:S(2)}) collective-permute-start(bf16[3,1,16,128]{3,2,1,0:T(8,128)(2,1)S(1)} %get-tuple-element.31), channel_id=1, source_target_pairs={{0,8},{1,9},{2,10},{3,11},{4,12},{5,13},{6,14},{7,15},{16,24},{17,... | collective-permute-start | bytes 36872 | tf_op jit(solution)/shard_map/ppermute | solution.py:24
  39.7 3.5 collective-permute-start
  47.3 7.9 %collective-permute-start.2 = (bf16[3,1,16,128]{3,2,1,0:T(8,128)(2,1)S(1)}, bf16[3,1,16,128]{3,2,1,0:T(8,128)(2,1)S(1)}, u32[]{:S(2)}, u32[]{:S(2)}) collective-permute-start(bf16[3,1,16,128]{3,2,1,0:T(8,128)(2,1)S(1)} %get-tuple-element.37), channel_id=1, source_target_pairs={{0,8},{1,9},{2,10},{3,11},{4,12},{5,13},{6,14},{7,15},{16,24},{17,... | collective-permute-start | bytes 36872 | tf_op jit(solution)/shard_map/ppermute | solution.py:24
  64.1 3.6 collective-permute-start.4
  70.6 8.1 %collective-permute-start.6 = (bf16[3,1,16,128]{3,2,1,0:T(8,128)(2,1)S(1)}, bf16[3,1,16,128]{3,2,1,0:T(8,128)(2,1)S(1)}, u32[]{:S(2)}, u32[]{:S(2)}) collective-permute-start(bf16[3,1,16,128]{3,2,1,0:T(8,128)(2,1)S(1)} %get-tuple-element.35), channel_id=1, source_target_pairs={{0,8},{1,9},{2,10},{3,11},{4,12},{5,13},{6,14},{7,15},{16,24},{17,... | collective-permute-start | bytes 36872 | tf_op jit(solution)/shard_map/ppermute | solution.py:24
  86.6 3.1 fusion.28
  98.8 4.2 collective-permute-start.16
  104.9 3.6 collective-permute-start.8
  115.9 7.9 %collective-permute-start.18 = (bf16[3,1,16,128]{3,2,1,0:T(8,128)(2,1)S(1)}, bf16[3,1,16,128]{3,2,1,0:T(8,128)(2,1)S(1)}, u32[]{:S(2)}, u32[]{:S(2)}) collective-permute-start(bf16[3,1,16,128]{3,2,1,0:T(8,128)(2,1)S(1)} %get-tuple-element.29), channel_id=1, source_target_pairs={{0,8},{1,9},{2,10},{3,11},{4,12},{5,13},{6,14},{7,15},{16,24},{17,... | collective-permute-start | bytes 36872 | tf_op jit(solution)/shard_map/ppermute | solution.py:24
  125.7 8.5 %collective-permute-start.10 = (bf16[3,1,16,128]{3,2,1,0:T(8,128)(2,1)}, bf16[3,1,16,128]{3,2,1,0:T(8,128)(2,1)}, u32[]{:S(2)}, u32[]{:S(2)}) collective-permute-start(bf16[3,1,16,128]{3,2,1,0:T(8,128)(2,1)} %get-tuple-element.33), channel_id=1, source_target_pairs={{0,8},{1,9},{2,10},{3,11},{4,12},{5,13},{6,14},{7,15},{16,24},{17,... | collective-permute-start | bytes 36872 | tf_op jit(solution)/shard_map/ppermute | solution.py:24
  137.0 3.0 fusion.36
  144.7 3.9 collective-permute-start.20
  149.4 3.5 copy.144
  153.0 9.9 %fusion.125 = f32[16,16,3,3,3]{0,1,4,3,2:T(8,128)} fusion(bf16[1,3,10,16,130]{3,0,4,2,1:T(2,128)(2,1)} %copy.144, bf16[1,1,8,16,128]{3,0,4,2,1:T(2,128)(2,1)S(1)} %copy-done.10), kind=kOutput, calls=%fused_computation.191 | convolution fusion | flops 14155776 | bytes 185216 | tf_op jit(solution)/shard_map/conv_general_dilated | solution.py:92
  169.1 8.5 %collective-permute-start.22 = (bf16[3,1,16,128]{3,2,1,0:T(8,128)(2,1)}, bf16[3,1,16,128]{3,2,1,0:T(8,128)(2,1)}, u32[]{:S(2)}, u32[]{:S(2)}) collective-permute-start(bf16[3,1,16,128]{3,2,1,0:T(8,128)(2,1)} %get-tuple-element.27), channel_id=1, source_target_pairs={{0,8},{1,9},{2,10},{3,11},{4,12},{5,13},{6,14},{7,15},{16,24},{17,... | collective-permute-start | bytes 36872 | tf_op jit(solution)/shard_map/ppermute | solution.py:24
  181.4 3.0 copy.146
  197.7 3.8 fusion
  204.8 4.1 fusion.6
  213.4 14.6 %all-to-all-start.1 = ((bf16[8,1,8,16,128]{4,3,2,1,0:T(8,128)(2,1)}), bf16[8,1,8,16,128]{4,3,2,1,0:T(8,128)(2,1)S(1)}, u32[]{:S(2)}, u32[]{:S(2)}) async-start(bf16[8,1,8,16,128]{4,3,2,1,0:T(8,128)(2,1)} %broadcast_in_dim.54), calls=%async_computation.1 | async-start | bytes 524288 | tf_op jit(solution)/shard_map/all_to_all | solution.py:54
  228.0 262.4 %all-reduce.9.cloned.1.call-done = f32[20768]{0:T(1024)} async-done(((f32[20768]{0:T(1024)}), f32[20768]{0:T(1024)}) %all-reduce.9.cloned.1.call-update) | async-done | bytes 83088 | tf_op jit(solution)/shard_map/psum | solution.py:45
  (213 shorter events, 100.6 us)
Async XLA Ops:
  7.2 19.2 %collective-permute-start.12 = (bf16[1,8,16,128]{3,2,1,0:T(8,128)(2,1)}, bf16[1,8,16,128]{3,2,1,0:T(8,128)(2,1)S(1)}, u32[]{:S(2)}, u32[]{:S(2)}) collective-permute-start(bf16[1,8,16,128]{3,2,1,0:T(8,128)(2,1)} %param.19), channel_id=1, source_target_pairs={{0,1},{1,2},{2,3},{3,4},{4,5},{5,6},{6,7},{7,16},{16,17},{17,18},{... | collective-permute-start | bytes 98312 | tf_op jit(solution)/shard_map/ppermute | solution.py:24
  11.8 14.6 %collective-permute-start.13 = (bf16[1,8,16,128]{3,2,1,0:T(8,128)(2,1)}, bf16[1,8,16,128]{3,2,1,0:T(8,128)(2,1)S(1)}, u32[]{:S(2)}, u32[]{:S(2)}) collective-permute-start(bf16[1,8,16,128]{3,2,1,0:T(8,128)(2,1)} %param.19), channel_id=1, source_target_pairs={{1,0},{2,1},{3,2},{4,3},{5,4},{6,5},{7,6},{16,7},{17,16},{18,17},{... | collective-permute-start | bytes 98312 | tf_op jit(solution)/shard_map/ppermute | solution.py:27
  22.9 14.5 %all-to-all-start = ((bf16[8,1,8,16,128]{4,3,2,1,0:T(8,128)(2,1)}), bf16[8,1,8,16,128]{4,3,2,1,0:T(8,128)(2,1)S(1)}, u32[]{:S(2)}, u32[]{:S(2)}) async-start(bf16[8,1,8,16,128]{4,3,2,1,0:T(8,128)(2,1)} %bitcast.5), calls=%async_computation | async-start | bytes 524288 | tf_op jit(solution)/shard_map/all_to_all | solution.py:39
  26.3 464.2 %all-reduce.9.cloned.1.call-start = ((), (), s32[]{:S(2)}) async-start(), calls=%async_computation.2 | async-start | bytes 172032 | tf_op jit(solution)/shard_map/psum | solution.py:45
  26.4 16.8 %collective-permute-start.15 = (bf16[3,1,16,128]{3,2,1,0:T(8,128)(2,1)S(1)}, bf16[3,1,16,128]{3,2,1,0:T(8,128)(2,1)S(1)}, u32[]{:S(2)}, u32[]{:S(2)}) collective-permute-start(bf16[3,1,16,128]{3,2,1,0:T(8,128)(2,1)S(1)} %get-tuple-element.32), channel_id=1, source_target_pairs={{8,0},{9,1},{10,2},{11,3},{12,4},{13,5},{14,6},{15,7},{24,16},{25,... | collective-permute-start | bytes 36872 | tf_op jit(solution)/shard_map/ppermute | solution.py:27
  27.7 15.5 %collective-permute-start.14 = (bf16[3,1,16,128]{3,2,1,0:T(8,128)(2,1)S(1)}, bf16[3,1,16,128]{3,2,1,0:T(8,128)(2,1)S(1)}, u32[]{:S(2)}, u32[]{:S(2)}) collective-permute-start(bf16[3,1,16,128]{3,2,1,0:T(8,128)(2,1)S(1)} %get-tuple-element.31), channel_id=1, source_target_pairs={{0,8},{1,9},{2,10},{3,11},{4,12},{5,13},{6,14},{7,15},{16,24},{17,... | collective-permute-start | bytes 36872 | tf_op jit(solution)/shard_map/ppermute | solution.py:24
  37.4 8.5 %collective-permute-start.1 = (bf16[1,8,16,128]{3,2,1,0:T(8,128)(2,1)S(1)}, bf16[1,8,16,128]{3,2,1,0:T(8,128)(2,1)S(1)}, u32[]{:S(2)}, u32[]{:S(2)}) collective-permute-start(bf16[1,8,16,128]{3,2,1,0:T(8,128)(2,1)S(1)} %bitcast.205), channel_id=1, source_target_pairs={{1,0},{2,1},{3,2},{4,3},{5,4},{6,5},{7,6},{16,7},{17,16},{18,17},{... | collective-permute-start | bytes 98312 | tf_op jit(solution)/shard_map/ppermute | solution.py:27
  46.0 11.0 %collective-permute-start.3 = (bf16[3,1,16,128]{3,2,1,0:T(8,128)(2,1)S(1)}, bf16[3,1,16,128]{3,2,1,0:T(8,128)(2,1)S(1)}, u32[]{:S(2)}, u32[]{:S(2)}) collective-permute-start(bf16[3,1,16,128]{3,2,1,0:T(8,128)(2,1)S(1)} %get-tuple-element.38), channel_id=1, source_target_pairs={{8,0},{9,1},{10,2},{11,3},{12,4},{13,5},{14,6},{15,7},{24,16},{25,... | collective-permute-start | bytes 36872 | tf_op jit(solution)/shard_map/ppermute | solution.py:27
  47.3 9.7 %collective-permute-start.2 = (bf16[3,1,16,128]{3,2,1,0:T(8,128)(2,1)S(1)}, bf16[3,1,16,128]{3,2,1,0:T(8,128)(2,1)S(1)}, u32[]{:S(2)}, u32[]{:S(2)}) collective-permute-start(bf16[3,1,16,128]{3,2,1,0:T(8,128)(2,1)S(1)} %get-tuple-element.37), channel_id=1, source_target_pairs={{0,8},{1,9},{2,10},{3,11},{4,12},{5,13},{6,14},{7,15},{16,24},{17,... | collective-permute-start | bytes 36872 | tf_op jit(solution)/shard_map/ppermute | solution.py:24
  69.3 13.8 %collective-permute-start.7 = (bf16[3,1,16,128]{3,2,1,0:T(8,128)(2,1)S(1)}, bf16[3,1,16,128]{3,2,1,0:T(8,128)(2,1)S(1)}, u32[]{:S(2)}, u32[]{:S(2)}) collective-permute-start(bf16[3,1,16,128]{3,2,1,0:T(8,128)(2,1)S(1)} %get-tuple-element.36), channel_id=1, source_target_pairs={{8,0},{9,1},{10,2},{11,3},{12,4},{13,5},{14,6},{15,7},{24,16},{25,... | collective-permute-start | bytes 36872 | tf_op jit(solution)/shard_map/ppermute | solution.py:27
  70.6 12.5 %collective-permute-start.6 = (bf16[3,1,16,128]{3,2,1,0:T(8,128)(2,1)S(1)}, bf16[3,1,16,128]{3,2,1,0:T(8,128)(2,1)S(1)}, u32[]{:S(2)}, u32[]{:S(2)}) collective-permute-start(bf16[3,1,16,128]{3,2,1,0:T(8,128)(2,1)S(1)} %get-tuple-element.35), channel_id=1, source_target_pairs={{0,8},{1,9},{2,10},{3,11},{4,12},{5,13},{6,14},{7,15},{16,24},{17,... | collective-permute-start | bytes 36872 | tf_op jit(solution)/shard_map/ppermute | solution.py:24
  96.8 17.7 %collective-permute-start.17 = (bf16[1,8,16,128]{3,2,1,0:T(8,128)(2,1)S(1)}, bf16[1,8,16,128]{3,2,1,0:T(8,128)(2,1)S(1)}, u32[]{:S(2)}, u32[]{:S(2)}) collective-permute-start(bf16[1,8,16,128]{3,2,1,0:T(8,128)(2,1)S(1)} %get-tuple-element.9), channel_id=1, source_target_pairs={{1,0},{2,1},{3,2},{4,3},{5,4},{6,5},{7,6},{16,7},{17,16},{18,17},{... | collective-permute-start | bytes 98312 | tf_op jit(solution)/shard_map/ppermute | solution.py:27
  98.8 15.8 %collective-permute-start.16 = (bf16[1,8,16,128]{3,2,1,0:T(8,128)(2,1)S(1)}, bf16[1,8,16,128]{3,2,1,0:T(8,128)(2,1)S(1)}, u32[]{:S(2)}, u32[]{:S(2)}) collective-permute-start(bf16[1,8,16,128]{3,2,1,0:T(8,128)(2,1)S(1)} %get-tuple-element.9), channel_id=1, source_target_pairs={{0,1},{1,2},{2,3},{3,4},{4,5},{5,6},{6,7},{7,16},{16,17},{17,18},{... | collective-permute-start | bytes 98312 | tf_op jit(solution)/shard_map/ppermute | solution.py:24
  103.0 20.8 %collective-permute-start.9 = (bf16[1,8,16,128]{3,2,1,0:T(8,128)(2,1)S(1)}, bf16[1,8,16,128]{3,2,1,0:T(8,128)(2,1)S(1)}, u32[]{:S(2)}, u32[]{:S(2)}) collective-permute-start(bf16[1,8,16,128]{3,2,1,0:T(8,128)(2,1)S(1)} %get-tuple-element.24), channel_id=1, source_target_pairs={{1,0},{2,1},{3,2},{4,3},{5,4},{6,5},{7,6},{16,7},{17,16},{18,17},{... | collective-permute-start | bytes 98312 | tf_op jit(solution)/shard_map/ppermute | solution.py:27
  104.9 18.9 %collective-permute-start.8 = (bf16[1,8,16,128]{3,2,1,0:T(8,128)(2,1)S(1)}, bf16[1,8,16,128]{3,2,1,0:T(8,128)(2,1)S(1)}, u32[]{:S(2)}, u32[]{:S(2)}) collective-permute-start(bf16[1,8,16,128]{3,2,1,0:T(8,128)(2,1)S(1)} %get-tuple-element.24), channel_id=1, source_target_pairs={{0,1},{1,2},{2,3},{3,4},{4,5},{5,6},{6,7},{7,16},{16,17},{17,18},{... | collective-permute-start | bytes 98312 | tf_op jit(solution)/shard_map/ppermute | solution.py:24
  114.6 19.6 %collective-permute-start.19 = (bf16[3,1,16,128]{3,2,1,0:T(8,128)(2,1)S(1)}, bf16[3,1,16,128]{3,2,1,0:T(8,128)(2,1)S(1)}, u32[]{:S(2)}, u32[]{:S(2)}) collective-permute-start(bf16[3,1,16,128]{3,2,1,0:T(8,128)(2,1)S(1)} %get-tuple-element.30), channel_id=1, source_target_pairs={{8,0},{9,1},{10,2},{11,3},{12,4},{13,5},{14,6},{15,7},{24,16},{25,... | collective-permute-start | bytes 36872 | tf_op jit(solution)/shard_map/ppermute | solution.py:27
  115.9 18.3 %collective-permute-start.18 = (bf16[3,1,16,128]{3,2,1,0:T(8,128)(2,1)S(1)}, bf16[3,1,16,128]{3,2,1,0:T(8,128)(2,1)S(1)}, u32[]{:S(2)}, u32[]{:S(2)}) collective-permute-start(bf16[3,1,16,128]{3,2,1,0:T(8,128)(2,1)S(1)} %get-tuple-element.29), channel_id=1, source_target_pairs={{0,8},{1,9},{2,10},{3,11},{4,12},{5,13},{6,14},{7,15},{16,24},{17,... | collective-permute-start | bytes 36872 | tf_op jit(solution)/shard_map/ppermute | solution.py:24
  124.4 24.1 %collective-permute-start.11 = (bf16[3,1,16,128]{3,2,1,0:T(8,128)(2,1)}, bf16[3,1,16,128]{3,2,1,0:T(8,128)(2,1)S(1)}, u32[]{:S(2)}, u32[]{:S(2)}) collective-permute-start(bf16[3,1,16,128]{3,2,1,0:T(8,128)(2,1)} %get-tuple-element.34), channel_id=1, source_target_pairs={{8,0},{9,1},{10,2},{11,3},{12,4},{13,5},{14,6},{15,7},{24,16},{25,... | collective-permute-start | bytes 36872 | tf_op jit(solution)/shard_map/ppermute | solution.py:27
  125.7 22.8 %collective-permute-start.10 = (bf16[3,1,16,128]{3,2,1,0:T(8,128)(2,1)}, bf16[3,1,16,128]{3,2,1,0:T(8,128)(2,1)}, u32[]{:S(2)}, u32[]{:S(2)}) collective-permute-start(bf16[3,1,16,128]{3,2,1,0:T(8,128)(2,1)} %get-tuple-element.33), channel_id=1, source_target_pairs={{0,8},{1,9},{2,10},{3,11},{4,12},{5,13},{6,14},{7,15},{16,24},{17,... | collective-permute-start | bytes 36872 | tf_op jit(solution)/shard_map/ppermute | solution.py:24
  142.7 24.4 %collective-permute-start.21 = (bf16[1,8,16,128]{3,2,1,0:T(8,128)(2,1)S(1)}, bf16[1,8,16,128]{3,2,1,0:T(8,128)(2,1)S(1)}, u32[]{:S(2)}, u32[]{:S(2)}) collective-permute-start(bf16[1,8,16,128]{3,2,1,0:T(8,128)(2,1)S(1)} %get-tuple-element.11), channel_id=1, source_target_pairs={{1,0},{2,1},{3,2},{4,3},{5,4},{6,5},{7,6},{16,7},{17,16},{18,17},{... | collective-permute-start | bytes 98312 | tf_op jit(solution)/shard_map/ppermute | solution.py:27
  144.7 22.5 %collective-permute-start.20 = (bf16[1,8,16,128]{3,2,1,0:T(8,128)(2,1)S(1)}, bf16[1,8,16,128]{3,2,1,0:T(8,128)(2,1)S(1)}, u32[]{:S(2)}, u32[]{:S(2)}) collective-permute-start(bf16[1,8,16,128]{3,2,1,0:T(8,128)(2,1)S(1)} %get-tuple-element.11), channel_id=1, source_target_pairs={{0,1},{1,2},{2,3},{3,4},{4,5},{5,6},{6,7},{7,16},{16,17},{17,18},{... | collective-permute-start | bytes 98312 | tf_op jit(solution)/shard_map/ppermute | solution.py:24
  167.8 17.6 %collective-permute-start.23 = (bf16[3,1,16,128]{3,2,1,0:T(8,128)(2,1)}, bf16[3,1,16,128]{3,2,1,0:T(8,128)(2,1)S(1)}, u32[]{:S(2)}, u32[]{:S(2)}) collective-permute-start(bf16[3,1,16,128]{3,2,1,0:T(8,128)(2,1)} %get-tuple-element.28), channel_id=1, source_target_pairs={{8,0},{9,1},{10,2},{11,3},{12,4},{13,5},{14,6},{15,7},{24,16},{25,... | collective-permute-start | bytes 36872 | tf_op jit(solution)/shard_map/ppermute | solution.py:27
  169.1 16.3 %collective-permute-start.22 = (bf16[3,1,16,128]{3,2,1,0:T(8,128)(2,1)}, bf16[3,1,16,128]{3,2,1,0:T(8,128)(2,1)}, u32[]{:S(2)}, u32[]{:S(2)}) collective-permute-start(bf16[3,1,16,128]{3,2,1,0:T(8,128)(2,1)} %get-tuple-element.27), channel_id=1, source_target_pairs={{0,8},{1,9},{2,10},{3,11},{4,12},{5,13},{6,14},{7,15},{16,24},{17,... | collective-permute-start | bytes 36872 | tf_op jit(solution)/shard_map/ppermute | solution.py:24
  213.4 286.2 %all-to-all-start.1 = ((bf16[8,1,8,16,128]{4,3,2,1,0:T(8,128)(2,1)}), bf16[8,1,8,16,128]{4,3,2,1,0:T(8,128)(2,1)S(1)}, u32[]{:S(2)}, u32[]{:S(2)}) async-start(bf16[8,1,8,16,128]{4,3,2,1,0:T(8,128)(2,1)} %broadcast_in_dim.54), calls=%async_computation.1 | async-start | bytes 524288 | tf_op jit(solution)/shard_map/all_to_all | solution.py:54
  (33 other events, 199.7 us)
Sparse Core Ops, SparseCore 0:
  212.8 277.6 all-reduce.8
where the time goes:
time: 516 us; the launch traced here: 508 us
  waiting for transfers between devices  262 us (51%)
  starting transfers between devices  114 us (22%)
  local copies, waits for them, and re-layouts  63 us (12%)
  matrix products  33.7 us (7%)
  other arithmetic  19.5 us (4%)
  between operations  15.4 us (3%)
    psum x1, waiting for transfers between devices, together(): subtotal = lax.psum(flat, axis)  262 us
    ppermute x12, starting transfers between devices, extended(): lax.ppermute(lax.slice_in_dim(block, block.shape[dim] - width, None, axis...  72.8 us
    conv_general_dilated x32, local copies, waits for them, and re-layouts, conv_valid(): lax.conv_general_dilated(padded[None], weight, (1, 1, 1), ((0, 0), (0, 0)...  28.5 us
    ppermute x12, starting transfers between devices, extended(): lax.ppermute(lax.slice_in_dim(block, 0, width, axis=dim), axis, backward)  23.2 us
    conv_general_dilated x3, matrix products, weight_grad(): lax.conv_general_dilated(padded[None], grad_out[None], (1, 1, 1), ((0, 0)...  17.8 us
    all_to_all x1, starting transfers between devices, copy_for_each(): lax.all_to_all(jnp.broadcast_to(shard[None], (peers, *shard.shape)), axis...  14.6 us
    conv_general_dilated x6, matrix products, conv_valid(): lax.conv_general_dilated(padded[None], weight, (1, 1, 1), ((0, 0), (0, 0)...  14.1 us
    broadcast_in_dim x17, local copies, waits for them, and re-layouts, conv_valid(): padded[None]  10.8 us
  transfers between devices with their start and end apart: 27, of which 1 were waited for; matrix products, arithmetic and copies ran while one was open for 13% of the time, Pallas kernels for 0%

commit v1 on v0

v1 whole, which is shorter than its diff:
```python
import math

import jax
import jax.numpy as jnp
from jax import lax
from jax.experimental import pallas as pl
from jax.experimental.pallas import tpu as pltpu
from jax.sharding import PartitionSpec as P

C = 16
X = 128
YB = 8
YC = 256
HALF = 128
RIM = 64
VIEWS = 8
F32, BF16 = jnp.float32, jnp.bfloat16
MIB = 1 << 20


def call(kernel, outs, scratch=(), vmem=32, flops=0, moved=0):
    return dict(
        out_shape=outs,
        scratch_shapes=list(scratch),
        compiler_params=pltpu.CompilerParams(vmem_limit_bytes=vmem * MIB),
        cost_estimate=pl.CostEstimate(flops=flops, bytes_accessed=moved, transcendentals=0),
    )


def vmem_spec():
    return pl.BlockSpec(memory_space=pltpu.VMEM)


def smem_spec():
    return pl.BlockSpec(memory_space=pltpu.SMEM)


def band_kernel(taps_ref, band_ref):
    at = lax.broadcasted_iota(jnp.int32, (X, YC), 0)
    to = lax.broadcasted_iota(jnp.int32, (X, YC), 1)
    for y in range(16):
        spread = jnp.where(to == at + (y - 1) * C, 1.0, 0.0).astype(BF16)
        rows = jnp.dot(taps_ref[...], spread, preferred_element_type=F32).astype(BF16)
        for n in range(6):
            for a in range(3):
                for c in range(3):
                    first = ((n * 3 + a) * 3 + c) * C
                    band_ref[n, a, y * C : (y + 1) * C, c * YC : (c + 1) * YC] = rows[
                        first : first + C, :
                    ]


def lift_kernel(bricks_ref, rows_ref, feats_ref, weights_ref, out_ref, total):
    total[...] = jnp.zeros_like(total)
    tiles, slots = bricks_ref.shape
    for k in range(slots):
        blocks = lax.dot_general(
            feats_ref[...], weights_ref[k], (((1,), (1,)), ((), ())), preferred_element_type=F32
        )
        for t in range(tiles):
            row = bricks_ref[t, k] * YB + rows_ref[t, k]
            total[row] += blocks[t * C : (t + 1) * C, :]
    out_ref[...] = total[...].astype(BF16).reshape(out_ref.shape)


def camera_kernel(bricks_ref, rows_ref, arrived_ref, weights_ref, out_ref, chosen):
    tiles, slots = bricks_ref.shape
    for k in range(slots):
        for t in range(tiles):
            at = pl.multiple_of(rows_ref[t, k] * C, C)
            chosen[t * C : (t + 1) * C, k * X : (k + 1) * X] = arrived_ref[
                bricks_ref[t, k], pl.ds(at, C), :
            ]
    out_ref[...] = jnp.dot(
        chosen[...], weights_ref[...].reshape(slots * X, X), preferred_element_type=F32
    )


def silu_and_slope(v):
    s = jax.nn.sigmoid(v)
    return v * s, s * (1.0 + v * (1.0 - s))


def main_kernel(
    arrived_ref,
    band_ref,
    bias_ref,
    field_ref,
    payload_ref,
    s_lift,
    s_grad,
    s_act1,
    s_act2,
    s_back2,
    s_back1,
    slope1,
    slope2,
    up2,
):
    depth, height, view = (lax.axis_index(n) for n in ("depth", "height", "view"))
    lane = lax.broadcasted_iota(jnp.int32, (YC, X), 1)
    first_lane, last_lane = lane == 0, lane == X - 1
    low = height == 0

    def put(dst, index, plane):
        cols = slice(index * X, (index + 1) * X)
        dst[0:YC, cols] = jnp.where(first_lane, 0.0, pltpu.roll(plane, 1, 1)).astype(BF16)
        dst[YC : 2 * YC, cols] = plane.astype(BF16)
        dst[2 * YC : 3 * YC, cols] = jnp.where(last_lane, 0.0, pltpu.roll(plane, X - 1, 1)).astype(
            BF16
        )

    def fetch(offset, kind):
        source = lax.rem(view + offset + VIEWS, VIEWS)
        if offset == -4:
            kind = jnp.where(view < 4, 1, 0)
        if offset == 4:
            kind = jnp.where(view < 4, 0, 1)
        part = arrived_ref[source, kind].astype(F32)
        own, rim = part[:HALF], part[HALF:]
        none = jnp.zeros((RIM, X), F32)
        return jnp.where(
            low,
            jnp.concatenate([own, rim, none], axis=0),
            jnp.concatenate([none, rim, own], axis=0),
        )

    def inside(offset):
        z = depth * VIEWS + view + offset
        return jnp.logical_and(z >= 0, z < lax.axis_size("depth") * VIEWS)

    def masked(offset, plane):
        return jnp.where(inside(offset), plane, 0.0)

    def conv(n, src, start, count):
        out = jnp.zeros((YC, count * X), F32)
        for a in range(3):
            out += jnp.dot(
                band_ref[n, a],
                src[:, (start + a) * X : (start + a + count) * X],
                preferred_element_type=F32,
            )
        return [out[:, i * X : (i + 1) * X] for i in range(count)]

    def pairs(count):
        return [(i, min(2, count - i)) for i in range(0, count, 2)]

    for i in range(9):
        put(s_lift, i, fetch(i - 4, 0))
    for i in range(7):
        put(s_grad, i, fetch(i - 3, 2))

    bias1, bias2 = bias_ref[0], bias_ref[1]
    for i, n in pairs(7):
        for j, pre in enumerate(conv(0, s_lift, i, n)):
            act, slope = silu_and_slope(pre + bias1)
            put(s_act1, i + j, masked(i + j - 3, act))
            if abs(i + j - 3) <= 1:
                slope1[i + j - 2] = slope
    for i, n in pairs(5):
        for j, up in enumerate(conv(3, s_grad, i, n)):
            up2[i + j] = up
    for i, n in pairs(5):
        for j, pre in enumerate(conv(1, s_act1, i, n)):
            at = i + j
            act, slope = silu_and_slope(pre + bias2)
            back = up2[at] * slope
            put(s_back2, at, masked(at - 2, back))
            if at == 2:
                slope2[...] = back
            if abs(at - 2) <= 1:
                before = s_act1[YC : 2 * YC, (at + 1) * X : (at + 2) * X].astype(F32)
                put(s_act2, at - 1, masked(at - 2, act + before))
    for i, n in pairs(3):
        for j, up in enumerate(conv(4, s_back2, i, n)):
            at = i + j
            back = (up2[at + 1] + up) * slope1[at]
            if at == 1:
                slope1[at] = back
            put(s_back1, at, masked(at - 1, back))

    def own_rows(plane):
        return jnp.where(low, plane[:HALF], plane[HALF:])

    (lift_grad,) = conv(5, s_back1, 0, 1)
    lift_grad = own_rows(lift_grad).astype(BF16)
    for v in range(VIEWS):
        payload_ref[v, :HALF, :] = lift_grad
    (field,) = conv(2, s_act2, 0, 1)
    field_ref[...] = own_rows(field).astype(BF16)

    own_at = pl.multiple_of(YC + height * HALF, HALF)
    wide = (HALF, 3 * YC)
    row_y = lax.broadcasted_iota(jnp.int32, wide, 0) // C + height * YB
    col_y = lax.rem(lax.broadcasted_iota(jnp.int32, wide, 1), YC) // C
    bands = [col_y == row_y + (b - 1) for b in range(3)]
    group = lax.broadcasted_iota(jnp.int32, (3 * C, X), 1) // C
    packed = [jnp.zeros((3 * C, X), F32) for _ in range(4)]
    layers = ((s_back1, 1, s_lift, 4), (s_back2, 2, s_act1, 3), (s_grad, 3, s_act2, 1))
    for layer, (g_ref, g_at, v_ref, v_at) in enumerate(layers):
        g = g_ref[pl.ds(own_at, HALF), g_at * X : (g_at + 1) * X]
        for a in range(3):
            at = v_at + a - 1
            products = lax.dot_general(
                g,
                v_ref[:, at * X : (at + 1) * X],
                (((1,), (1,)), ((), ())),
                preferred_element_type=F32,
            )
            by_row = [
                jnp.where(band, products, 0.0).reshape(YB, C, 3 * YC).sum(axis=0) for band in bands
            ]
            by_row = jnp.concatenate(by_row, axis=0)
            for c in range(3):
                part = by_row[:, c * YC : c * YC + X] + by_row[:, c * YC + X : (c + 1) * YC]
                for step in (64, 32, 16):
                    part = part + pltpu.roll(part, step, 1)
                q = (layer * 3 + a) * 3 + c
                packed[q // 8] = jnp.where(group == q % 8, part, packed[q // 8])
    for layer, plane in enumerate((slope1[1], slope2[...])):
        sums = jnp.sum(own_rows(plane), axis=1, keepdims=True)
        sums = jnp.broadcast_to(sums, (HALF, X)).reshape(YB, C, X).sum(axis=0)
        packed[3] = jnp.where(group == 3 + layer, jnp.concatenate([sums] * 3, axis=0), packed[3])
    for v in range(VIEWS):
        start = (v % 2) * 24
        rows = packed[v // 2][start : start + 24]
        high = rows.astype(BF16).astype(F32)
        both = jnp.concatenate([high, rows - high], axis=0)
        payload_ref[v, HALF:, :] = both.astype(BF16)


def main_call(arrived, bands, bias):
    return pl.pallas_call(
        main_kernel,
        in_specs=[vmem_spec()] * 3,
        out_specs=[vmem_spec()] * 2,
        **call(
            main_kernel,
            (
                jax.ShapeDtypeStruct((HALF, X), BF16),
                jax.ShapeDtypeStruct((VIEWS, HALF + 48, X), BF16),
            ),
            [pltpu.VMEM((3 * YC, n * X), BF16) for n in (9, 7, 7, 3, 5, 3)]
            + [
                pltpu.VMEM((3, YC, X), F32),
                pltpu.VMEM((YC, X), F32),
                pltpu.VMEM((5, YC, X), F32),
            ],
            vmem=40,
            flops=10**10,
            moved=10**7,
        ),
    )(arrived, bands, bias)


def flip_swap(weight):
    return jnp.transpose(jnp.flip(weight, (2, 3, 4)), (1, 0, 2, 3, 4))


def for_each(block, axes):
    peers = lax.axis_size(axes)
    tiles = jnp.broadcast_to(block[None], (peers, *block.shape))
    return lax.all_to_all(tiles, axes, 0, 0, tiled=True)


def body(
    camera_feats,
    footprint_slot_weights,
    tile_bricks,
    tile_rows,
    conv_first,
    conv_second,
    conv_third,
    bias_first,
    bias_second,
    out_grad,
):
    depths, heights, views = (lax.axis_size(n) for n in ("depth", "height", "view"))
    height, view = lax.axis_index("height"), lax.axis_index("view")
    tiles, slots = tile_bricks.shape

    partial = pl.pallas_call(
        lift_kernel,
        in_specs=[smem_spec(), smem_spec(), vmem_spec(), vmem_spec()],
        out_specs=vmem_spec(),
        **call(
            lift_kernel,
            jax.ShapeDtypeStruct((views, HALF, X), BF16),
            [pltpu.VMEM((views * YB, C, X), F32)],
            flops=10**8,
            moved=10**6,
        ),
    )(tile_bricks, tile_rows, camera_feats.reshape(tiles * C, X), footprint_slot_weights)
    pieces = lax.all_to_all(partial, "view", 0, 0, tiled=True)

    convs = [conv_first, conv_second, conv_third]
    convs = jnp.stack(convs + [flip_swap(w) for w in reversed(convs)])
    taps = jnp.transpose(convs, (0, 3, 5, 1, 4, 2)).reshape(-1, 3 * C)
    taps = jnp.pad(taps, ((0, 0), (0, X - 3 * C)))
    bands = pl.pallas_call(
        band_kernel,
        in_specs=[vmem_spec()],
        out_specs=vmem_spec(),
        **call(
            band_kernel,
            jax.ShapeDtypeStruct((6, 3, YC, 3 * YC), BF16),
            flops=10**9,
            moved=7 * 10**6,
        ),
    )(taps)
    bias = jnp.stack([jnp.tile(b, 16) for b in (bias_first, bias_second)])[:, :, None]

    lifted = pieces.astype(F32).sum(axis=0).astype(BF16)
    own = jnp.stack([lifted, out_grad.reshape(HALF, X)])
    moves = []
    for d in range(depths):
        for v in range(views):
            to = d + (1 if v >= views // 2 else -1)
            if 0 <= to < depths:
                moves.append((d * views + v, to * views + v))
    far = lax.ppermute(own, ("depth", "view"), moves)
    planes = jnp.concatenate([own, far])
    facing = jnp.where(height == 0, planes[:, HALF - RIM :], planes[:, :RIM])
    rim = lax.ppermute(facing, "height", [(0, 1), (1, 0)])
    planes = jnp.concatenate([planes, rim], axis=1)
    near = jnp.abs(lax.iota(jnp.int32, views) - view) <= views // 2
    near = near[:, None, None]
    parts = jnp.stack(
        [
            jnp.where(near, planes[0], planes[2]),
            jnp.broadcast_to(planes[2], (views, *planes[2].shape)),
            jnp.where(near, planes[1], planes[3]),
        ],
        axis=1,
    )
    arrived = lax.all_to_all(parts, "view", 0, 0, tiled=True)

    field, payload = main_call(arrived, bands, bias)
    arrived = lax.all_to_all(payload, "view", 0, 0, tiled=True)

    sums = arrived[:, HALF:].astype(F32).sum(axis=0)
    sums = sums[:24] + sums[24:]
    sums = for_each(sums, ("depth", "height")).sum(axis=0)

    camera_grad = pl.pallas_call(
        camera_kernel,
        in_specs=[smem_spec(), smem_spec(), vmem_spec(), vmem_spec()],
        out_specs=vmem_spec(),
        **call(
            camera_kernel,
            jax.ShapeDtypeStruct((tiles * C, X), F32),
            [pltpu.VMEM((tiles * C, slots * X), BF16)],
            flops=10**8,
            moved=10**6,
        ),
    )(tile_bricks, tile_rows, arrived, footprint_slot_weights)

    sums = for_each(sums, "view").reshape(4, 3, C, 8, C)
    scale = 1.0 / math.sqrt(YB * X * depths * heights * views)
    sums = sums * scale
    bias_gradient_pair = jnp.transpose(sums[3, 0, :, 3:5, 0])
    sums = jnp.transpose(sums, (0, 3, 2, 4, 1)).reshape(32, C, C, 3)[:27]
    weight_grads = jnp.transpose(sums.reshape(3, 3, 3, C, C, 3), (0, 3, 4, 1, 5, 2))
    return (
        field.reshape(1, YB, C, X),
        camera_grad.reshape(tiles, C, X),
        weight_grads,
        bias_gradient_pair,
    )


def solution(mesh):
    in_specs = (
        P(("depth", "height", "view"), None, None),
        P(),
        P(("depth", "height", "view"), None),
        P(("depth", "height", "view"), None),
        P(),
        P(),
        P(),
        P(),
        P(),
        P(("depth", "view"), "height", None, None),
    )
    out_specs = (
        P(("depth", "view"), "height", None, None),
        P(("depth", "height", "view"), None, None),
        P(),
        P(),
    )
    return jax.shard_map(body, mesh=mesh, in_specs=in_specs, out_specs=out_specs, check_vma=False)
```

time: 516 us -> 133 us (0.26); the launches traced: 508 us -> 132 us
  waiting for transfers between devices: 262 us -> 25 us
  starting transfers between devices: 114 us -> 32.2 us
  local copies, waits for them, and re-layouts: 63 us -> 14.7 us
  blocking collectives: 0 us -> 46 us
  matrix products: 33.7 us -> 0 us
  other arithmetic: 19.5 us -> 1.53 us
  between operations: 15.4 us -> 0.95 us
  Pallas kernels: 0 us -> 12.2 us
    psum x1 -> x0, waiting for transfers between devices: 262 us -> none  [together(): subtotal = lax.psum(flat, axis)]
    ppermute x24 -> x2, starting transfers between devices: 96 us -> 7.52 us  [the longest x1 6.23 us: body(): rim = lax.ppermute(facing, 'height', [(0, 1), (1, 0)])]
    all_to_all x0 -> x2, blocking collectives: none -> 46 us  [the longest x1 35 us: for_each(): return lax.all_to_all(tiles, axes, 0, 0, tiled=True)]
    conv_general_dilated x35 -> x0, local copies, waits for them, and re-layouts: 35.2 us -> none  [the longest x32 28.5 us: conv_valid(): lax.conv_general_dilated(padded[None], weight, (1, 1, 1), ((0, 0), (0, 0)...]
    conv_general_dilated x9 -> x0, matrix products: 31.9 us -> none  [the longest x3 17.8 us: weight_grad(): lax.conv_general_dilated(padded[None], grad_out[None], (1, 1, 1), ((0, 0)...]
    all_to_all x2 -> x3, waiting for transfers between devices: 0.01 us -> 18.8 us  [the longest x1 10.7 us: body(): arrived = lax.all_to_all(parts, 'view', 0, 0, tiled=True)]
    pallas_call x0 -> x4, Pallas kernels: none -> 12.2 us  [the longest x1 6.86 us: main_call(): pl.pallas_call(main_kernel, in_specs=[vmem_spec()] * 3, out_specs=[vmem_s...]
    broadcast_in_dim x21 -> x4, local copies, waits for them, and re-layouts: 12.6 us -> 0.9 us  [the longest x2 0.7 us: for_each(): tiles = jnp.broadcast_to(block[None], (peers, *block.shape))]
  transfers between devices with their start and end apart: 27 -> 5, of which waited for: 1 -> 5; matrix products, arithmetic and copies ran while one was open for 13% -> 2% of each run, Pallas kernels for 0% -> 3%
where the time goes in v1:
time: 133 us; the launch traced here: 132 us
  blocking collectives  46 us (35%)
  starting transfers between devices  32.2 us (24%)
  waiting for transfers between devices  25 us (19%)
  local copies, waits for them, and re-layouts  14.7 us (11%)
  Pallas kernels  12.2 us (9%)
  other arithmetic  1.53 us (1%)
    all_to_all x1, blocking collectives, for_each(): return lax.all_to_all(tiles, axes, 0, 0, tiled=True)  35 us
    all_to_all x1, blocking collectives, body(): arrived = lax.all_to_all(payload, 'view', 0, 0, tiled=True)  11 us
    all_to_all x1, waiting for transfers between devices, body(): arrived = lax.all_to_all(parts, 'view', 0, 0, tiled=True)  10.7 us
    unnamed x35, local copies, waits for them, and re-layouts  10.3 us
    all_to_all x1, starting transfers between devices, body(): pieces = lax.all_to_all(partial, 'view', 0, 0, tiled=True)  10.2 us
    all_to_all x1, starting transfers between devices, for_each(): return lax.all_to_all(tiles, axes, 0, 0, tiled=True)  7.6 us
    all_to_all x1, starting transfers between devices, body(): arrived = lax.all_to_all(parts, 'view', 0, 0, tiled=True)  6.87 us
    pallas_call x1, Pallas kernels, main_call(): pl.pallas_call(main_kernel, in_specs=[vmem_spec()] * 3, out_specs=[vmem_s...  6.86 us
  transfers between devices with their start and end apart: 5, of which 5 were waited for; matrix products, arithmetic and copies ran while one was open for 2% of the time, Pallas kernels for 3%

profile of v1, /device:TPU:1, one launch (start us, length us, event | category | flops | bytes accessed | tf_op | source)
XLA Modules:
  0.0 132.5 jit_solution(5284939995480656130)
XLA Ops:
  0.6 0.9 copy-done.2
  1.6 0.8 copy-done.4
  2.3 0.7 copy-done.5
  3.0 0.7 copy-done.7
  3.7 1.8 %shard_map.129 = bf16[8,128,128]{2,1,0:T(8,128)(2,1)} custom-call(s32[8,8]{1,0:T(8,128)S(1)} %copy-done.5, s32[8,8]{1,0:T(8,128)S(1)} %copy-done.7, bf16[128,128]{1,0:T(8,128)(2,1)S(1)} %bitcast.42, bf16[8,128,128]{2,1,0:T(8,128)(2,1)S(1)} %copy-done.2), custom_call_target="tpu_custom_call" | custom-call | flops 100000000 | bytes 1000000 | tf_op jit(solution)/shard_map/pallas_call | solution.py:282
  5.6 10.2 %all-to-all-start = ((bf16[8,128,128]{2,1,0:T(8,128)(2,1)}), bf16[8,128,128]{2,1,0:T(8,128)(2,1)S(1)}, u32[]{:S(2)}, u32[]{:S(2)}) async-start(bf16[8,128,128]{2,1,0:T(8,128)(2,1)} %shard_map.129), calls=%async_computation | async-start | bytes 524288 | tf_op jit(solution)/shard_map/all_to_all | solution.py:294
  17.6 4.6 %all-to-all-done = bf16[8,128,128]{2,1,0:T(8,128)(2,1)S(1)} async-done(((bf16[8,128,128]{2,1,0:T(8,128)(2,1)}), bf16[8,128,128]{2,1,0:T(8,128)(2,1)S(1)}, u32[]{:S(2)}, u32[]{:S(2)}) %all-to-all-start) | async-done | bytes 262176 | tf_op jit(solution)/shard_map/all_to_all | solution.py:294
  22.3 1.3 collective-permute-start
  23.8 3.5 %collective-permute-done = bf16[2,128,128]{2,1,0:T(8,128)(2,1)S(1)} collective-permute-done((bf16[2,128,128]{2,1,0:T(8,128)(2,1)S(1)}, bf16[2,128,128]{2,1,0:T(8,128)(2,1)S(1)}, u32[]{:S(2)}, u32[]{:S(2)}) %collective-permute-start) | collective-permute-done | bytes 65568 | tf_op jit(solution)/shard_map/ppermute | solution.py:321
  27.4 6.2 %collective-permute-start.1 = (bf16[4,64,128]{2,1,0:T(8,128)(2,1)S(1)}, bf16[4,64,128]{2,1,0:T(8,128)(2,1)S(1)}, u32[]{:S(2)}, u32[]{:S(2)}) collective-permute-start(bf16[4,64,128]{2,1,0:T(8,128)(2,1)S(1)} %slice_select_fusion), channel_id=1, source_target_pairs={{0,8},{8,0},{1,9},{9,1},{2,10},{10,2},{3,11},{11,3},{4,12},{12,4},... | collective-permute-start | bytes 196616 | tf_op jit(solution)/shard_map/ppermute | solution.py:324
  33.6 2.7 %collective-permute-done.1 = bf16[4,64,128]{2,1,0:T(8,128)(2,1)S(1)} collective-permute-done((bf16[4,64,128]{2,1,0:T(8,128)(2,1)S(1)}, bf16[4,64,128]{2,1,0:T(8,128)(2,1)S(1)}, u32[]{:S(2)}, u32[]{:S(2)}) %collective-permute-start.1) | collective-permute-done | bytes 65568 | tf_op jit(solution)/shard_map/ppermute | solution.py:324
  36.6 1.2 pad_maximum_fusion
  37.7 6.9 %all-to-all-start.1 = ((bf16[8,3,192,128]{3,2,1,0:T(8,128)(2,1)}), bf16[8,3,192,128]{3,2,1,0:T(8,128)(2,1)S(1)}, u32[]{:S(2)}, u32[]{:S(2)}) async-start(bf16[8,3,192,128]{3,2,1,0:T(8,128)(2,1)} %pad_maximum_fusion), calls=%async_computation.1 | async-start | bytes 2359296 | tf_op jit(solution)/shard_map/all_to_all | solution.py:336
  45.6 1.9 %shard_map.130.band_ref = bf16[6,3,256,768]{3,2,1,0:T(8,128)(2,1)S(1)} custom-call(bf16[864,128]{1,0:T(8,128)(2,1)S(1)} %pad.4.taps_ref), custom_call_target="tpu_custom_call" | custom-call | flops 1000000000 | bytes 7000000 | tf_op jit(solution)/shard_map/pallas_call | solution.py:300
  47.5 2.9 %copy-done = bf16[6,3,256,768]{3,2,1,0:T(8,128)(2,1)} copy-done((bf16[6,3,256,768]{3,2,1,0:T(8,128)(2,1)}, bf16[6,3,256,768]{3,2,1,0:T(8,128)(2,1)S(1)}, u32[]{:S(2)}) %copy-start) | copy-done | bytes 7077912
  50.4 10.7 %all-to-all-done.1.arrived_ref = bf16[8,3,192,128]{3,2,1,0:T(8,128)(2,1)S(1)} async-done(((bf16[8,3,192,128]{3,2,1,0:T(8,128)(2,1)}), bf16[8,3,192,128]{3,2,1,0:T(8,128)(2,1)S(1)}, u32[]{:S(2)}, u32[]{:S(2)}) %all-to-all-start.1) | async-done | bytes 1179680 | tf_op jit(solution)/shard_map/all_to_all | solution.py:336
  61.1 3.0 %copy-done.1 = bf16[6,3,256,768]{3,2,1,0:T(8,128)(2,1)S(1)} copy-done((bf16[6,3,256,768]{3,2,1,0:T(8,128)(2,1)S(1)}, bf16[6,3,256,768]{3,2,1,0:T(8,128)(2,1)}, u32[]{:S(2)}) %copy-start.1) | copy-done | bytes 7077912
  64.2 6.9 %shard_map.131 = (bf16[128,128]{1,0:T(8,128)(2,1)}, bf16[8,176,128]{2,1,0:T(8,128)(2,1)S(1)}) custom-call(bf16[8,3,192,128]{3,2,1,0:T(8,128)(2,1)S(1)} %all-to-all-done.1.arrived_ref, bf16[6,3,256,768]{3,2,1,0:T(8,128)(2,1)S(1)} %copy-done.1, f32[2,256,1]{2,1,0:T(8,128)S(1)} %copy.31.bias_ref), custom_call_target="tpu_custom_call" | custom-call | flops 10000000000 | bytes 10000000 | tf_op jit(solution)/shard_map/pallas_call | solution.py:233
  71.0 11.0 %all_to_all.25.arrived_ref = bf16[8,176,128]{2,1,0:T(8,128)(2,1)S(1)} all-to-all(bf16[8,176,128]{2,1,0:T(8,128)(2,1)S(1)} %get-tuple-element.7), channel_id=1, replica_groups=mesh['depth'=32,'height'=2,'view'=8] {'view'}, dimensions={0} | all-to-all | bytes 720896 | tf_op jit(solution)/shard_map/all_to_all | solution.py:339
  82.2 35.0 %all_to_all.26 = f32[64,24,128]{2,1,0:T(8,128)S(1)} all-to-all(f32[64,24,128]{2,1,0:T(8,128)S(1)} %broadcast_in_dim.47), channel_id=1, replica_groups=mesh['depth'=32,'height'=2,'view'=8] {'depth','height'}, dimensions={0} | all-to-all | bytes 1572864 | tf_op jit(solution)/shard_map/all_to_all | solution.py:263
  117.8 7.6 %all-to-all-start.4 = ((f32[8,24,128]{2,1,0:T(8,128)}), f32[8,24,128]{2,1,0:T(8,128)S(1)}, u32[]{:S(2)}, u32[]{:S(2)}) async-start(f32[8,24,128]{2,1,0:T(8,128)} %broadcast_in_dim.48), calls=%async_computation.4 | async-start | bytes 196608 | tf_op jit(solution)/shard_map/all_to_all | solution.py:263
  125.5 1.6 %shard_map.132 = f32[128,128]{1,0:T(8,128)} custom-call(s32[8,8]{1,0:T(8,128)S(1)} %copy-done.6, s32[8,8]{1,0:T(8,128)S(1)} %copy-done.8, bf16[8,176,128]{2,1,0:T(8,128)(2,1)S(1)} %all_to_all.25.arrived_ref, bf16[8,128,128]{2,1,0:T(8,128)(2,1)S(1)} %copy-done.3), custom_call_target="tpu_custom_call" | custom-call | flops 100000000 | bytes 1000000 | tf_op jit(solution)/shard_map/pallas_call | solution.py:345
  127.1 3.4 %all-to-all-done.4 = f32[8,24,128]{2,1,0:T(8,128)S(1)} async-done(((f32[8,24,128]{2,1,0:T(8,128)}), f32[8,24,128]{2,1,0:T(8,128)S(1)}, u32[]{:S(2)}, u32[]{:S(2)}) %all-to-all-start.4) | async-done | bytes 98336 | tf_op jit(solution)/shard_map/all_to_all | solution.py:263
  131.6 0.9 copy.34
  (58 shorter events, 5.2 us)
Async XLA Ops:
  0.6 1.0 copy-start.2
  1.6 0.8 copy-start.4
  2.3 0.7 copy-start.5
  3.0 0.7 copy-start.7
  3.7 13.5 %copy-start.9 = (bf16[16,16,3,3,3]{1,0,4,3,2:T(8,128)(2,1)S(1)}, bf16[16,16,3,3,3]{1,0,4,3,2:T(8,128)(2,1)}, u32[]{:S(2)}) copy-start(bf16[16,16,3,3,3]{1,0,4,3,2:T(8,128)(2,1)} %param.14) | copy-start | bytes 41476
  3.7 13.6 %copy-start.10 = (bf16[16,16,3,3,3]{1,0,4,3,2:T(8,128)(2,1)S(1)}, bf16[16,16,3,3,3]{1,0,4,3,2:T(8,128)(2,1)}, u32[]{:S(2)}) copy-start(bf16[16,16,3,3,3]{1,0,4,3,2:T(8,128)(2,1)} %param.15) | copy-start | bytes 41476
  3.7 13.8 %copy-start.11 = (bf16[16,16,3,3,3]{1,0,4,3,2:T(8,128)(2,1)S(1)}, bf16[16,16,3,3,3]{1,0,4,3,2:T(8,128)(2,1)}, u32[]{:S(2)}) copy-start(bf16[16,16,3,3,3]{1,0,4,3,2:T(8,128)(2,1)} %param.16) | copy-start | bytes 41476
  3.7 18.6 %copy-start.12 = (bf16[1,8,16,128]{3,2,1,0:T(8,128)(2,1)S(1)}, bf16[1,8,16,128]{3,2,1,0:T(8,128)(2,1)}, u32[]{:S(2)}) copy-start(bf16[1,8,16,128]{3,2,1,0:T(8,128)(2,1)} %param.19) | copy-start | bytes 98308
  5.6 16.7 %all-to-all-start = ((bf16[8,128,128]{2,1,0:T(8,128)(2,1)}), bf16[8,128,128]{2,1,0:T(8,128)(2,1)S(1)}, u32[]{:S(2)}, u32[]{:S(2)}) async-start(bf16[8,128,128]{2,1,0:T(8,128)(2,1)} %shard_map.129), calls=%async_computation | async-start | bytes 524288 | tf_op jit(solution)/shard_map/all_to_all | solution.py:294
  22.3 5.0 %collective-permute-start = (bf16[2,128,128]{2,1,0:T(8,128)(2,1)S(1)}, bf16[2,128,128]{2,1,0:T(8,128)(2,1)S(1)}, u32[]{:S(2)}, u32[]{:S(2)}) collective-permute-start(bf16[2,128,128]{2,1,0:T(8,128)(2,1)S(1)} %pad_maximum_fusion.3), channel_id=1, source_target_pairs={{4,20},{5,21},{6,22},{7,23},{16,0},{17,1},{18,2},{19,3},{20,36},{2... | collective-permute-start | bytes 196616 | tf_op jit(solution)/shard_map/ppermute | solution.py:321
  27.4 8.9 %collective-permute-start.1 = (bf16[4,64,128]{2,1,0:T(8,128)(2,1)S(1)}, bf16[4,64,128]{2,1,0:T(8,128)(2,1)S(1)}, u32[]{:S(2)}, u32[]{:S(2)}) collective-permute-start(bf16[4,64,128]{2,1,0:T(8,128)(2,1)S(1)} %slice_select_fusion), channel_id=1, source_target_pairs={{0,8},{8,0},{1,9},{9,1},{2,10},{10,2},{3,11},{11,3},{4,12},{12,4},... | collective-permute-start | bytes 196616 | tf_op jit(solution)/shard_map/ppermute | solution.py:324
  37.7 23.4 %all-to-all-start.1 = ((bf16[8,3,192,128]{3,2,1,0:T(8,128)(2,1)}), bf16[8,3,192,128]{3,2,1,0:T(8,128)(2,1)S(1)}, u32[]{:S(2)}, u32[]{:S(2)}) async-start(bf16[8,3,192,128]{3,2,1,0:T(8,128)(2,1)} %pad_maximum_fusion), calls=%async_computation.1 | async-start | bytes 2359296 | tf_op jit(solution)/shard_map/all_to_all | solution.py:336
  47.5 2.9 %copy-start = (bf16[6,3,256,768]{3,2,1,0:T(8,128)(2,1)}, bf16[6,3,256,768]{3,2,1,0:T(8,128)(2,1)S(1)}, u32[]{:S(2)}) copy-start(bf16[6,3,256,768]{3,2,1,0:T(8,128)(2,1)S(1)} %shard_map.130.band_ref) | copy-start | bytes 21233668
  61.1 3.0 %copy-start.1 = (bf16[6,3,256,768]{3,2,1,0:T(8,128)(2,1)S(1)}, bf16[6,3,256,768]{3,2,1,0:T(8,128)(2,1)}, u32[]{:S(2)}) copy-start(bf16[6,3,256,768]{3,2,1,0:T(8,128)(2,1)} %copy-done) | copy-start | bytes 21233668
  82.1 43.3 %copy-start.3 = (bf16[8,128,128]{2,1,0:T(8,128)(2,1)S(1)}, bf16[8,128,128]{2,1,0:T(8,128)(2,1)}, u32[]{:S(2)}) copy-start(bf16[8,128,128]{2,1,0:T(8,128)(2,1)} %weights_ref.3) | copy-start | bytes 786436
  82.1 43.3 %copy-start.6 = (s32[8,8]{1,0:T(8,128)S(1)}, s32[8,8]{1,0:T(8,128)}, u32[]{:S(2)}) copy-start(s32[8,8]{1,0:T(8,128)} %bricks_ref.3) | copy-start | bytes 772
  82.1 43.3 %copy-start.8 = (s32[8,8]{1,0:T(8,128)S(1)}, s32[8,8]{1,0:T(8,128)}, u32[]{:S(2)}) copy-start(s32[8,8]{1,0:T(8,128)} %rows_ref.3) | copy-start | bytes 772
  117.8 12.6 %all-to-all-start.4 = ((f32[8,24,128]{2,1,0:T(8,128)}), f32[8,24,128]{2,1,0:T(8,128)S(1)}, u32[]{:S(2)}, u32[]{:S(2)}) async-start(f32[8,24,128]{2,1,0:T(8,128)} %broadcast_in_dim.48), calls=%async_computation.4 | async-start | bytes 196608 | tf_op jit(solution)/shard_map/all_to_all | solution.py:263

commit v2 on v1

--- a/solution.py
+++ b/solution.py
@@ -1,3 +1,4 @@
+import functools
 import math
 
 import jax
@@ -29,6 +30,10 @@
 
 def vmem_spec():
     return pl.BlockSpec(memory_space=pltpu.VMEM)
+
+
+def hbm_spec():
+    return pl.BlockSpec(memory_space=pltpu.HBM)
 
 
 def smem_spec():
@@ -50,32 +55,50 @@
                     ]
 
 
-def lift_kernel(bricks_ref, rows_ref, feats_ref, weights_ref, out_ref, total):
+def lift_kernel(targets_ref, feats_hbm, weights_hbm, out_ref, feats, weights, total, sems):
+    fetch_feats = pltpu.make_async_copy(feats_hbm, feats, sems.at[0])
+    fetch_weights = pltpu.make_async_copy(weights_hbm, weights, sems.at[1])
+    fetch_feats.start()
+    fetch_weights.start()
     total[...] = jnp.zeros_like(total)
-    tiles, slots = bricks_ref.shape
+    tiles, slots = targets_ref.shape
+    fetch_feats.wait()
+    fetch_weights.wait()
     for k in range(slots):
         blocks = lax.dot_general(
-            feats_ref[...], weights_ref[k], (((1,), (1,)), ((), ())), preferred_element_type=F32
+            feats[...], weights[k], (((1,), (1,)), ((), ())), preferred_element_type=F32
         )
         for t in range(tiles):
-            row = bricks_ref[t, k] * YB + rows_ref[t, k]
-            total[row] += blocks[t * C : (t + 1) * C, :]
+            total[targets_ref[t, k]] += blocks[t * C : (t + 1) * C, :]
     out_ref[...] = total[...].astype(BF16).reshape(out_ref.shape)
 
 
-def camera_kernel(bricks_ref, rows_ref, arrived_ref, weights_ref, out_ref, chosen):
-    tiles, slots = bricks_ref.shape
+def camera_kernel(targets_ref, arrived_ref, weights_ref, out_ref, chosen):
+    tiles, slots = targets_ref.shape
     for k in range(slots):
         for t in range(tiles):
-            at = pl.multiple_of(rows_ref[t, k] * C, C)
+            target = targets_ref[t, k]
+            at = pl.multiple_of(lax.rem(target, YB) * C, C)
             chosen[t * C : (t + 1) * C, k * X : (k + 1) * X] = arrived_ref[
-                bricks_ref[t, k], pl.ds(at, C), :
+                lax.div(target, YB), pl.ds(at, C), :
             ]
     out_ref[...] = jnp.dot(
         chosen[...], weights_ref[...].reshape(slots * X, X), preferred_element_type=F32
     )
 
 
+def spread_kernel(scale, sums_ref, weight_ref, bias_ref):
+    for q in range(27):
+        layer, a, c = q // 9, q // 3 % 3, q % 3
+        for b in range(3):
+            row = (q // 8 * 3 + b) * C
+            block = sums_ref[row : row + C, q % 8 * C : (q % 8 + 1) * C]
+            weight_ref[((layer * 3 + a) * 3 + b) * 3 + c] = block * scale
+    for layer in range(2):
+        lanes = slice((3 + layer) * C, (4 + layer) * C)
+        bias_ref[layer : layer + 1, :] = sums_ref[9 * C : 9 * C + 1, lanes] * scale
+
+
 def silu_and_slope(v):
     s = jax.nn.sigmoid(v)
     return v * s, s * (1.0 + v * (1.0 - s))
@@ -83,7 +106,7 @@
 
 def main_kernel(
     arrived_ref,
-    band_ref,
+    band_hbm,
     bias_ref,
     field_ref,
     payload_ref,
@@ -96,7 +119,12 @@
     slope1,
     slope2,
     up2,
+    band_ref,
+    sems,
 ):
+    fetches = [pltpu.make_async_copy(band_hbm.at[n], band_ref.at[n], sems.at[n]) for n in range(6)]
+    for n in (0, 3, 1, 4, 5, 2):
+        fetches[n].start()
     depth, height, view = (lax.axis_index(n) for n in ("depth", "height", "view"))
     lane = lax.broadcasted_iota(jnp.int32, (YC, X), 1)
     first_lane, last_lane = lane == 0, lane == X - 1
@@ -113,9 +141,9 @@
     def fetch(offset, kind):
         source = lax.rem(view + offset + VIEWS, VIEWS)
         if offset == -4:
-            kind = jnp.where(view < 4, 1, 0)
+            kind = jnp.where(view < VIEWS // 2, 1, 0)
         if offset == 4:
-            kind = jnp.where(view < 4, 0, 1)
+            kind = jnp.where(view < VIEWS // 2, 0, 1)
         part = arrived_ref[source, kind].astype(F32)
         own, rim = part[:HALF], part[HALF:]
         none = jnp.zeros((RIM, X), F32)
@@ -148,18 +176,21 @@
     for i in range(9):
         put(s_lift, i, fetch(i - 4, 0))
     for i in range(7):
-        put(s_grad, i, fetch(i - 3, 2))
+        put(s_grad, i, fetch(i - 3, 1))
 
     bias1, bias2 = bias_ref[0], bias_ref[1]
+    fetches[0].wait()
     for i, n in pairs(7):
         for j, pre in enumerate(conv(0, s_lift, i, n)):
             act, slope = silu_and_slope(pre + bias1)
             put(s_act1, i + j, masked(i + j - 3, act))
             if abs(i + j - 3) <= 1:
                 slope1[i + j - 2] = slope
+    fetches[3].wait()
     for i, n in pairs(5):
         for j, up in enumerate(conv(3, s_grad, i, n)):
             up2[i + j] = up
+    fetches[1].wait()
     for i, n in pairs(5):
         for j, pre in enumerate(conv(1, s_act1, i, n)):
             at = i + j
@@ -171,6 +202,7 @@
             if abs(at - 2) <= 1:
                 before = s_act1[YC : 2 * YC, (at + 1) * X : (at + 2) * X].astype(F32)
                 put(s_act2, at - 1, masked(at - 2, act + before))
+    fetches[4].wait()
     for i, n in pairs(3):
         for j, up in enumerate(conv(4, s_back2, i, n)):
             at = i + j
@@ -182,10 +214,12 @@
     def own_rows(plane):
         return jnp.where(low, plane[:HALF], plane[HALF:])
 
+    fetches[5].wait()
     (lift_grad,) = conv(5, s_back1, 0, 1)
     lift_grad = own_rows(lift_grad).astype(BF16)
     for v in range(VIEWS):
         payload_ref[v, :HALF, :] = lift_grad
+    fetches[2].wait()
     (field,) = conv(2, s_act2, 0, 1)
     field_ref[...] = own_rows(field).astype(BF16)
 
@@ -220,7 +254,10 @@
     for layer, plane in enumerate((slope1[1], slope2[...])):
         sums = jnp.sum(own_rows(plane), axis=1, keepdims=True)
         sums = jnp.broadcast_to(sums, (HALF, X)).reshape(YB, C, X).sum(axis=0)
-        packed[3] = jnp.where(group == 3 + layer, jnp.concatenate([sums] * 3, axis=0), packed[3])
+        out_at = lax.broadcasted_iota(jnp.int32, (C, X), 0)
+        to = lax.rem(lax.broadcasted_iota(jnp.int32, (C, X), 1), C)
+        sums = jnp.sum(jnp.where(out_at == to, sums, 0.0), axis=0, keepdims=True)
+        packed[3] = jnp.where(group == 3 + layer, jnp.broadcast_to(sums, (3 * C, X)), packed[3])
     for v in range(VIEWS):
         start = (v % 2) * 24
         rows = packed[v // 2][start : start + 24]
@@ -232,7 +269,7 @@
 def main_call(arrived, bands, bias):
     return pl.pallas_call(
         main_kernel,
-        in_specs=[vmem_spec()] * 3,
+        in_specs=[vmem_spec(), hbm_spec(), vmem_spec()],
         out_specs=[vmem_spec()] * 2,
         **call(
             main_kernel,
@@ -245,6 +282,8 @@
                 pltpu.VMEM((3, YC, X), F32),
                 pltpu.VMEM((YC, X), F32),
                 pltpu.VMEM((5, YC, X), F32),
+                pltpu.VMEM((6, 3, YC, 3 * YC), BF16),
+                pltpu.SemaphoreType.DMA((6,)),
             ],
             vmem=40,
             flops=10**10,
@@ -257,10 +296,10 @@
     return jnp.transpose(jnp.flip(weight, (2, 3, 4)), (1, 0, 2, 3, 4))
 
 
-def for_each(block, axes):
-    peers = lax.axis_size(axes)
+def for_each(block, axes, groups=None):
+    peers = len(groups[0]) if groups else lax.axis_size(axes)
     tiles = jnp.broadcast_to(block[None], (peers, *block.shape))
-    return lax.all_to_all(tiles, axes, 0, 0, tiled=True)
+    return lax.all_to_all(tiles, axes, 0, 0, axis_index_groups=groups, tiled=True)
 
 
 def body(
@@ -279,18 +318,24 @@
     height, view = lax.axis_index("height"), lax.axis_index("view")
     tiles, slots = tile_bricks.shape
 
+    targets = tile_bricks * YB + tile_rows
     partial = pl.pallas_call(
         lift_kernel,
-        in_specs=[smem_spec(), smem_spec(), vmem_spec(), vmem_spec()],
+        in_specs=[smem_spec(), hbm_spec(), hbm_spec()],
         out_specs=vmem_spec(),
         **call(
             lift_kernel,
             jax.ShapeDtypeStruct((views, HALF, X), BF16),
-            [pltpu.VMEM((views * YB, C, X), F32)],
+            [
+                pltpu.VMEM((tiles * C, X), BF16),
+                pltpu.VMEM((slots, X, X), BF16),
+                pltpu.VMEM((views * YB, C, X), F32),
+                pltpu.SemaphoreType.DMA((2,)),
+            ],
             flops=10**8,
             moved=10**6,
         ),
-    )(tile_bricks, tile_rows, camera_feats.reshape(tiles * C, X), footprint_slot_weights)
+    )(targets, camera_feats.reshape(tiles * C, X), footprint_slot_weights)
     pieces = lax.all_to_all(partial, "view", 0, 0, tiled=True)
 
     convs = [conv_first, conv_second, conv_third]
@@ -323,13 +368,13 @@
     facing = jnp.where(height == 0, planes[:, HALF - RIM :], planes[:, :RIM])
     rim = lax.ppermute(facing, "height", [(0, 1), (1, 0)])
     planes = jnp.concatenate([planes, rim], axis=1)
-    near = jnp.abs(lax.iota(jnp.int32, views) - view) <= views // 2
-    near = near[:, None, None]
+    away = jnp.abs(lax.iota(jnp.int32, views) - view)[:, None, None]
+    half = views // 2
+    own_grad = jnp.where(away < half, planes[1], planes[3])
     parts = jnp.stack(
         [
-            jnp.where(near, planes[0], planes[2]),
-            jnp.broadcast_to(planes[2], (views, *planes[2].shape)),
-            jnp.where(near, planes[1], planes[3]),
+            jnp.where(away <= half, planes[0], planes[2]),
+            jnp.where(away == half, planes[2], own_grad),
         ],
         axis=1,
     )
@@ -340,11 +385,18 @@
 
     sums = arrived[:, HALF:].astype(F32).sum(axis=0)
     sums = sums[:24] + sums[24:]
-    sums = for_each(sums, ("depth", "height")).sum(axis=0)
+    run = views
+    rings = [list(range(i, i + run)) for i in range(0, depths, run)]
+    sums = for_each(sums, "depth", rings).sum(axis=0)
+    rings = [
+        [(i * run + j) * heights + h for h in range(heights) for i in range(depths // run)]
+        for j in range(run)
+    ]
+    sums = for_each(sums, ("depth", "height"), rings).sum(axis=0)
 
     camera_grad = pl.pallas_call(
         camera_kernel,
-        in_specs=[smem_spec(), smem_spec(), vmem_spec(), vmem_spec()],
+        in_specs=[smem_spec(), vmem_spec(), vmem_spec()],
         out_specs=vmem_spec(),
         **call(
             camera_kernel,
@@ -353,14 +405,20 @@
             flops=10**8,
             moved=10**6,
         ),
-    )(tile_bricks, tile_rows, arrived, footprint_slot_weights)
-
-    sums = for_each(sums, "view").reshape(4, 3, C, 8, C)
+    )(targets, arrived, footprint_slot_weights)
+
+    sums = for_each(sums, "view").reshape(12 * C, X)
     scale = 1.0 / math.sqrt(YB * X * depths * heights * views)
-    sums = sums * scale
-    bias_gradient_pair = jnp.transpose(sums[3, 0, :, 3:5, 0])
-    sums = jnp.transpose(sums, (0, 3, 2, 4, 1)).reshape(32, C, C, 3)[:27]
-    weight_grads = jnp.transpose(sums.reshape(3, 3, 3, C, C, 3), (0, 3, 4, 1, 5, 2))
+    weight_grads, bias_gradient_pair = pl.pallas_call(
+        functools.partial(spread_kernel, scale),
+        in_specs=[vmem_spec()],
+        out_specs=[vmem_spec()] * 2,
+        **call(
+            spread_kernel,
+            (jax.ShapeDtypeStruct((81, C, C), F32), jax.ShapeDtypeStruct((2, C), F32)),
+        ),
+    )(sums)
+    weight_grads = jnp.transpose(weight_grads.reshape(3, 3, 3, 3, C, C), (0, 4, 5, 1, 2, 3))
     return (
         field.reshape(1, YB, C, X),
         camera_grad.reshape(tiles, C, X),

time: 133 us -> 125 us (0.940)
  blocking collectives: 46 us -> 39.1 us
  waiting for transfers between devices: 25 us -> 18.9 us
  Pallas kernels: 12.2 us -> 16.5 us
  other arithmetic: 1.53 us -> 4.25 us
  local copies, waits for them, and re-layouts: 14.7 us -> 13.1 us
    all_to_all x1 -> x2, blocking collectives: 35 us -> 28.1 us  [for_each(): lax.all_to_all(tiles, axes, 0, 0, axis_index_groups=groups, tiled=True)]
    all_to_all x1, waiting for transfers between devices: 10.7 us -> 5.94 us  [body(): arrived = lax.all_to_all(parts, 'view', 0, 0, tiled=True)]
    pallas_call x3 -> x4, Pallas kernels: 10.3 us -> 14.6 us  [the longest x1 10.1 us: main_call(): pl.pallas_call(main_kernel, in_specs=[vmem_spec(), hbm_spec(), vmem_spec(...]
    all_to_all x1, waiting for transfers between devices: 4.65 us -> 3.22 us  [body(): pieces = lax.all_to_all(partial, 'view', 0, 0, tiled=True)]
    unnamed x35 -> x24, local copies, waits for them, and re-layouts: 10.3 us -> 9.87 us
  transfers between devices with their start and end apart: 5 -> 5, of which waited for: 5 -> 5; matrix products, arithmetic and copies ran while one was open for 2% -> 4% of each run, Pallas kernels for 3% -> 3%
where the time goes in v2:
time: 125 us; the launch traced here: 124 us
  blocking collectives  39.1 us (31%)
  starting transfers between devices  31.4 us (25%)
  waiting for transfers between devices  18.9 us (15%)
  Pallas kernels  16.5 us (13%)
  local copies, waits for them, and re-layouts  13.1 us (10%)
  other arithmetic  4.25 us (3%)
    all_to_all x2, blocking collectives, for_each(): lax.all_to_all(tiles, axes, 0, 0, axis_index_groups=groups, tiled=True)  28.1 us
    all_to_all x1, blocking collectives, body(): arrived = lax.all_to_all(payload, 'view', 0, 0, tiled=True)  11 us
    all_to_all x1, starting transfers between devices, body(): pieces = lax.all_to_all(partial, 'view', 0, 0, tiled=True)  10.2 us
    pallas_call x1, Pallas kernels, main_call(): pl.pallas_call(main_kernel, in_specs=[vmem_spec(), hbm_spec(), vmem_spec(...  10.1 us
    unnamed x24, local copies, waits for them, and re-layouts  9.87 us
    all_to_all x1, starting transfers between devices, body(): arrived = lax.all_to_all(parts, 'view', 0, 0, tiled=True)  6.86 us
    all_to_all x1, starting transfers between devices, for_each(): lax.all_to_all(tiles, axes, 0, 0, axis_index_groups=groups, tiled=True)  6.84 us
    ppermute x1, starting transfers between devices, body(): rim = lax.ppermute(facing, 'height', [(0, 1), (1, 0)])  6.23 us
  transfers between devices with their start and end apart: 5, of which 5 were waited for; matrix products, arithmetic and copies ran while one was open for 4% of the time, Pallas kernels for 3%

profile of v2, /device:TPU:1, one launch (start us, length us, event | category | flops | bytes accessed | tf_op | source)
XLA Modules:
  0.0 124.1 jit_solution(10884442932678186521)
XLA Ops:
  1.3 0.9 copy-done.2
  3.1 1.9 %shard_map.129 = bf16[8,128,128]{2,1,0:T(8,128)(2,1)} custom-call(s32[8,8]{1,0:T(8,128)S(1)} %multiply_add_fusion.targets_ref, bf16[128,128]{1,0:T(8,128)(2,1)S(1)} %bitcast.39, bf16[8,128,128]{2,1,0:T(8,128)(2,1)S(1)} %copy-done.2), custom_call_target="tpu_custom_call" | custom-call | flops 100000000 | bytes 1000000 | tf_op jit(solution)/shard_map/pallas_call | solution.py:322
  4.9 10.2 %all-to-all-start = ((bf16[8,128,128]{2,1,0:T(8,128)(2,1)}), bf16[8,128,128]{2,1,0:T(8,128)(2,1)S(1)}, u32[]{:S(2)}, u32[]{:S(2)}) async-start(bf16[8,128,128]{2,1,0:T(8,128)(2,1)} %shard_map.129), calls=%async_computation | async-start | bytes 524288 | tf_op jit(solution)/shard_map/all_to_all | solution.py:339
  16.6 0.9 bitcast_dynamic-update-slice_fusion.5
  17.5 0.9 bitcast_dynamic-update-slice_fusion.4
  18.4 3.2 %all-to-all-done = bf16[8,128,128]{2,1,0:T(8,128)(2,1)S(1)} async-done(((bf16[8,128,128]{2,1,0:T(8,128)(2,1)}), bf16[8,128,128]{2,1,0:T(8,128)(2,1)S(1)}, u32[]{:S(2)}, u32[]{:S(2)}) %all-to-all-start) | async-done | bytes 262176 | tf_op jit(solution)/shard_map/all_to_all | solution.py:339
  22.5 1.3 %collective-permute-start = (bf16[2,128,128]{2,1,0:T(8,128)(2,1)S(1)}, bf16[2,128,128]{2,1,0:T(8,128)(2,1)S(1)}, u32[]{:S(2)}, u32[]{:S(2)}) collective-permute-start(bf16[2,128,128]{2,1,0:T(8,128)(2,1)S(1)} %pad_maximum_fusion.3), channel_id=1, source_target_pairs={{4,20},{5,21},{6,22},{7,23},{16,0},{17,1},{18,2},{19,3},{20,36},{2... | collective-permute-start | bytes 196616 | tf_op jit(solution)/shard_map/ppermute | solution.py:366
  23.8 3.7 %collective-permute-done = bf16[2,128,128]{2,1,0:T(8,128)(2,1)S(1)} collective-permute-done((bf16[2,128,128]{2,1,0:T(8,128)(2,1)S(1)}, bf16[2,128,128]{2,1,0:T(8,128)(2,1)S(1)}, u32[]{:S(2)}, u32[]{:S(2)}) %collective-permute-start) | collective-permute-done | bytes 65568 | tf_op jit(solution)/shard_map/ppermute | solution.py:366
  28.3 6.2 %collective-permute-start.1 = (bf16[4,64,128]{2,1,0:T(8,128)(2,1)S(1)}, bf16[4,64,128]{2,1,0:T(8,128)(2,1)S(1)}, u32[]{:S(2)}, u32[]{:S(2)}) collective-permute-start(bf16[4,64,128]{2,1,0:T(8,128)(2,1)S(1)} %slice_select_fusion), channel_id=1, source_target_pairs={{0,8},{8,0},{1,9},{9,1},{2,10},{10,2},{3,11},{11,3},{4,12},{12,4},... | collective-permute-start | bytes 196616 | tf_op jit(solution)/shard_map/ppermute | solution.py:369
  34.5 2.7 %collective-permute-done.1 = bf16[4,64,128]{2,1,0:T(8,128)(2,1)S(1)} collective-permute-done((bf16[4,64,128]{2,1,0:T(8,128)(2,1)S(1)}, bf16[4,64,128]{2,1,0:T(8,128)(2,1)S(1)}, u32[]{:S(2)}, u32[]{:S(2)}) %collective-permute-start.1) | collective-permute-done | bytes 65568 | tf_op jit(solution)/shard_map/ppermute | solution.py:369
  38.2 1.0 pad_maximum_fusion
  39.1 6.9 %all-to-all-start.1 = ((bf16[8,2,192,128]{3,2,1,0:T(8,128)(2,1)}), bf16[8,2,192,128]{3,2,1,0:T(8,128)(2,1)S(1)}, u32[]{:S(2)}, u32[]{:S(2)}) async-start(bf16[8,2,192,128]{3,2,1,0:T(8,128)(2,1)} %pad_maximum_fusion), calls=%async_computation.1 | async-start | bytes 1572864 | tf_op jit(solution)/shard_map/all_to_all | solution.py:381
  47.5 1.9 %shard_map.130.band_hbm = bf16[6,3,256,768]{3,2,1,0:T(8,128)(2,1)S(1)} custom-call(bf16[864,128]{1,0:T(8,128)(2,1)S(1)} %pad.4.taps_ref), custom_call_target="tpu_custom_call" | custom-call | flops 1000000000 | bytes 7000000 | tf_op jit(solution)/shard_map/pallas_call | solution.py:345
  49.4 2.9 %copy-done = bf16[6,3,256,768]{3,2,1,0:T(8,128)(2,1)} copy-done((bf16[6,3,256,768]{3,2,1,0:T(8,128)(2,1)}, bf16[6,3,256,768]{3,2,1,0:T(8,128)(2,1)S(1)}, u32[]{:S(2)}) %copy-start) | copy-done | bytes 7077912
  52.4 5.9 %all-to-all-done.1.arrived_ref = bf16[8,2,192,128]{3,2,1,0:T(8,128)(2,1)S(1)} async-done(((bf16[8,2,192,128]{3,2,1,0:T(8,128)(2,1)}), bf16[8,2,192,128]{3,2,1,0:T(8,128)(2,1)S(1)}, u32[]{:S(2)}, u32[]{:S(2)}) %all-to-all-start.1) | async-done | bytes 786464 | tf_op jit(solution)/shard_map/all_to_all | solution.py:381
  58.3 3.0 %copy-done.1 = bf16[6,3,256,768]{3,2,1,0:T(8,128)(2,1)S(1)} copy-done((bf16[6,3,256,768]{3,2,1,0:T(8,128)(2,1)S(1)}, bf16[6,3,256,768]{3,2,1,0:T(8,128)(2,1)}, u32[]{:S(2)}) %copy-start.1) | copy-done | bytes 7077912
  61.3 10.1 %shard_map.131 = (bf16[128,128]{1,0:T(8,128)(2,1)}, bf16[8,176,128]{2,1,0:T(8,128)(2,1)S(1)}) custom-call(bf16[8,2,192,128]{3,2,1,0:T(8,128)(2,1)S(1)} %all-to-all-done.1.arrived_ref, bf16[6,3,256,768]{3,2,1,0:T(8,128)(2,1)S(1)} %copy-done.1, f32[2,256,1]{2,1,0:T(8,128)S(1)} %copy.28.bias_ref), custom_call_target="tpu_custom_call" | custom-call | flops 10000000000 | bytes 10000000 | tf_op jit(solution)/shard_map/pallas_call | solution.py:270
  71.4 11.0 %all_to_all.30.arrived_ref = bf16[8,176,128]{2,1,0:T(8,128)(2,1)S(1)} all-to-all(bf16[8,176,128]{2,1,0:T(8,128)(2,1)S(1)} %get-tuple-element.9), channel_id=1, replica_groups=mesh['depth'=32,'height'=2,'view'=8] {'view'}, dimensions={0} | all-to-all | bytes 720896 | tf_op jit(solution)/shard_map/all_to_all | solution.py:384
  82.4 13.3 %all_to_all.31 = f32[8,24,128]{2,1,0:T(8,128)S(1)} all-to-all(f32[8,24,128]{2,1,0:T(8,128)S(1)} %broadcast_in_dim.67), channel_id=1, replica_groups={{0,16,32,48,64,80,96,112},{128,144,160,176,192,208,224,240},{256,272,28..., dimensions={0} | all-to-all | bytes 196608 | tf_op jit(solution)/shard_map/all_to_all | solution.py:302
  95.8 14.8 %all_to_all.32 = f32[8,24,128]{2,1,0:T(8,128)S(1)} all-to-all(f32[8,24,128]{2,1,0:T(8,128)S(1)} %broadcast_in_dim.68), channel_id=1, replica_groups={{0,128,256,384,8,136,264,392},{16,144,272,400,24,152,280,408},{32,160,2..., dimensions={0} | all-to-all | bytes 196608 | tf_op jit(solution)/shard_map/all_to_all | solution.py:302
  111.2 6.8 %all-to-all-start.5 = ((f32[8,24,128]{2,1,0:T(8,128)}), f32[8,24,128]{2,1,0:T(8,128)S(1)}, u32[]{:S(2)}, u32[]{:S(2)}) async-start(f32[8,24,128]{2,1,0:T(8,128)} %broadcast_in_dim.69), calls=%async_computation.5 | async-start | bytes 196608 | tf_op jit(solution)/shard_map/all_to_all | solution.py:302
  118.0 1.7 %shard_map.132 = f32[128,128]{1,0:T(8,128)} custom-call(s32[8,8]{1,0:T(8,128)S(1)} %multiply_add_fusion.targets_ref, bf16[8,176,128]{2,1,0:T(8,128)(2,1)S(1)} %all_to_all.30.arrived_ref, bf16[8,128,128]{2,1,0:T(8,128)(2,1)S(1)} %copy-done.3), custom_call_target="tpu_custom_call" | custom-call | flops 100000000 | bytes 1000000 | tf_op jit(solution)/shard_map/pallas_call | solution.py:397
  119.7 3.3 %all-to-all-done.5 = f32[8,24,128]{2,1,0:T(8,128)S(1)} async-done(((f32[8,24,128]{2,1,0:T(8,128)}), f32[8,24,128]{2,1,0:T(8,128)S(1)}, u32[]{:S(2)}, u32[]{:S(2)}) %all-to-all-start.5) | async-done | bytes 98336 | tf_op jit(solution)/shard_map/all_to_all | solution.py:302
  123.0 1.1 shard_map.133
  (46 shorter events, 7.7 us)
Async XLA Ops:
  1.3 0.9 copy-start.2
  2.3 0.8 copy-start.4
  3.0 43.0 %copy-start.5 = (bf16[16,16,3,3,3]{1,0,4,3,2:T(8,128)(2,1)S(1)}, bf16[16,16,3,3,3]{1,0,4,3,2:T(8,128)(2,1)}, u32[]{:S(2)}) copy-start(bf16[16,16,3,3,3]{1,0,4,3,2:T(8,128)(2,1)} %param.14) | copy-start | bytes 41476
  3.0 43.1 %copy-start.6 = (bf16[16,16,3,3,3]{1,0,4,3,2:T(8,128)(2,1)S(1)}, bf16[16,16,3,3,3]{1,0,4,3,2:T(8,128)(2,1)}, u32[]{:S(2)}) copy-start(bf16[16,16,3,3,3]{1,0,4,3,2:T(8,128)(2,1)} %param.15) | copy-start | bytes 41476
  3.1 43.2 %copy-start.7 = (bf16[16,16,3,3,3]{1,0,4,3,2:T(8,128)(2,1)S(1)}, bf16[16,16,3,3,3]{1,0,4,3,2:T(8,128)(2,1)}, u32[]{:S(2)}) copy-start(bf16[16,16,3,3,3]{1,0,4,3,2:T(8,128)(2,1)} %param.16) | copy-start | bytes 41476
  4.9 16.7 %all-to-all-start = ((bf16[8,128,128]{2,1,0:T(8,128)(2,1)}), bf16[8,128,128]{2,1,0:T(8,128)(2,1)S(1)}, u32[]{:S(2)}, u32[]{:S(2)}) async-start(bf16[8,128,128]{2,1,0:T(8,128)(2,1)} %shard_map.129), calls=%async_computation | async-start | bytes 524288 | tf_op jit(solution)/shard_map/all_to_all | solution.py:339
  22.5 5.0 %collective-permute-start = (bf16[2,128,128]{2,1,0:T(8,128)(2,1)S(1)}, bf16[2,128,128]{2,1,0:T(8,128)(2,1)S(1)}, u32[]{:S(2)}, u32[]{:S(2)}) collective-permute-start(bf16[2,128,128]{2,1,0:T(8,128)(2,1)S(1)} %pad_maximum_fusion.3), channel_id=1, source_target_pairs={{4,20},{5,21},{6,22},{7,23},{16,0},{17,1},{18,2},{19,3},{20,36},{2... | collective-permute-start | bytes 196616 | tf_op jit(solution)/shard_map/ppermute | solution.py:366
  28.3 8.9 %collective-permute-start.1 = (bf16[4,64,128]{2,1,0:T(8,128)(2,1)S(1)}, bf16[4,64,128]{2,1,0:T(8,128)(2,1)S(1)}, u32[]{:S(2)}, u32[]{:S(2)}) collective-permute-start(bf16[4,64,128]{2,1,0:T(8,128)(2,1)S(1)} %slice_select_fusion), channel_id=1, source_target_pairs={{0,8},{8,0},{1,9},{9,1},{2,10},{10,2},{3,11},{11,3},{4,12},{12,4},... | collective-permute-start | bytes 196616 | tf_op jit(solution)/shard_map/ppermute | solution.py:369
  39.1 19.2 %all-to-all-start.1 = ((bf16[8,2,192,128]{3,2,1,0:T(8,128)(2,1)}), bf16[8,2,192,128]{3,2,1,0:T(8,128)(2,1)S(1)}, u32[]{:S(2)}, u32[]{:S(2)}) async-start(bf16[8,2,192,128]{3,2,1,0:T(8,128)(2,1)} %pad_maximum_fusion), calls=%async_computation.1 | async-start | bytes 1572864 | tf_op jit(solution)/shard_map/all_to_all | solution.py:381
  49.4 2.9 %copy-start = (bf16[6,3,256,768]{3,2,1,0:T(8,128)(2,1)}, bf16[6,3,256,768]{3,2,1,0:T(8,128)(2,1)S(1)}, u32[]{:S(2)}) copy-start(bf16[6,3,256,768]{3,2,1,0:T(8,128)(2,1)S(1)} %shard_map.130.band_hbm) | copy-start | bytes 21233668
  58.3 3.0 %copy-start.1 = (bf16[6,3,256,768]{3,2,1,0:T(8,128)(2,1)S(1)}, bf16[6,3,256,768]{3,2,1,0:T(8,128)(2,1)}, u32[]{:S(2)}) copy-start(bf16[6,3,256,768]{3,2,1,0:T(8,128)(2,1)} %copy-done) | copy-start | bytes 21233668
  61.3 56.7 %copy-start.3 = (bf16[8,128,128]{2,1,0:T(8,128)(2,1)S(1)}, bf16[8,128,128]{2,1,0:T(8,128)(2,1)}, u32[]{:S(2)}) copy-start(bf16[8,128,128]{2,1,0:T(8,128)(2,1)} %weights_ref.1) | copy-start | bytes 786436
  111.2 11.8 %all-to-all-start.5 = ((f32[8,24,128]{2,1,0:T(8,128)}), f32[8,24,128]{2,1,0:T(8,128)S(1)}, u32[]{:S(2)}, u32[]{:S(2)}) async-start(f32[8,24,128]{2,1,0:T(8,128)} %broadcast_in_dim.69), calls=%async_computation.5 | async-start | bytes 196608 | tf_op jit(solution)/shard_map/all_to_all | solution.py:302

commit v3 on v2

--- a/solution.py
+++ b/solution.py
@@ -3,6 +3,7 @@
 
 import jax
 import jax.numpy as jnp
+import numpy as np
 from jax import lax
 from jax.experimental import pallas as pl
 from jax.experimental.pallas import tpu as pltpu
@@ -11,9 +12,10 @@
 C = 16
 X = 128
 YB = 8
-YC = 256
 HALF = 128
 RIM = 64
+YC = HALF + RIM
+K3 = 3 * YC
 VIEWS = 8
 F32, BF16 = jnp.float32, jnp.bfloat16
 MIB = 1 << 20
@@ -40,19 +42,52 @@
     return pl.BlockSpec(memory_space=pltpu.SMEM)
 
 
-def band_kernel(taps_ref, band_ref):
-    at = lax.broadcasted_iota(jnp.int32, (X, YC), 0)
-    to = lax.broadcasted_iota(jnp.int32, (X, YC), 1)
-    for y in range(16):
-        spread = jnp.where(to == at + (y - 1) * C, 1.0, 0.0).astype(BF16)
+def band_kernel(taps_ref, base_ref, band_ref):
+    lane = lax.broadcasted_iota(jnp.int32, (4 * X, 3 * K3), 1)
+    last = YC // C - 1
+    for y in range(last + 1):
+        kind = 1 if y == 0 else 2 if y == last else 0
+        hit = lane == base_ref[:, kind : kind + 1] + y * C
+        spread = jnp.where(hit, 1.0, 0.0).astype(BF16)
         rows = jnp.dot(taps_ref[...], spread, preferred_element_type=F32).astype(BF16)
         for n in range(6):
-            for a in range(3):
-                for c in range(3):
-                    first = ((n * 3 + a) * 3 + c) * C
-                    band_ref[n, a, y * C : (y + 1) * C, c * YC : (c + 1) * YC] = rows[
-                        first : first + C, :
-                    ]
+            band_ref[n, y * C : (y + 1) * C, :] = rows[n * C : (n + 1) * C, :]
+
+
+def band_places():
+    a, c, b, i = np.indices((3, 3, 3, C)).reshape(4, -1)
+    base = a * K3 + c * YC + (b - 1) * C + i
+    base = np.stack([base, np.where(b == 0, -(10**6), base), np.where(b == 2, -(10**6), base)], 1)
+    out = np.full((4 * X, 3), -(10**6), np.int32)
+    out[: base.shape[0]] = base
+    return out
+
+
+def own_kernel(pieces_ref, grad_hbm, own_ref, sem):
+    fetch = pltpu.make_async_copy(grad_hbm, own_ref.at[1], sem)
+    fetch.start()
+    own_ref[0] = pieces_ref[...].astype(F32).sum(axis=0).astype(BF16)
+    fetch.wait()
+
+
+def facing_kernel(own_ref, far_ref, facing_ref):
+    at = pl.multiple_of((1 - lax.axis_index("height")) * RIM, RIM)
+    facing_ref[0:2] = own_ref[:, pl.ds(at, RIM), :]
+    facing_ref[2:4] = far_ref[:, pl.ds(at, RIM), :]
+
+
+def parts_kernel(own_ref, far_ref, rim_ref, parts_ref, planes):
+    height, view = lax.axis_index("height"), lax.axis_index("view")
+    own_at = pl.multiple_of(height * RIM, RIM)
+    rim_at = pl.multiple_of((1 - height) * HALF, RIM)
+    planes[0:2, pl.ds(own_at, HALF), :] = own_ref[...]
+    planes[2:4, pl.ds(own_at, HALF), :] = far_ref[...]
+    planes[:, pl.ds(rim_at, RIM), :] = rim_ref[...]
+    half = VIEWS // 2
+    for v in range(VIEWS):
+        away = jnp.abs(v - view)
+        parts_ref[v, 0] = planes[jnp.where(away <= half, 0, 2)]
+        parts_ref[v, 1] = planes[jnp.where(away == half, 2, jnp.where(away < half, 1, 3))]
 
 
 def lift_kernel(targets_ref, feats_hbm, weights_hbm, out_ref, feats, weights, total, sems):
@@ -134,7 +169,7 @@
         cols = slice(index * X, (index + 1) * X)
         dst[0:YC, cols] = jnp.where(first_lane, 0.0, pltpu.roll(plane, 1, 1)).astype(BF16)
         dst[YC : 2 * YC, cols] = plane.astype(BF16)
-        dst[2 * YC : 3 * YC, cols] = jnp.where(last_lane, 0.0, pltpu.roll(plane, X - 1, 1)).astype(
+        dst[2 * YC : K3, cols] = jnp.where(last_lane, 0.0, pltpu.roll(plane, X - 1, 1)).astype(
             BF16
         )
 
@@ -144,14 +179,7 @@
             kind = jnp.where(view < VIEWS // 2, 1, 0)
         if offset == 4:
             kind = jnp.where(view < VIEWS // 2, 0, 1)
-        part = arrived_ref[source, kind].astype(F32)
-        own, rim = part[:HALF], part[HALF:]
-        none = jnp.zeros((RIM, X), F32)
-        return jnp.where(
-            low,
-            jnp.concatenate([own, rim, none], axis=0),
-            jnp.concatenate([none, rim, own], axis=0),
-        )
+        return arrived_ref[source, kind].astype(F32)
 
     def inside(offset):
         z = depth * VIEWS + view + offset
@@ -161,14 +189,19 @@
         return jnp.where(inside(offset), plane, 0.0)
 
     def conv(n, src, start, count):
-        out = jnp.zeros((YC, count * X), F32)
-        for a in range(3):
-            out += jnp.dot(
-                band_ref[n, a],
-                src[:, (start + a) * X : (start + a + count) * X],
-                preferred_element_type=F32,
-            )
+        taken = [src[:, (start + a) * X : (start + a + count) * X] for a in range(3)]
+        out = jnp.dot(band_ref[n], jnp.concatenate(taken, axis=0), preferred_element_type=F32)
         return [out[:, i * X : (i + 1) * X] for i in range(count)]
+
+    own_at = pl.multiple_of(height * RIM, RIM)
+
+    def conv_own(n, src):
+        taken = [src[:, a * X : (a + 1) * X] for a in range(3)]
+        return jnp.dot(
+            band_ref[n, pl.ds(own_at, HALF), :],
+            jnp.concatenate(taken, axis=0),
+            preferred_element_type=F32,
+        )
 
     def pairs(count):
         return [(i, min(2, count - i)) for i in range(0, count, 2)]
@@ -212,27 +245,26 @@
             put(s_back1, at, masked(at - 1, back))
 
     def own_rows(plane):
-        return jnp.where(low, plane[:HALF], plane[HALF:])
+        return jnp.where(low, plane[:HALF], plane[RIM:])
 
     fetches[5].wait()
-    (lift_grad,) = conv(5, s_back1, 0, 1)
-    lift_grad = own_rows(lift_grad).astype(BF16)
+    lift_grad = conv_own(5, s_back1).astype(BF16)
     for v in range(VIEWS):
         payload_ref[v, :HALF, :] = lift_grad
     fetches[2].wait()
-    (field,) = conv(2, s_act2, 0, 1)
-    field_ref[...] = own_rows(field).astype(BF16)
-
-    own_at = pl.multiple_of(YC + height * HALF, HALF)
-    wide = (HALF, 3 * YC)
-    row_y = lax.broadcasted_iota(jnp.int32, wide, 0) // C + height * YB
-    col_y = lax.rem(lax.broadcasted_iota(jnp.int32, wide, 1), YC) // C
+    field_ref[...] = conv_own(2, s_act2).astype(BF16)
+
+    wide = (HALF, K3)
+    row_y = (lax.broadcasted_iota(jnp.int32, wide, 0) >> 4) + height * (RIM // C)
+    col = lax.broadcasted_iota(jnp.int32, wide, 1)
+    col_y = (col - jnp.where(col >= 2 * YC, 2 * YC, jnp.where(col >= YC, YC, 0))) >> 4
     bands = [col_y == row_y + (b - 1) for b in range(3)]
     group = lax.broadcasted_iota(jnp.int32, (3 * C, X), 1) // C
+    left = lax.broadcasted_iota(jnp.int32, (3 * C, X), 1) < X // 2
     packed = [jnp.zeros((3 * C, X), F32) for _ in range(4)]
     layers = ((s_back1, 1, s_lift, 4), (s_back2, 2, s_act1, 3), (s_grad, 3, s_act2, 1))
     for layer, (g_ref, g_at, v_ref, v_at) in enumerate(layers):
-        g = g_ref[pl.ds(own_at, HALF), g_at * X : (g_at + 1) * X]
+        g = g_ref[pl.ds(YC + own_at, HALF), g_at * X : (g_at + 1) * X]
         for a in range(3):
             at = v_at + a - 1
             products = lax.dot_general(
@@ -242,11 +274,17 @@
                 preferred_element_type=F32,
             )
             by_row = [
-                jnp.where(band, products, 0.0).reshape(YB, C, 3 * YC).sum(axis=0) for band in bands
+                jnp.where(band, products, 0.0).reshape(YB, C, K3).sum(axis=0) for band in bands
             ]
             by_row = jnp.concatenate(by_row, axis=0)
-            for c in range(3):
-                part = by_row[:, c * YC : c * YC + X] + by_row[:, c * YC + X : (c + 1) * YC]
+            end = jnp.concatenate([by_row[:, 4 * X :], jnp.zeros((3 * C, X // 2), F32)], axis=1)
+            shared = by_row[:, X : 2 * X]
+            parts = (
+                by_row[:, :X] + jnp.where(left, shared, 0.0),
+                by_row[:, 2 * X : 3 * X] + jnp.where(left, 0.0, shared),
+                by_row[:, 3 * X : 4 * X] + end,
+            )
+            for c, part in enumerate(parts):
                 for step in (64, 32, 16):
                     part = part + pltpu.roll(part, step, 1)
                 q = (layer * 3 + a) * 3 + c
@@ -277,15 +315,15 @@
                 jax.ShapeDtypeStruct((HALF, X), BF16),
                 jax.ShapeDtypeStruct((VIEWS, HALF + 48, X), BF16),
             ),
-            [pltpu.VMEM((3 * YC, n * X), BF16) for n in (9, 7, 7, 3, 5, 3)]
+            [pltpu.VMEM((K3, n * X), BF16) for n in (9, 7, 7, 3, 5, 3)]
             + [
                 pltpu.VMEM((3, YC, X), F32),
                 pltpu.VMEM((YC, X), F32),
                 pltpu.VMEM((5, YC, X), F32),
-                pltpu.VMEM((6, 3, YC, 3 * YC), BF16),
+                pltpu.VMEM((6, YC, 3 * K3), BF16),
                 pltpu.SemaphoreType.DMA((6,)),
             ],
-            vmem=40,
+            vmem=58,
             flops=10**10,
             moved=10**7,
         ),
@@ -315,7 +353,6 @@
     out_grad,
 ):
     depths, heights, views = (lax.axis_size(n) for n in ("depth", "height", "view"))
-    height, view = lax.axis_index("height"), lax.axis_index("view")
     tiles, slots = tile_bricks.shape
 
     targets = tile_bricks * YB + tile_rows
@@ -332,6 +369,7 @@
                 pltpu.VMEM((views * YB, C, X), F32),
                 pltpu.SemaphoreType.DMA((2,)),
             ],
+            vmem=62,
             flops=10**8,
             moved=10**6,
         ),
@@ -340,23 +378,32 @@
 
     convs = [conv_first, conv_second, conv_third]
     convs = jnp.stack(convs + [flip_swap(w) for w in reversed(convs)])
-    taps = jnp.transpose(convs, (0, 3, 5, 1, 4, 2)).reshape(-1, 3 * C)
-    taps = jnp.pad(taps, ((0, 0), (0, X - 3 * C)))
+    taps = jnp.transpose(convs, (0, 1, 3, 5, 4, 2)).reshape(6 * C, 27 * C)
+    taps = jnp.pad(taps, ((0, 0), (0, 4 * X - 27 * C)))
     bands = pl.pallas_call(
         band_kernel,
-        in_specs=[vmem_spec()],
+        in_specs=[vmem_spec()] * 2,
         out_specs=vmem_spec(),
         **call(
             band_kernel,
-            jax.ShapeDtypeStruct((6, 3, YC, 3 * YC), BF16),
+            jax.ShapeDtypeStruct((6, YC, 3 * K3), BF16),
             flops=10**9,
             moved=7 * 10**6,
         ),
-    )(taps)
-    bias = jnp.stack([jnp.tile(b, 16) for b in (bias_first, bias_second)])[:, :, None]
-
-    lifted = pieces.astype(F32).sum(axis=0).astype(BF16)
-    own = jnp.stack([lifted, out_grad.reshape(HALF, X)])
+    )(taps, band_places())
+    bias = jnp.stack([jnp.tile(b, YC // C) for b in (bias_first, bias_second)])[:, :, None]
+
+    own = pl.pallas_call(
+        own_kernel,
+        in_specs=[vmem_spec(), hbm_spec()],
+        out_specs=vmem_spec(),
+        **call(
+            own_kernel,
+            jax.ShapeDtypeStruct((2, HALF, X), BF16),
+            [pltpu.SemaphoreType.DMA],
+            vmem=60,
+        ),
+    )(pieces, out_grad.reshape(HALF, X))
     moves = []
     for d in range(depths):
         for v in range(views):
@@ -364,20 +411,23 @@
             if 0 <= to < depths:
                 moves.append((d * views + v, to * views + v))
     far = lax.ppermute(own, ("depth", "view"), moves)
-    planes = jnp.concatenate([own, far])
-    facing = jnp.where(height == 0, planes[:, HALF - RIM :], planes[:, :RIM])
+    facing = pl.pallas_call(
+        facing_kernel,
+        in_specs=[vmem_spec()] * 2,
+        out_specs=vmem_spec(),
+        **call(facing_kernel, jax.ShapeDtypeStruct((4, RIM, X), BF16)),
+    )(own, far)
     rim = lax.ppermute(facing, "height", [(0, 1), (1, 0)])
-    planes = jnp.concatenate([planes, rim], axis=1)
-    away = jnp.abs(lax.iota(jnp.int32, views) - view)[:, None, None]
-    half = views // 2
-    own_grad = jnp.where(away < half, planes[1], planes[3])
-    parts = jnp.stack(
-        [
-            jnp.where(away <= half, planes[0], planes[2]),
-            jnp.where(away == half, planes[2], own_grad),
-        ],
-        axis=1,
-    )
+    parts = pl.pallas_call(
+        parts_kernel,
+        in_specs=[vmem_spec()] * 3,
+        out_specs=vmem_spec(),
+        **call(
+            parts_kernel,
+            jax.ShapeDtypeStruct((VIEWS, 2, YC, X), BF16),
+            [pltpu.VMEM((4, YC, X), BF16)],
+        ),
+    )(own, far, rim)
     arrived = lax.all_to_all(parts, "view", 0, 0, tiled=True)
 
     field, payload = main_call(arrived, bands, bias)

time: 125 us -> 124 us (level)
  blocking collectives: 39.1 us -> 57 us
  starting transfers between devices: 31.4 us -> 20.4 us
  waiting for transfers between devices: 18.9 us -> 11.7 us
  Pallas kernels: 16.5 us -> 21.5 us
  other arithmetic: 4.25 us -> 1.4 us
  local copies, waits for them, and re-layouts: 13.1 us -> 10.5 us
    all_to_all x0 -> x1, blocking collectives: none -> 17.4 us  [body(): pieces = lax.all_to_all(partial, 'view', 0, 0, tiled=True)]
    all_to_all x1 -> x0, starting transfers between devices: 10.2 us -> none  [body(): pieces = lax.all_to_all(partial, 'view', 0, 0, tiled=True)]
    pallas_call x1 -> x4, Pallas kernels: 1.88 us -> 7.28 us  [the longest x1 3.92 us: body(): pl.pallas_call(band_kernel, in_specs=[vmem_spec()] * 2, out_specs=vmem_sp...]
    all_to_all x1 -> x0, waiting for transfers between devices: 3.22 us -> none  [body(): pieces = lax.all_to_all(partial, 'view', 0, 0, tiled=True)]
    unnamed x24 -> x28, local copies, waits for them, and re-layouts: 9.87 us -> 6.73 us
    another operation x2 -> x0, other arithmetic: 1.73 us -> none  [the longest x1 0.96 us: body(): jnp.stack([jnp.where(away <= half, planes[0], planes[2]), jnp.where(away...]
    ppermute x1, waiting for transfers between devices: 2.7 us -> 0.98 us  [body(): rim = lax.ppermute(facing, 'height', [(0, 1), (1, 0)])]
    all_to_all x1, waiting for transfers between devices: 5.94 us -> 4.34 us  [body(): arrived = lax.all_to_all(parts, 'view', 0, 0, tiled=True)]
  transfers between devices with their start and end apart: 5 -> 4, of which waited for: 5 -> 4; matrix products, arithmetic and copies ran while one was open for 4% -> 4% of each run, Pallas kernels for 3% -> 5%
where the time goes in v3:
time: 124 us; the launch traced here: 123 us
  blocking collectives  57 us (46%)
  Pallas kernels  21.5 us (17%)
  starting transfers between devices  20.4 us (16%)
  waiting for transfers between devices  11.7 us (9%)
  local copies, waits for them, and re-layouts  10.5 us (8%)
  other arithmetic  1.4 us (1%)
    all_to_all x2, blocking collectives, for_each(): lax.all_to_all(tiles, axes, 0, 0, axis_index_groups=groups, tiled=True)  27.5 us
    all_to_all x1, blocking collectives, body(): pieces = lax.all_to_all(partial, 'view', 0, 0, tiled=True)  17.4 us
    all_to_all x1, blocking collectives, body(): arrived = lax.all_to_all(payload, 'view', 0, 0, tiled=True)  12 us
    pallas_call x1, Pallas kernels, main_call(): pl.pallas_call(main_kernel, in_specs=[vmem_spec(), hbm_spec(), vmem_spec(...  8.68 us
    all_to_all x1, starting transfers between devices, for_each(): lax.all_to_all(tiles, axes, 0, 0, axis_index_groups=groups, tiled=True)  6.84 us
    unnamed x28, local copies, waits for them, and re-layouts  6.73 us
    all_to_all x1, starting transfers between devices, body(): arrived = lax.all_to_all(parts, 'view', 0, 0, tiled=True)  6.69 us
    ppermute x1, starting transfers between devices, body(): rim = lax.ppermute(facing, 'height', [(0, 1), (1, 0)])  5.62 us
  transfers between devices with their start and end apart: 4, of which 4 were waited for; matrix products, arithmetic and copies ran while one was open for 4% of the time, Pallas kernels for 5%

profile of v3, /device:TPU:1, one launch (start us, length us, event | category | flops | bytes accessed | tf_op | source)
XLA Modules:
  0.0 123.3 jit_solution(2355101321381467628)
XLA Ops:
  0.7 1.3 %multiply_add_fusion.targets_ref = s32[8,8]{1,0:T(8,128)} fusion(s32[8,8]{1,0:T(8,128)} %param.14, s32[8,8]{1,0:T(8,128)} %param.13), kind=kLoop, calls=%fused_computation.8 | loop fusion | flops 128 | bytes 768 | tf_op jit(solution)/shard_map/add | solution.py:358
  2.0 2.9 %shard_map.138 = bf16[8,128,128]{2,1,0:T(8,128)(2,1)} custom-call(s32[8,8]{1,0:T(8,128)} %multiply_add_fusion.targets_ref, bf16[128,128]{1,0:T(8,128)(2,1)} %bitcast.32, bf16[8,128,128]{2,1,0:T(8,128)(2,1)} %weights_ref.1), custom_call_target="tpu_custom_call" | custom-call | flops 100000000 | bytes 1000000 | tf_op jit(solution)/shard_map/pallas_call | solution.py:359
  4.9 17.4 %all_to_all.30.pieces_ref = bf16[8,128,128]{2,1,0:T(8,128)(2,1)} all-to-all(bf16[8,128,128]{2,1,0:T(8,128)(2,1)} %shard_map.138), channel_id=1, replica_groups=mesh['depth'=32,'height'=2,'view'=8] {'view'}, dimensions={0} | all-to-all | bytes 524288 | tf_op jit(solution)/shard_map/all_to_all | solution.py:377
  22.3 2.4 %shard_map.139.own_ref = bf16[2,128,128]{2,1,0:T(8,128)(2,1)} custom-call(bf16[8,128,128]{2,1,0:T(8,128)(2,1)} %all_to_all.30.pieces_ref, bf16[128,128]{1,0:T(8,128)(2,1)} %bitcast.33), custom_call_target="tpu_custom_call" | custom-call | tf_op jit(solution)/shard_map/pallas_call | solution.py:396
  24.7 1.3 %collective-permute-start = (bf16[2,128,128]{2,1,0:T(8,128)(2,1)}, bf16[2,128,128]{2,1,0:T(8,128)(2,1)S(1)}, u32[]{:S(2)}, u32[]{:S(2)}) collective-permute-start(bf16[2,128,128]{2,1,0:T(8,128)(2,1)} %shard_map.139.own_ref), channel_id=1, source_target_pairs={{4,20},{5,21},{6,22},{7,23},{16,0},{17,1},{18,2},{19,3},{20,36},{2... | collective-permute-start | bytes 196616 | tf_op jit(solution)/shard_map/ppermute | solution.py:413
  26.0 0.9 bitcast_dynamic-update-slice_fusion.5
  26.9 3.0 %collective-permute-done.far_ref = bf16[2,128,128]{2,1,0:T(8,128)(2,1)S(1)} collective-permute-done((bf16[2,128,128]{2,1,0:T(8,128)(2,1)}, bf16[2,128,128]{2,1,0:T(8,128)(2,1)S(1)}, u32[]{:S(2)}, u32[]{:S(2)}) %collective-permute-start) | collective-permute-done | bytes 65568 | tf_op jit(solution)/shard_map/ppermute | solution.py:413
  30.8 5.6 %collective-permute-start.1 = (bf16[4,64,128]{2,1,0:T(8,128)(2,1)S(1)}, bf16[4,64,128]{2,1,0:T(8,128)(2,1)S(1)}, u32[]{:S(2)}, u32[]{:S(2)}) collective-permute-start(bf16[4,64,128]{2,1,0:T(8,128)(2,1)S(1)} %shard_map.140), channel_id=1, source_target_pairs={{0,8},{8,0},{1,9},{9,1},{2,10},{10,2},{3,11},{11,3},{4,12},{12,4},... | collective-permute-start | bytes 196616 | tf_op jit(solution)/shard_map/ppermute | solution.py:420
  36.4 0.9 bitcast_dynamic-update-slice_fusion.4
  38.8 1.0 collective-permute-done.1.rim_ref
  40.6 1.0 shard_map.141
  41.6 6.7 %all-to-all-start.1 = ((bf16[8,2,192,128]{3,2,1,0:T(8,128)(2,1)}), bf16[8,2,192,128]{3,2,1,0:T(8,128)(2,1)S(1)}, u32[]{:S(2)}, u32[]{:S(2)}) async-start(bf16[8,2,192,128]{3,2,1,0:T(8,128)(2,1)} %shard_map.141), calls=%async_computation.1 | async-start | bytes 1572864 | tf_op jit(solution)/shard_map/all_to_all | solution.py:431
  50.4 3.9 %shard_map.142.band_hbm = bf16[6,192,1728]{2,1,0:T(8,128)(2,1)S(1)} custom-call(bf16[96,512]{1,0:T(8,128)(2,1)S(1)} %pad.4.taps_ref, s32[512,3]{1,0:T(8,128)S(1)} %copy-done.4), custom_call_target="tpu_custom_call" | custom-call | flops 1000000000 | bytes 7000000 | tf_op jit(solution)/shard_map/pallas_call | solution.py:383
  54.3 1.9 %copy-done = bf16[6,192,1728]{2,1,0:T(8,128)(2,1)} copy-done((bf16[6,192,1728]{2,1,0:T(8,128)(2,1)}, bf16[6,192,1728]{2,1,0:T(8,128)(2,1)S(1)}, u32[]{:S(2)}) %copy-start) | copy-done | bytes 3981336
  56.2 4.3 %all-to-all-done.1.arrived_ref = bf16[8,2,192,128]{3,2,1,0:T(8,128)(2,1)S(1)} async-done(((bf16[8,2,192,128]{3,2,1,0:T(8,128)(2,1)}), bf16[8,2,192,128]{3,2,1,0:T(8,128)(2,1)S(1)}, u32[]{:S(2)}, u32[]{:S(2)}) %all-to-all-start.1) | async-done | bytes 786464 | tf_op jit(solution)/shard_map/all_to_all | solution.py:431
  60.6 0.9 copy-done.6
  61.5 8.7 %shard_map.143 = (bf16[128,128]{1,0:T(8,128)(2,1)}, bf16[8,176,128]{2,1,0:T(8,128)(2,1)}) custom-call(bf16[8,2,192,128]{3,2,1,0:T(8,128)(2,1)} %copy-done.6, bf16[6,192,1728]{2,1,0:T(8,128)(2,1)} %copy-done, f32[2,192,1]{2,1,0:T(8,128)} %copy.29.bias_ref), custom_call_target="tpu_custom_call" | custom-call | flops 10000000000 | bytes 10000000 | tf_op jit(solution)/shard_map/pallas_call | solution.py:308
  70.2 12.0 %all_to_all.31.arrived_ref = bf16[8,176,128]{2,1,0:T(8,128)(2,1)S(1)} all-to-all(bf16[8,176,128]{2,1,0:T(8,128)(2,1)} %get-tuple-element.9), channel_id=1, replica_groups=mesh['depth'=32,'height'=2,'view'=8] {'view'}, dimensions={0} | all-to-all | bytes 720896 | tf_op jit(solution)/shard_map/all_to_all | solution.py:434
  82.2 12.8 %all_to_all.32 = f32[8,24,128]{2,1,0:T(8,128)S(1)} all-to-all(f32[8,24,128]{2,1,0:T(8,128)S(1)} %broadcast_in_dim.9), channel_id=1, replica_groups={{0,16,32,48,64,80,96,112},{128,144,160,176,192,208,224,240},{256,272,28..., dimensions={0} | all-to-all | bytes 196608 | tf_op jit(solution)/shard_map/all_to_all | solution.py:340
  95.0 14.8 %all_to_all.33 = f32[8,24,128]{2,1,0:T(8,128)S(1)} all-to-all(f32[8,24,128]{2,1,0:T(8,128)S(1)} %broadcast_in_dim.10), channel_id=1, replica_groups={{0,128,256,384,8,136,264,392},{16,144,272,400,24,152,280,408},{32,160,2..., dimensions={0} | all-to-all | bytes 196608 | tf_op jit(solution)/shard_map/all_to_all | solution.py:340
  110.4 6.8 %all-to-all-start.5 = ((f32[8,24,128]{2,1,0:T(8,128)}), f32[8,24,128]{2,1,0:T(8,128)S(1)}, u32[]{:S(2)}, u32[]{:S(2)}) async-start(f32[8,24,128]{2,1,0:T(8,128)} %broadcast_in_dim.11), calls=%async_computation.5 | async-start | bytes 196608 | tf_op jit(solution)/shard_map/all_to_all | solution.py:340
  117.3 1.7 %shard_map.144 = f32[128,128]{1,0:T(8,128)} custom-call(s32[8,8]{1,0:T(8,128)S(1)} %copy-done.5, bf16[8,176,128]{2,1,0:T(8,128)(2,1)S(1)} %all_to_all.31.arrived_ref, bf16[8,128,128]{2,1,0:T(8,128)(2,1)S(1)} %copy-done.1), custom_call_target="tpu_custom_call" | custom-call | flops 100000000 | bytes 1000000 | tf_op jit(solution)/shard_map/pallas_call | solution.py:447
  118.9 3.3 %all-to-all-done.5 = f32[8,24,128]{2,1,0:T(8,128)S(1)} async-done(((f32[8,24,128]{2,1,0:T(8,128)}), f32[8,24,128]{2,1,0:T(8,128)S(1)}, u32[]{:S(2)}, u32[]{:S(2)}) %all-to-all-start.5) | async-done | bytes 98336 | tf_op jit(solution)/shard_map/all_to_all | solution.py:340
  122.3 1.1 shard_map.145
  (42 shorter events, 5.9 us)
Async XLA Ops:
  0.6 47.7 %copy-start.7 = (bf16[16,16,3,3,3]{1,0,4,3,2:T(8,128)(2,1)S(1)}, bf16[16,16,3,3,3]{1,0,4,3,2:T(8,128)(2,1)}, u32[]{:S(2)}) copy-start(bf16[16,16,3,3,3]{1,0,4,3,2:T(8,128)(2,1)} %param.15) | copy-start | bytes 41476
  0.6 47.8 %copy-start.8 = (bf16[16,16,3,3,3]{1,0,4,3,2:T(8,128)(2,1)S(1)}, bf16[16,16,3,3,3]{1,0,4,3,2:T(8,128)(2,1)}, u32[]{:S(2)}) copy-start(bf16[16,16,3,3,3]{1,0,4,3,2:T(8,128)(2,1)} %param.16) | copy-start | bytes 41476
  0.7 47.9 %copy-start.9 = (bf16[16,16,3,3,3]{1,0,4,3,2:T(8,128)(2,1)S(1)}, bf16[16,16,3,3,3]{1,0,4,3,2:T(8,128)(2,1)}, u32[]{:S(2)}) copy-start(bf16[16,16,3,3,3]{1,0,4,3,2:T(8,128)(2,1)} %param.17) | copy-start | bytes 41476
  22.3 28.1 %copy-start.4 = (s32[512,3]{1,0:T(8,128)S(1)}, s32[512,3]{1,0:T(8,128)}, u32[]{:S(2)}) copy-start(s32[512,3]{1,0:T(8,128)} %constant.9.clone.base_ref) | copy-start | bytes 18436
  24.7 5.2 %collective-permute-start = (bf16[2,128,128]{2,1,0:T(8,128)(2,1)}, bf16[2,128,128]{2,1,0:T(8,128)(2,1)S(1)}, u32[]{:S(2)}, u32[]{:S(2)}) collective-permute-start(bf16[2,128,128]{2,1,0:T(8,128)(2,1)} %shard_map.139.own_ref), channel_id=1, source_target_pairs={{4,20},{5,21},{6,22},{7,23},{16,0},{17,1},{18,2},{19,3},{20,36},{2... | collective-permute-start | bytes 196616 | tf_op jit(solution)/shard_map/ppermute | solution.py:413
  29.9 0.8 copy-start.2
  30.8 9.0 %collective-permute-start.1 = (bf16[4,64,128]{2,1,0:T(8,128)(2,1)S(1)}, bf16[4,64,128]{2,1,0:T(8,128)(2,1)S(1)}, u32[]{:S(2)}, u32[]{:S(2)}) collective-permute-start(bf16[4,64,128]{2,1,0:T(8,128)(2,1)S(1)} %shard_map.140), channel_id=1, source_target_pairs={{0,8},{8,0},{1,9},{9,1},{2,10},{10,2},{3,11},{11,3},{4,12},{12,4},... | collective-permute-start | bytes 196616 | tf_op jit(solution)/shard_map/ppermute | solution.py:420
  39.8 0.8 copy-start.3
  41.6 19.0 %all-to-all-start.1 = ((bf16[8,2,192,128]{3,2,1,0:T(8,128)(2,1)}), bf16[8,2,192,128]{3,2,1,0:T(8,128)(2,1)S(1)}, u32[]{:S(2)}, u32[]{:S(2)}) async-start(bf16[8,2,192,128]{3,2,1,0:T(8,128)(2,1)} %shard_map.141), calls=%async_computation.1 | async-start | bytes 1572864 | tf_op jit(solution)/shard_map/all_to_all | solution.py:431
  54.3 1.9 %copy-start = (bf16[6,192,1728]{2,1,0:T(8,128)(2,1)}, bf16[6,192,1728]{2,1,0:T(8,128)(2,1)S(1)}, u32[]{:S(2)}) copy-start(bf16[6,192,1728]{2,1,0:T(8,128)(2,1)S(1)} %shard_map.142.band_hbm) | copy-start | bytes 11943940
  56.2 61.0 %copy-start.1 = (bf16[8,128,128]{2,1,0:T(8,128)(2,1)S(1)}, bf16[8,128,128]{2,1,0:T(8,128)(2,1)}, u32[]{:S(2)}) copy-start(bf16[8,128,128]{2,1,0:T(8,128)(2,1)} %weights_ref.1) | copy-start | bytes 786436
  56.2 61.0 %copy-start.5 = (s32[8,8]{1,0:T(8,128)S(1)}, s32[8,8]{1,0:T(8,128)}, u32[]{:S(2)}) copy-start(s32[8,8]{1,0:T(8,128)} %multiply_add_fusion.targets_ref) | copy-start | bytes 772
  60.6 0.9 copy-start.6
  110.4 11.8 %all-to-all-start.5 = ((f32[8,24,128]{2,1,0:T(8,128)}), f32[8,24,128]{2,1,0:T(8,128)S(1)}, u32[]{:S(2)}, u32[]{:S(2)}) async-start(f32[8,24,128]{2,1,0:T(8,128)} %broadcast_in_dim.11), calls=%async_computation.5 | async-start | bytes 196608 | tf_op jit(solution)/shard_map/all_to_all | solution.py:340

commit v4 on v3

--- a/solution.py
+++ b/solution.py
@@ -63,11 +63,9 @@
     return out
 
 
-def own_kernel(pieces_ref, grad_hbm, own_ref, sem):
-    fetch = pltpu.make_async_copy(grad_hbm, own_ref.at[1], sem)
-    fetch.start()
+def own_kernel(pieces_ref, grad_ref, own_ref):
     own_ref[0] = pieces_ref[...].astype(F32).sum(axis=0).astype(BF16)
-    fetch.wait()
+    own_ref[1] = grad_ref[...]
 
 
 def facing_kernel(own_ref, far_ref, facing_ref):
@@ -90,13 +88,13 @@
         parts_ref[v, 1] = planes[jnp.where(away == half, 2, jnp.where(away < half, 1, 3))]
 
 
-def lift_kernel(targets_ref, feats_hbm, weights_hbm, out_ref, feats, weights, total, sems):
+def lift_kernel(bricks_ref, rows_ref, feats_hbm, weights_hbm, out_ref, feats, weights, total, sems):
     fetch_feats = pltpu.make_async_copy(feats_hbm, feats, sems.at[0])
     fetch_weights = pltpu.make_async_copy(weights_hbm, weights, sems.at[1])
     fetch_feats.start()
     fetch_weights.start()
     total[...] = jnp.zeros_like(total)
-    tiles, slots = targets_ref.shape
+    tiles, slots = bricks_ref.shape
     fetch_feats.wait()
     fetch_weights.wait()
     for k in range(slots):
@@ -104,22 +102,30 @@
             feats[...], weights[k], (((1,), (1,)), ((), ())), preferred_element_type=F32
         )
         for t in range(tiles):
-            total[targets_ref[t, k]] += blocks[t * C : (t + 1) * C, :]
+            total[bricks_ref[t, k] * YB + rows_ref[t, k]] += blocks[t * C : (t + 1) * C, :]
     out_ref[...] = total[...].astype(BF16).reshape(out_ref.shape)
 
 
-def camera_kernel(targets_ref, arrived_ref, weights_ref, out_ref, chosen):
-    tiles, slots = targets_ref.shape
+def camera_kernel(bricks_ref, rows_ref, arrived_ref, weights_ref, out_ref, chosen):
+    tiles, slots = bricks_ref.shape
     for k in range(slots):
         for t in range(tiles):
-            target = targets_ref[t, k]
-            at = pl.multiple_of(lax.rem(target, YB) * C, C)
+            at = pl.multiple_of(rows_ref[t, k] * C, C)
             chosen[t * C : (t + 1) * C, k * X : (k + 1) * X] = arrived_ref[
-                lax.div(target, YB), pl.ds(at, C), :
+                bricks_ref[t, k], pl.ds(at, C), :
             ]
     out_ref[...] = jnp.dot(
         chosen[...], weights_ref[...].reshape(slots * X, X), preferred_element_type=F32
     )
+
+
+def first_sum_kernel(arrived_ref, out_ref):
+    sums = arrived_ref[:, HALF:, :].astype(F32).sum(axis=0)
+    out_ref[...] = jnp.broadcast_to((sums[:24] + sums[24:])[None], out_ref.shape)
+
+
+def next_sum_kernel(arrived_ref, out_ref):
+    out_ref[...] = jnp.broadcast_to(arrived_ref[...].sum(axis=0, keepdims=True), out_ref.shape)
 
 
 def spread_kernel(scale, sums_ref, weight_ref, bias_ref):
@@ -323,7 +329,7 @@
                 pltpu.VMEM((6, YC, 3 * K3), BF16),
                 pltpu.SemaphoreType.DMA((6,)),
             ],
-            vmem=58,
+            vmem=52,
             flops=10**10,
             moved=10**7,
         ),
@@ -334,10 +340,13 @@
     return jnp.transpose(jnp.flip(weight, (2, 3, 4)), (1, 0, 2, 3, 4))
 
 
-def for_each(block, axes, groups=None):
-    peers = len(groups[0]) if groups else lax.axis_size(axes)
-    tiles = jnp.broadcast_to(block[None], (peers, *block.shape))
-    return lax.all_to_all(tiles, axes, 0, 0, axis_index_groups=groups, tiled=True)
+def for_each_sum(kernel, arrived):
+    return pl.pallas_call(
+        kernel,
+        in_specs=[vmem_spec()],
+        out_specs=vmem_spec(),
+        **call(kernel, jax.ShapeDtypeStruct((VIEWS, 24, X), F32), vmem=16),
+    )(arrived)
 
 
 def body(
@@ -355,10 +364,9 @@
     depths, heights, views = (lax.axis_size(n) for n in ("depth", "height", "view"))
     tiles, slots = tile_bricks.shape
 
-    targets = tile_bricks * YB + tile_rows
     partial = pl.pallas_call(
         lift_kernel,
-        in_specs=[smem_spec(), hbm_spec(), hbm_spec()],
+        in_specs=[smem_spec(), smem_spec(), hbm_spec(), hbm_spec()],
         out_specs=vmem_spec(),
         **call(
             lift_kernel,
@@ -373,7 +381,7 @@
             flops=10**8,
             moved=10**6,
         ),
-    )(targets, camera_feats.reshape(tiles * C, X), footprint_slot_weights)
+    )(tile_bricks, tile_rows, camera_feats.reshape(tiles * C, X), footprint_slot_weights)
     pieces = lax.all_to_all(partial, "view", 0, 0, tiled=True)
 
     convs = [conv_first, conv_second, conv_third]
@@ -395,14 +403,9 @@
 
     own = pl.pallas_call(
         own_kernel,
-        in_specs=[vmem_spec(), hbm_spec()],
-        out_specs=vmem_spec(),
-        **call(
-            own_kernel,
-            jax.ShapeDtypeStruct((2, HALF, X), BF16),
-            [pltpu.SemaphoreType.DMA],
-            vmem=60,
-        ),
+        in_specs=[vmem_spec()] * 2,
+        out_specs=vmem_spec(),
+        **call(own_kernel, jax.ShapeDtypeStruct((2, HALF, X), BF16), vmem=16),
     )(pieces, out_grad.reshape(HALF, X))
     moves = []
     for d in range(depths):
@@ -433,20 +436,23 @@
     field, payload = main_call(arrived, bands, bias)
     arrived = lax.all_to_all(payload, "view", 0, 0, tiled=True)
 
-    sums = arrived[:, HALF:].astype(F32).sum(axis=0)
-    sums = sums[:24] + sums[24:]
     run = views
+    sums = for_each_sum(first_sum_kernel, arrived)
     rings = [list(range(i, i + run)) for i in range(0, depths, run)]
-    sums = for_each(sums, "depth", rings).sum(axis=0)
+    sums = lax.all_to_all(sums, "depth", 0, 0, axis_index_groups=rings, tiled=True)
+    sums = for_each_sum(next_sum_kernel, sums)
     rings = [
         [(i * run + j) * heights + h for h in range(heights) for i in range(depths // run)]
         for j in range(run)
     ]
-    sums = for_each(sums, ("depth", "height"), rings).sum(axis=0)
+    sums = lax.all_to_all(
+        sums, ("depth", "height"), 0, 0, axis_index_groups=rings, tiled=True
+    )
+    sums = for_each_sum(next_sum_kernel, sums)
 
     camera_grad = pl.pallas_call(
         camera_kernel,
-        in_specs=[smem_spec(), vmem_spec(), vmem_spec()],
+        in_specs=[smem_spec(), smem_spec(), vmem_spec(), vmem_spec()],
         out_specs=vmem_spec(),
         **call(
             camera_kernel,
@@ -455,9 +461,9 @@
             flops=10**8,
             moved=10**6,
         ),
-    )(targets, arrived, footprint_slot_weights)
-
-    sums = for_each(sums, "view").reshape(12 * C, X)
+    )(tile_bricks, tile_rows, arrived, footprint_slot_weights)
+
+    sums = lax.all_to_all(sums, "view", 0, 0, tiled=True).reshape(12 * C, X)
     scale = 1.0 / math.sqrt(YB * X * depths * heights * views)
     weight_grads, bias_gradient_pair = pl.pallas_call(
         functools.partial(spread_kernel, scale),

time: 124 us -> 116 us (0.935)
  local copies, waits for them, and re-layouts: 10.5 us -> 7.39 us
  Pallas kernels: 21.5 us -> 18.5 us
  other arithmetic: 1.4 us -> 0.01 us
    unnamed x28 -> x26, local copies, waits for them, and re-layouts: 6.73 us -> 4.99 us
    pallas_call x3 -> x6, Pallas kernels: 6.91 us -> 5.38 us  [the longest x1 3.06 us: body(): pl.pallas_call(lift_kernel, in_specs=[smem_spec(), smem_spec(), hbm_spec(...]
    pallas_call x1, Pallas kernels: 8.68 us -> 7.18 us  [main_call(): pl.pallas_call(main_kernel, in_specs=[vmem_spec(), hbm_spec(), vmem_spec(...]
    add x2 -> x0, other arithmetic: 1.35 us -> none  [the longest x1 1.34 us: body(): targets = tile_bricks * YB + tile_rows]
where the time goes in v4:
time: 116 us; the launch traced here: 115 us
  blocking collectives  55.8 us (48%)
  starting transfers between devices  21.2 us (18%)
  Pallas kernels  18.5 us (16%)
  waiting for transfers between devices  11.5 us (10%)
  local copies, waits for them, and re-layouts  7.39 us (6%)
    all_to_all x1, blocking collectives, body(): pieces = lax.all_to_all(partial, 'view', 0, 0, tiled=True)  16.7 us
    all_to_all x1, blocking collectives, body(): lax.all_to_all(sums, ('depth', 'height'), 0, 0, axis_index_groups=rings,...  14.8 us
    all_to_all x1, blocking collectives, body(): lax.all_to_all(sums, 'depth', 0, 0, axis_index_groups=rings, tiled=True)  13.3 us
    all_to_all x1, blocking collectives, body(): arrived = lax.all_to_all(payload, 'view', 0, 0, tiled=True)  11 us
    pallas_call x1, Pallas kernels, main_call(): pl.pallas_call(main_kernel, in_specs=[vmem_spec(), hbm_spec(), vmem_spec(...  7.18 us
    all_to_all x1, starting transfers between devices, body(): arrived = lax.all_to_all(parts, 'view', 0, 0, tiled=True)  6.85 us
    all_to_all x1, starting transfers between devices, body(): sums = lax.all_to_all(sums, 'view', 0, 0, tiled=True).reshape(12 * C, X)  6.84 us
    ppermute x1, starting transfers between devices, body(): rim = lax.ppermute(facing, 'height', [(0, 1), (1, 0)])  6.23 us
  transfers between devices with their start and end apart: 4, of which 4 were waited for; matrix products, arithmetic and copies ran while one was open for 4% of the time, Pallas kernels for 5%

profile of v4, /device:TPU:1, one launch (start us, length us, event | category | flops | bytes accessed | tf_op | source)
XLA Modules:
  0.0 115.3 jit_solution(6909114369362815421)
XLA Ops:
  0.7 3.1 %shard_map.138 = bf16[8,128,128]{2,1,0:T(8,128)(2,1)} custom-call(s32[8,8]{1,0:T(8,128)} %bricks_ref.3, s32[8,8]{1,0:T(8,128)} %rows_ref.3, bf16[128,128]{1,0:T(8,128)(2,1)} %bitcast.33, bf16[8,128,128]{2,1,0:T(8,128)(2,1)} %weights_ref.1), custom_call_target="tpu_custom_call" | custom-call | flops 100000000 | bytes 1000000 | tf_op jit(solution)/shard_map/pallas_call | solution.py:367
  3.7 16.7 %all_to_all.30.pieces_ref = bf16[8,128,128]{2,1,0:T(8,128)(2,1)S(1)} all-to-all(bf16[8,128,128]{2,1,0:T(8,128)(2,1)} %shard_map.138), channel_id=1, replica_groups=mesh['depth'=32,'height'=2,'view'=8] {'view'}, dimensions={0} | all-to-all | bytes 524288 | tf_op jit(solution)/shard_map/all_to_all | solution.py:385
  20.4 0.8 copy-done.3
  21.3 1.3 %collective-permute-start = (bf16[2,128,128]{2,1,0:T(8,128)(2,1)S(1)}, bf16[2,128,128]{2,1,0:T(8,128)(2,1)S(1)}, u32[]{:S(2)}, u32[]{:S(2)}) collective-permute-start(bf16[2,128,128]{2,1,0:T(8,128)(2,1)S(1)} %shard_map.139.own_ref), channel_id=1, source_target_pairs={{4,20},{5,21},{6,22},{7,23},{16,0},{17,1},{18,2},{19,3},{20,36},{2... | collective-permute-start | bytes 196616 | tf_op jit(solution)/shard_map/ppermute | solution.py:416
  22.6 0.9 bitcast_dynamic-update-slice_fusion.5
  23.5 2.8 %collective-permute-done.far_ref = bf16[2,128,128]{2,1,0:T(8,128)(2,1)S(1)} collective-permute-done((bf16[2,128,128]{2,1,0:T(8,128)(2,1)S(1)}, bf16[2,128,128]{2,1,0:T(8,128)(2,1)S(1)}, u32[]{:S(2)}, u32[]{:S(2)}) %collective-permute-start) | collective-permute-done | bytes 65568 | tf_op jit(solution)/shard_map/ppermute | solution.py:416
  26.3 6.2 %collective-permute-start.1 = (bf16[4,64,128]{2,1,0:T(8,128)(2,1)S(1)}, bf16[4,64,128]{2,1,0:T(8,128)(2,1)S(1)}, u32[]{:S(2)}, u32[]{:S(2)}) collective-permute-start(bf16[4,64,128]{2,1,0:T(8,128)(2,1)S(1)} %shard_map.140), channel_id=1, source_target_pairs={{0,8},{8,0},{1,9},{9,1},{2,10},{10,2},{3,11},{11,3},{4,12},{12,4},... | collective-permute-start | bytes 196616 | tf_op jit(solution)/shard_map/ppermute | solution.py:423
  32.5 0.9 bitcast_dynamic-update-slice_fusion.4
  33.5 0.7 tile.4
  34.2 0.7 tile.5
  35.2 1.0 shard_map.141
  36.2 6.9 %all-to-all-start.1 = ((bf16[8,2,192,128]{3,2,1,0:T(8,128)(2,1)}), bf16[8,2,192,128]{3,2,1,0:T(8,128)(2,1)S(1)}, u32[]{:S(2)}, u32[]{:S(2)}) async-start(bf16[8,2,192,128]{3,2,1,0:T(8,128)(2,1)} %shard_map.141), calls=%async_computation.1 | async-start | bytes 1572864 | tf_op jit(solution)/shard_map/all_to_all | solution.py:434
  44.5 3.9 %shard_map.142.band_hbm = bf16[6,192,1728]{2,1,0:T(8,128)(2,1)S(1)} custom-call(bf16[96,512]{1,0:T(8,128)(2,1)S(1)} %pad.4.taps_ref, s32[512,3]{1,0:T(8,128)S(1)} %copy-done.2), custom_call_target="tpu_custom_call" | custom-call | flops 1000000000 | bytes 7000000 | tf_op jit(solution)/shard_map/pallas_call | solution.py:391
  48.4 1.9 %copy-done = bf16[6,192,1728]{2,1,0:T(8,128)(2,1)} copy-done((bf16[6,192,1728]{2,1,0:T(8,128)(2,1)}, bf16[6,192,1728]{2,1,0:T(8,128)(2,1)S(1)}, u32[]{:S(2)}) %copy-start) | copy-done | bytes 3981336
  50.4 5.0 %all-to-all-done.1.arrived_ref = bf16[8,2,192,128]{3,2,1,0:T(8,128)(2,1)S(1)} async-done(((bf16[8,2,192,128]{3,2,1,0:T(8,128)(2,1)}), bf16[8,2,192,128]{3,2,1,0:T(8,128)(2,1)S(1)}, u32[]{:S(2)}, u32[]{:S(2)}) %all-to-all-start.1) | async-done | bytes 786464 | tf_op jit(solution)/shard_map/all_to_all | solution.py:434
  55.4 7.2 %shard_map.143 = (bf16[128,128]{1,0:T(8,128)(2,1)}, bf16[8,176,128]{2,1,0:T(8,128)(2,1)S(1)}) custom-call(bf16[8,2,192,128]{3,2,1,0:T(8,128)(2,1)S(1)} %all-to-all-done.1.arrived_ref, bf16[6,192,1728]{2,1,0:T(8,128)(2,1)} %copy-done, f32[2,192,1]{2,1,0:T(8,128)S(1)} %copy.23.bias_ref), custom_call_target="tpu_custom_call" | custom-call | flops 10000000000 | bytes 10000000 | tf_op jit(solution)/shard_map/pallas_call | solution.py:314
  62.6 11.0 %all_to_all.31.arrived_ref = bf16[8,176,128]{2,1,0:T(8,128)(2,1)S(1)} all-to-all(bf16[8,176,128]{2,1,0:T(8,128)(2,1)S(1)} %get-tuple-element.9), channel_id=1, replica_groups=mesh['depth'=32,'height'=2,'view'=8] {'view'}, dimensions={0} | all-to-all | bytes 720896 | tf_op jit(solution)/shard_map/all_to_all | solution.py:437
  73.6 13.3 %all_to_all.32.arrived_ref = f32[8,24,128]{2,1,0:T(8,128)S(1)} all-to-all(f32[8,24,128]{2,1,0:T(8,128)S(1)} %shard_map.145), channel_id=1, replica_groups={{0,16,32,48,64,80,96,112},{128,144,160,176,192,208,224,240},{256,272,28..., dimensions={0} | all-to-all | bytes 196608 | tf_op jit(solution)/shard_map/all_to_all | solution.py:442
  86.9 14.8 %all_to_all.33.arrived_ref = f32[8,24,128]{2,1,0:T(8,128)S(1)} all-to-all(f32[8,24,128]{2,1,0:T(8,128)S(1)} %shard_map.146), channel_id=1, replica_groups={{0,128,256,384,8,136,264,392},{16,144,272,400,24,152,280,408},{32,160,2..., dimensions={0} | all-to-all | bytes 196608 | tf_op jit(solution)/shard_map/all_to_all | solution.py:448
  101.7 0.7 shard_map.147
  102.4 6.8 %all-to-all-start.5 = ((f32[8,24,128]{2,1,0:T(8,128)}), f32[8,24,128]{2,1,0:T(8,128)S(1)}, u32[]{:S(2)}, u32[]{:S(2)}) async-start(f32[8,24,128]{2,1,0:T(8,128)} %shard_map.147), calls=%async_computation.5 | async-start | bytes 196608 | tf_op jit(solution)/shard_map/all_to_all | solution.py:466
  109.2 1.6 %shard_map.144 = f32[128,128]{1,0:T(8,128)} custom-call(s32[8,8]{1,0:T(8,128)S(1)} %copy-done.4, s32[8,8]{1,0:T(8,128)S(1)} %copy-done.5, bf16[8,176,128]{2,1,0:T(8,128)(2,1)S(1)} %all_to_all.31.arrived_ref, bf16[8,128,128]{2,1,0:T(8,128)(2,1)S(1)} %copy-done.1), custom_call_target="tpu_custom_call" | custom-call | flops 100000000 | bytes 1000000 | tf_op jit(solution)/shard_map/pallas_call | solution.py:453
  110.8 3.4 %all-to-all-done.5 = f32[8,24,128]{2,1,0:T(8,128)S(1)} async-done(((f32[8,24,128]{2,1,0:T(8,128)}), f32[8,24,128]{2,1,0:T(8,128)S(1)}, u32[]{:S(2)}, u32[]{:S(2)}) %all-to-all-start.5) | async-done | bytes 98336 | tf_op jit(solution)/shard_map/all_to_all | solution.py:466
  114.2 1.1 shard_map.148
  (35 shorter events, 1.9 us)
Async XLA Ops:
  0.6 42.4 %copy-start.6 = (bf16[16,16,3,3,3]{1,0,4,3,2:T(8,128)(2,1)S(1)}, bf16[16,16,3,3,3]{1,0,4,3,2:T(8,128)(2,1)}, u32[]{:S(2)}) copy-start(bf16[16,16,3,3,3]{1,0,4,3,2:T(8,128)(2,1)} %param.15) | copy-start | bytes 41476
  0.6 42.6 %copy-start.7 = (bf16[16,16,3,3,3]{1,0,4,3,2:T(8,128)(2,1)S(1)}, bf16[16,16,3,3,3]{1,0,4,3,2:T(8,128)(2,1)}, u32[]{:S(2)}) copy-start(bf16[16,16,3,3,3]{1,0,4,3,2:T(8,128)(2,1)} %param.16) | copy-start | bytes 41476
  0.7 42.7 %copy-start.8 = (bf16[16,16,3,3,3]{1,0,4,3,2:T(8,128)(2,1)S(1)}, bf16[16,16,3,3,3]{1,0,4,3,2:T(8,128)(2,1)}, u32[]{:S(2)}) copy-start(bf16[16,16,3,3,3]{1,0,4,3,2:T(8,128)(2,1)} %param.17) | copy-start | bytes 41476
  20.4 24.1 %copy-start.2 = (s32[512,3]{1,0:T(8,128)S(1)}, s32[512,3]{1,0:T(8,128)}, u32[]{:S(2)}) copy-start(s32[512,3]{1,0:T(8,128)} %constant.5.clone.base_ref) | copy-start | bytes 18436
  20.4 0.8 copy-start.3
  21.3 5.0 %collective-permute-start = (bf16[2,128,128]{2,1,0:T(8,128)(2,1)S(1)}, bf16[2,128,128]{2,1,0:T(8,128)(2,1)S(1)}, u32[]{:S(2)}, u32[]{:S(2)}) collective-permute-start(bf16[2,128,128]{2,1,0:T(8,128)(2,1)S(1)} %shard_map.139.own_ref), channel_id=1, source_target_pairs={{4,20},{5,21},{6,22},{7,23},{16,0},{17,1},{18,2},{19,3},{20,36},{2... | collective-permute-start | bytes 196616 | tf_op jit(solution)/shard_map/ppermute | solution.py:416
  26.3 8.9 %collective-permute-start.1 = (bf16[4,64,128]{2,1,0:T(8,128)(2,1)S(1)}, bf16[4,64,128]{2,1,0:T(8,128)(2,1)S(1)}, u32[]{:S(2)}, u32[]{:S(2)}) collective-permute-start(bf16[4,64,128]{2,1,0:T(8,128)(2,1)S(1)} %shard_map.140), channel_id=1, source_target_pairs={{0,8},{8,0},{1,9},{9,1},{2,10},{10,2},{3,11},{11,3},{4,12},{12,4},... | collective-permute-start | bytes 196616 | tf_op jit(solution)/shard_map/ppermute | solution.py:423
  36.2 19.2 %all-to-all-start.1 = ((bf16[8,2,192,128]{3,2,1,0:T(8,128)(2,1)}), bf16[8,2,192,128]{3,2,1,0:T(8,128)(2,1)S(1)}, u32[]{:S(2)}, u32[]{:S(2)}) async-start(bf16[8,2,192,128]{3,2,1,0:T(8,128)(2,1)} %shard_map.141), calls=%async_computation.1 | async-start | bytes 1572864 | tf_op jit(solution)/shard_map/all_to_all | solution.py:434
  48.4 1.9 %copy-start = (bf16[6,192,1728]{2,1,0:T(8,128)(2,1)}, bf16[6,192,1728]{2,1,0:T(8,128)(2,1)S(1)}, u32[]{:S(2)}) copy-start(bf16[6,192,1728]{2,1,0:T(8,128)(2,1)S(1)} %shard_map.142.band_hbm) | copy-start | bytes 11943940
  50.4 58.8 %copy-start.1 = (bf16[8,128,128]{2,1,0:T(8,128)(2,1)S(1)}, bf16[8,128,128]{2,1,0:T(8,128)(2,1)}, u32[]{:S(2)}) copy-start(bf16[8,128,128]{2,1,0:T(8,128)(2,1)} %weights_ref.1) | copy-start | bytes 786436
  50.4 58.8 %copy-start.4 = (s32[8,8]{1,0:T(8,128)S(1)}, s32[8,8]{1,0:T(8,128)}, u32[]{:S(2)}) copy-start(s32[8,8]{1,0:T(8,128)} %bricks_ref.3) | copy-start | bytes 772
  50.4 58.8 %copy-start.5 = (s32[8,8]{1,0:T(8,128)S(1)}, s32[8,8]{1,0:T(8,128)}, u32[]{:S(2)}) copy-start(s32[8,8]{1,0:T(8,128)} %rows_ref.3) | copy-start | bytes 772
  102.4 11.8 %all-to-all-start.5 = ((f32[8,24,128]{2,1,0:T(8,128)}), f32[8,24,128]{2,1,0:T(8,128)S(1)}, u32[]{:S(2)}, u32[]{:S(2)}) async-start(f32[8,24,128]{2,1,0:T(8,128)} %shard_map.147), calls=%async_computation.5 | async-start | bytes 196608 | tf_op jit(solution)/shard_map/all_to_all | solution.py:466

commit v5 on v4

--- a/solution.py
+++ b/solution.py
@@ -42,24 +42,16 @@
     return pl.BlockSpec(memory_space=pltpu.SMEM)
 
 
-def band_kernel(taps_ref, base_ref, band_ref):
-    lane = lax.broadcasted_iota(jnp.int32, (4 * X, 3 * K3), 1)
-    last = YC // C - 1
-    for y in range(last + 1):
-        kind = 1 if y == 0 else 2 if y == last else 0
-        hit = lane == base_ref[:, kind : kind + 1] + y * C
-        spread = jnp.where(hit, 1.0, 0.0).astype(BF16)
-        rows = jnp.dot(taps_ref[...], spread, preferred_element_type=F32).astype(BF16)
-        for n in range(6):
-            band_ref[n, y * C : (y + 1) * C, :] = rows[n * C : (n + 1) * C, :]
-
-
-def band_places():
+def block_kernel(taps_ref, place_ref, block_ref):
+    lane = lax.broadcasted_iota(jnp.int32, (4 * X, 14 * X), 1)
+    spread = jnp.where(lane == place_ref[...], 1.0, 0.0).astype(BF16)
+    block_ref[...] = jnp.dot(taps_ref[...], spread, preferred_element_type=F32).astype(BF16)
+
+
+def block_places():
     a, c, b, i = np.indices((3, 3, 3, C)).reshape(4, -1)
-    base = a * K3 + c * YC + (b - 1) * C + i
-    base = np.stack([base, np.where(b == 0, -(10**6), base), np.where(b == 2, -(10**6), base)], 1)
-    out = np.full((4 * X, 3), -(10**6), np.int32)
-    out[: base.shape[0]] = base
+    out = np.full((4 * X, 1), -1, np.int32)
+    out[: a.size, 0] = a * K3 + c * YC + b * C + i
     return out
 
 
@@ -121,11 +113,17 @@
 
 def first_sum_kernel(arrived_ref, out_ref):
     sums = arrived_ref[:, HALF:, :].astype(F32).sum(axis=0)
-    out_ref[...] = jnp.broadcast_to((sums[:24] + sums[24:])[None], out_ref.shape)
+    sums = sums[:24] + sums[24:]
+    lost = sums - sums.astype(BF16).astype(F32)
+    group = lax.broadcasted_iota(jnp.int32, sums.shape, 1) >> 4
+    spare = jnp.logical_and(group >= 5, lax.axis_index("view") >= VIEWS - 2)
+    sums = jnp.where(spare, pltpu.roll(lost, 2 * C, 1), sums).astype(BF16)
+    out_ref[...] = jnp.broadcast_to(sums[None], out_ref.shape)
 
 
 def next_sum_kernel(arrived_ref, out_ref):
-    out_ref[...] = jnp.broadcast_to(arrived_ref[...].sum(axis=0, keepdims=True), out_ref.shape)
+    sums = arrived_ref[...].astype(F32).sum(axis=0, keepdims=True)
+    out_ref[...] = jnp.broadcast_to(sums, out_ref.shape)
 
 
 def spread_kernel(scale, sums_ref, weight_ref, bias_ref):
@@ -136,8 +134,9 @@
             block = sums_ref[row : row + C, q % 8 * C : (q % 8 + 1) * C]
             weight_ref[((layer * 3 + a) * 3 + b) * 3 + c] = block * scale
     for layer in range(2):
-        lanes = slice((3 + layer) * C, (4 + layer) * C)
-        bias_ref[layer : layer + 1, :] = sums_ref[9 * C : 9 * C + 1, lanes] * scale
+        lanes, lost = (slice((n + layer) * C, (n + 1 + layer) * C) for n in (3, 5))
+        row = sums_ref[9 * C : 9 * C + 1, :]
+        bias_ref[layer : layer + 1, :] = (row[:, lanes] + row[:, lost]) * scale
 
 
 def silu_and_slope(v):
@@ -147,7 +146,7 @@
 
 def main_kernel(
     arrived_ref,
-    band_hbm,
+    block_hbm,
     bias_ref,
     field_ref,
     payload_ref,
@@ -161,11 +160,11 @@
     slope2,
     up2,
     band_ref,
-    sems,
+    block_ref,
+    sem,
 ):
-    fetches = [pltpu.make_async_copy(band_hbm.at[n], band_ref.at[n], sems.at[n]) for n in range(6)]
-    for n in (0, 3, 1, 4, 5, 2):
-        fetches[n].start()
+    fetch_blocks = pltpu.make_async_copy(block_hbm, block_ref, sem)
+    fetch_blocks.start()
     depth, height, view = (lax.axis_index(n) for n in ("depth", "height", "view"))
     lane = lax.broadcasted_iota(jnp.int32, (YC, X), 1)
     first_lane, last_lane = lane == 0, lane == X - 1
@@ -217,19 +216,35 @@
     for i in range(7):
         put(s_grad, i, fetch(i - 3, 1))
 
+    fetch_blocks.wait()
+    at = lax.broadcasted_iota(jnp.int32, (C, 14 * X), 1)
+    below, above = at < 0, at < 0
+    for w in range(9):
+        start = w * YC
+        below = jnp.logical_or(below, jnp.logical_and(at >= start, at < start + C))
+        above = jnp.logical_or(above, jnp.logical_and(at >= start + 2 * C, at < start + 3 * C))
+    for n in (0, 3, 1, 4, 5, 2):
+        block = block_ref[n * C : (n + 1) * C, :].astype(F32)
+        for y in range(YC // C):
+            rows = block
+            if y == 0:
+                rows = jnp.where(below, 0.0, block)
+            if y == YC // C - 1:
+                rows = jnp.where(above, 0.0, block)
+            if y != 1:
+                rows = pltpu.roll(rows, (y - 1) * C % (14 * X), 1)
+            band_ref[n, y * C : (y + 1) * C, :] = rows[:, : 3 * K3].astype(BF16)
+
     bias1, bias2 = bias_ref[0], bias_ref[1]
-    fetches[0].wait()
     for i, n in pairs(7):
         for j, pre in enumerate(conv(0, s_lift, i, n)):
             act, slope = silu_and_slope(pre + bias1)
             put(s_act1, i + j, masked(i + j - 3, act))
             if abs(i + j - 3) <= 1:
                 slope1[i + j - 2] = slope
-    fetches[3].wait()
     for i, n in pairs(5):
         for j, up in enumerate(conv(3, s_grad, i, n)):
             up2[i + j] = up
-    fetches[1].wait()
     for i, n in pairs(5):
         for j, pre in enumerate(conv(1, s_act1, i, n)):
             at = i + j
@@ -241,7 +256,6 @@
             if abs(at - 2) <= 1:
                 before = s_act1[YC : 2 * YC, (at + 1) * X : (at + 2) * X].astype(F32)
                 put(s_act2, at - 1, masked(at - 2, act + before))
-    fetches[4].wait()
     for i, n in pairs(3):
         for j, up in enumerate(conv(4, s_back2, i, n)):
             at = i + j
@@ -253,11 +267,9 @@
     def own_rows(plane):
         return jnp.where(low, plane[:HALF], plane[RIM:])
 
-    fetches[5].wait()
     lift_grad = conv_own(5, s_back1).astype(BF16)
     for v in range(VIEWS):
         payload_ref[v, :HALF, :] = lift_grad
-    fetches[2].wait()
     field_ref[...] = conv_own(2, s_act2).astype(BF16)
 
     wide = (HALF, K3)
@@ -310,7 +322,7 @@
         payload_ref[v, HALF:, :] = both.astype(BF16)
 
 
-def main_call(arrived, bands, bias):
+def main_call(arrived, blocks, bias):
     return pl.pallas_call(
         main_kernel,
         in_specs=[vmem_spec(), hbm_spec(), vmem_spec()],
@@ -327,25 +339,26 @@
                 pltpu.VMEM((YC, X), F32),
                 pltpu.VMEM((5, YC, X), F32),
                 pltpu.VMEM((6, YC, 3 * K3), BF16),
-                pltpu.SemaphoreType.DMA((6,)),
+                pltpu.VMEM((6 * C, 14 * X), BF16),
+                pltpu.SemaphoreType.DMA,
             ],
             vmem=52,
             flops=10**10,
             moved=10**7,
         ),
-    )(arrived, bands, bias)
+    )(arrived, blocks, bias)
 
 
 def flip_swap(weight):
     return jnp.transpose(jnp.flip(weight, (2, 3, 4)), (1, 0, 2, 3, 4))
 
 
-def for_each_sum(kernel, arrived):
+def for_each_sum(kernel, arrived, peers, dtype):
     return pl.pallas_call(
         kernel,
         in_specs=[vmem_spec()],
         out_specs=vmem_spec(),
-        **call(kernel, jax.ShapeDtypeStruct((VIEWS, 24, X), F32), vmem=16),
+        **call(kernel, jax.ShapeDtypeStruct((peers, 24, X), dtype), vmem=16),
     )(arrived)
 
 
@@ -388,17 +401,17 @@
     convs = jnp.stack(convs + [flip_swap(w) for w in reversed(convs)])
     taps = jnp.transpose(convs, (0, 1, 3, 5, 4, 2)).reshape(6 * C, 27 * C)
     taps = jnp.pad(taps, ((0, 0), (0, 4 * X - 27 * C)))
-    bands = pl.pallas_call(
-        band_kernel,
+    blocks = pl.pallas_call(
+        block_kernel,
         in_specs=[vmem_spec()] * 2,
         out_specs=vmem_spec(),
         **call(
-            band_kernel,
-            jax.ShapeDtypeStruct((6, YC, 3 * K3), BF16),
-            flops=10**9,
-            moved=7 * 10**6,
+            block_kernel,
+            jax.ShapeDtypeStruct((6 * C, 14 * X), BF16),
+            flops=10**8,
+            moved=10**6,
         ),
-    )(taps, band_places())
+    )(taps, block_places())
     bias = jnp.stack([jnp.tile(b, YC // C) for b in (bias_first, bias_second)])[:, :, None]
 
     own = pl.pallas_call(
@@ -433,22 +446,13 @@
     )(own, far, rim)
     arrived = lax.all_to_all(parts, "view", 0, 0, tiled=True)
 
-    field, payload = main_call(arrived, bands, bias)
+    field, payload = main_call(arrived, blocks, bias)
     arrived = lax.all_to_all(payload, "view", 0, 0, tiled=True)
 
-    run = views
-    sums = for_each_sum(first_sum_kernel, arrived)
-    rings = [list(range(i, i + run)) for i in range(0, depths, run)]
-    sums = lax.all_to_all(sums, "depth", 0, 0, axis_index_groups=rings, tiled=True)
-    sums = for_each_sum(next_sum_kernel, sums)
-    rings = [
-        [(i * run + j) * heights + h for h in range(heights) for i in range(depths // run)]
-        for j in range(run)
-    ]
-    sums = lax.all_to_all(
-        sums, ("depth", "height"), 0, 0, axis_index_groups=rings, tiled=True
-    )
-    sums = for_each_sum(next_sum_kernel, sums)
+    across = ("depth", "height")
+    sums = for_each_sum(first_sum_kernel, arrived, depths * heights, BF16)
+    sums = lax.all_to_all(sums, across, 0, 0, tiled=True)
+    sums = for_each_sum(next_sum_kernel, sums, views, F32)
 
     camera_grad = pl.pallas_call(
         camera_kernel,

time: 116 us -> 113 us (0.974)
  waiting for transfers between devices: 11.5 us -> 18.3 us
  Pallas kernels: 18.5 us -> 13.7 us
  local copies, waits for them, and re-layouts: 7.39 us -> 3.14 us
    all_to_all x1, waiting for transfers between devices: 5 us -> 9.72 us  [body(): arrived = lax.all_to_all(parts, 'view', 0, 0, tiled=True)]
    pallas_call x1, Pallas kernels: 3.92 us -> 0.54 us  [body(): pl.pallas_call(block_kernel, in_specs=[vmem_spec()] * 2, out_specs=vmem_s...]
    unnamed x26 -> x28, local copies, waits for them, and re-layouts: 4.99 us -> 2.05 us
    pallas_call x1, Pallas kernels: 7.18 us -> 5.69 us  [main_call(): pl.pallas_call(main_kernel, in_specs=[vmem_spec(), hbm_spec(), vmem_spec(...]
    another operation x2, local copies, waits for them, and re-layouts: 1.32 us -> 0.01 us  [body(): jnp.tile(b, YC // C)]
    ppermute x1, waiting for transfers between devices: 0.3 us -> 1.51 us  [body(): rim = lax.ppermute(facing, 'height', [(0, 1), (1, 0)])]
    all_to_all x2 -> x1, blocking collectives: 28.1 us -> 28.1 us  [body(): sums = lax.all_to_all(sums, across, 0, 0, tiled=True)]
  transfers between devices with their start and end apart: 4 -> 4, of which waited for: 4 -> 4; matrix products, arithmetic and copies ran while one was open for 4% -> 1% of each run, Pallas kernels for 5% -> 2%
where the time goes in v5:
time: 113 us
  blocking collectives  55.8 us (49%)
  starting transfers between devices  21 us (19%)
  waiting for transfers between devices  18.3 us (16%)
  Pallas kernels  13.7 us (12%)
  local copies, waits for them, and re-layouts  3.14 us (3%)
    all_to_all x1, blocking collectives, body(): sums = lax.all_to_all(sums, across, 0, 0, tiled=True)  28.1 us
    all_to_all x1, blocking collectives, body(): pieces = lax.all_to_all(partial, 'view', 0, 0, tiled=True)  16.7 us
    all_to_all x1, blocking collectives, body(): arrived = lax.all_to_all(payload, 'view', 0, 0, tiled=True)  11 us
    all_to_all x1, waiting for transfers between devices, body(): arrived = lax.all_to_all(parts, 'view', 0, 0, tiled=True)  9.72 us
    all_to_all x1, starting transfers between devices, body(): arrived = lax.all_to_all(parts, 'view', 0, 0, tiled=True)  6.86 us
    all_to_all x1, starting transfers between devices, body(): sums = lax.all_to_all(sums, 'view', 0, 0, tiled=True).reshape(12 * C, X)  6.65 us
    ppermute x1, starting transfers between devices, body(): rim = lax.ppermute(facing, 'height', [(0, 1), (1, 0)])  6.24 us
    pallas_call x1, Pallas kernels, main_call(): pl.pallas_call(main_kernel, in_specs=[vmem_spec(), hbm_spec(), vmem_spec(...  5.69 us
  transfers between devices with their start and end apart: 4, of which 4 were waited for; matrix products, arithmetic and copies ran while one was open for 1% of the time, Pallas kernels for 2%

profile of v5, /device:TPU:1, one launch (start us, length us, event | category | flops | bytes accessed | tf_op | source)
XLA Modules:
  0.0 112.8 jit_solution(9923611195665347762)
XLA Ops:
  0.6 2.9 %shard_map.138 = bf16[8,128,128]{2,1,0:T(8,128)(2,1)} custom-call(s32[8,8]{1,0:T(8,128)} %bricks_ref.3, s32[8,8]{1,0:T(8,128)} %rows_ref.3, bf16[128,128]{1,0:T(8,128)(2,1)} %bitcast.33, bf16[8,128,128]{2,1,0:T(8,128)(2,1)} %weights_ref.1), custom_call_target="tpu_custom_call" | custom-call | flops 100000000 | bytes 1000000 | tf_op jit(solution)/shard_map/pallas_call | solution.py:380
  3.6 16.7 %all_to_all.25.pieces_ref = bf16[8,128,128]{2,1,0:T(8,128)(2,1)S(1)} all-to-all(bf16[8,128,128]{2,1,0:T(8,128)(2,1)} %shard_map.138), channel_id=1, replica_groups=mesh['depth'=32,'height'=2,'view'=8] {'view'}, dimensions={0} | all-to-all | bytes 524288 | tf_op jit(solution)/shard_map/all_to_all | solution.py:398
  20.3 1.3 %collective-permute-start = (bf16[2,128,128]{2,1,0:T(8,128)(2,1)S(1)}, bf16[2,128,128]{2,1,0:T(8,128)(2,1)S(1)}, u32[]{:S(2)}, u32[]{:S(2)}) collective-permute-start(bf16[2,128,128]{2,1,0:T(8,128)(2,1)S(1)} %shard_map.139.own_ref), channel_id=1, source_target_pairs={{4,20},{5,21},{6,22},{7,23},{16,0},{17,1},{18,2},{19,3},{20,36},{2... | collective-permute-start | bytes 196616 | tf_op jit(solution)/shard_map/ppermute | solution.py:429
  21.7 3.7 %collective-permute-done.far_ref = bf16[2,128,128]{2,1,0:T(8,128)(2,1)S(1)} collective-permute-done((bf16[2,128,128]{2,1,0:T(8,128)(2,1)S(1)}, bf16[2,128,128]{2,1,0:T(8,128)(2,1)S(1)}, u32[]{:S(2)}, u32[]{:S(2)}) %collective-permute-start) | collective-permute-done | bytes 65568 | tf_op jit(solution)/shard_map/ppermute | solution.py:429
  25.3 6.2 %collective-permute-start.1 = (bf16[4,64,128]{2,1,0:T(8,128)(2,1)S(1)}, bf16[4,64,128]{2,1,0:T(8,128)(2,1)S(1)}, u32[]{:S(2)}, u32[]{:S(2)}) collective-permute-start(bf16[4,64,128]{2,1,0:T(8,128)(2,1)S(1)} %shard_map.140), channel_id=1, source_target_pairs={{0,8},{8,0},{1,9},{9,1},{2,10},{10,2},{3,11},{11,3},{4,12},{12,4},... | collective-permute-start | bytes 196616 | tf_op jit(solution)/shard_map/ppermute | solution.py:436
  31.9 0.8 copy-done.7
  32.8 1.5 %collective-permute-done.1.rim_ref = bf16[4,64,128]{2,1,0:T(8,128)(2,1)S(1)} collective-permute-done((bf16[4,64,128]{2,1,0:T(8,128)(2,1)S(1)}, bf16[4,64,128]{2,1,0:T(8,128)(2,1)S(1)}, u32[]{:S(2)}, u32[]{:S(2)}) %collective-permute-start.1) | collective-permute-done | bytes 65568 | tf_op jit(solution)/shard_map/ppermute | solution.py:436
  34.3 1.0 shard_map.141
  35.3 6.9 %all-to-all-start.1 = ((bf16[8,2,192,128]{3,2,1,0:T(8,128)(2,1)}), bf16[8,2,192,128]{3,2,1,0:T(8,128)(2,1)S(1)}, u32[]{:S(2)}, u32[]{:S(2)}) async-start(bf16[8,2,192,128]{3,2,1,0:T(8,128)(2,1)} %shard_map.141), calls=%async_computation.1 | async-start | bytes 1572864 | tf_op jit(solution)/shard_map/all_to_all | solution.py:447
  42.2 0.3 copy.24
  42.6 0.4 reshape.38
  43.0 0.2 copy-done.8
  43.4 0.1 copy.23.bias_ref
  43.6 0.6 copy-done.1
  44.2 0.5 shard_map.142.block_hbm
  44.7 9.7 %all-to-all-done.1.arrived_ref = bf16[8,2,192,128]{3,2,1,0:T(8,128)(2,1)S(1)} async-done(((bf16[8,2,192,128]{3,2,1,0:T(8,128)(2,1)}), bf16[8,2,192,128]{3,2,1,0:T(8,128)(2,1)S(1)}, u32[]{:S(2)}, u32[]{:S(2)}) %all-to-all-start.1) | async-done | bytes 786464 | tf_op jit(solution)/shard_map/all_to_all | solution.py:447
  54.4 5.7 %shard_map.143 = (bf16[128,128]{1,0:T(8,128)(2,1)}, bf16[8,176,128]{2,1,0:T(8,128)(2,1)S(1)}) custom-call(bf16[8,2,192,128]{3,2,1,0:T(8,128)(2,1)S(1)} %all-to-all-done.1.arrived_ref, bf16[96,1792]{1,0:T(8,128)(2,1)S(1)} %shard_map.142.block_hbm, f32[2,192,1]{2,1,0:T(8,128)S(1)} %copy.23.bias_ref), custom_call_target="tpu_custom_call" | custom-call | flops 10000000000 | bytes 10000000 | tf_op jit(solution)/shard_map/pallas_call | solution.py:326
  60.1 11.0 %all_to_all.26.arrived_ref = bf16[8,176,128]{2,1,0:T(8,128)(2,1)S(1)} all-to-all(bf16[8,176,128]{2,1,0:T(8,128)(2,1)S(1)} %get-tuple-element.9), channel_id=1, replica_groups=mesh['depth'=32,'height'=2,'view'=8] {'view'}, dimensions={0} | all-to-all | bytes 720896 | tf_op jit(solution)/shard_map/all_to_all | solution.py:450
  71.3 28.1 %all_to_all.27.arrived_ref = bf16[64,24,128]{2,1,0:T(8,128)(2,1)S(1)} all-to-all(bf16[64,24,128]{2,1,0:T(8,128)(2,1)S(1)} %shard_map.145), channel_id=1, replica_groups=mesh['depth'=32,'height'=2,'view'=8] {'depth','height'}, dimensions={0} | all-to-all | bytes 786432 | tf_op jit(solution)/shard_map/all_to_all | solution.py:454
  99.3 0.7 shard_map.146
  100.1 6.6 %all-to-all-start.4 = ((f32[8,24,128]{2,1,0:T(8,128)}), f32[8,24,128]{2,1,0:T(8,128)S(1)}, u32[]{:S(2)}, u32[]{:S(2)}) async-start(f32[8,24,128]{2,1,0:T(8,128)} %shard_map.146), calls=%async_computation.4 | async-start | bytes 196608 | tf_op jit(solution)/shard_map/all_to_all | solution.py:470
  106.7 1.6 %shard_map.144 = f32[128,128]{1,0:T(8,128)} custom-call(s32[8,8]{1,0:T(8,128)S(1)} %copy-done.3, s32[8,8]{1,0:T(8,128)S(1)} %copy-done.4, bf16[8,176,128]{2,1,0:T(8,128)(2,1)S(1)} %all_to_all.26.arrived_ref, bf16[8,128,128]{2,1,0:T(8,128)(2,1)S(1)} %copy-done), custom_call_target="tpu_custom_call" | custom-call | flops 100000000 | bytes 1000000 | tf_op jit(solution)/shard_map/pallas_call | solution.py:457
  108.3 3.4 %all-to-all-done.4 = f32[8,24,128]{2,1,0:T(8,128)S(1)} async-done(((f32[8,24,128]{2,1,0:T(8,128)}), f32[8,24,128]{2,1,0:T(8,128)S(1)}, u32[]{:S(2)}, u32[]{:S(2)}) %all-to-all-start.4) | async-done | bytes 98336 | tf_op jit(solution)/shard_map/all_to_all | solution.py:470
  111.7 1.1 shard_map.147
  (35 shorter events, 0.8 us)
Async XLA Ops:
  3.6 16.7 %copy-start.2 = (bf16[1,8,16,128]{3,2,1,0:T(8,128)(2,1)S(1)}, bf16[1,8,16,128]{3,2,1,0:T(8,128)(2,1)}, u32[]{:S(2)}) copy-start(bf16[1,8,16,128]{3,2,1,0:T(8,128)(2,1)} %param.20) | copy-start | bytes 98308
  20.3 1.3 %copy-start.6 = (bf16[16,16,3,3,3]{1,0,4,3,2:T(8,128)(2,1)S(1)}, bf16[16,16,3,3,3]{1,0,4,3,2:T(8,128)(2,1)}, u32[]{:S(2)}) copy-start(bf16[16,16,3,3,3]{1,0,4,3,2:T(8,128)(2,1)} %param.15) | copy-start | bytes 41476
  20.3 5.0 %collective-permute-start = (bf16[2,128,128]{2,1,0:T(8,128)(2,1)S(1)}, bf16[2,128,128]{2,1,0:T(8,128)(2,1)S(1)}, u32[]{:S(2)}, u32[]{:S(2)}) collective-permute-start(bf16[2,128,128]{2,1,0:T(8,128)(2,1)S(1)} %shard_map.139.own_ref), channel_id=1, source_target_pairs={{4,20},{5,21},{6,22},{7,23},{16,0},{17,1},{18,2},{19,3},{20,36},{2... | collective-permute-start | bytes 196616 | tf_op jit(solution)/shard_map/ppermute | solution.py:429
  21.7 9.9 %copy-start.5 = (bf16[16,16,3,3,3]{1,0,4,3,2:T(8,128)(2,1)S(1)}, bf16[16,16,3,3,3]{1,0,4,3,2:T(8,128)(2,1)}, u32[]{:S(2)}) copy-start(bf16[16,16,3,3,3]{1,0,4,3,2:T(8,128)(2,1)} %param.16) | copy-start | bytes 41476
  25.3 8.9 %collective-permute-start.1 = (bf16[4,64,128]{2,1,0:T(8,128)(2,1)S(1)}, bf16[4,64,128]{2,1,0:T(8,128)(2,1)S(1)}, u32[]{:S(2)}, u32[]{:S(2)}) collective-permute-start(bf16[4,64,128]{2,1,0:T(8,128)(2,1)S(1)} %shard_map.140), channel_id=1, source_target_pairs={{0,8},{8,0},{1,9},{9,1},{2,10},{10,2},{3,11},{11,3},{4,12},{12,4},... | collective-permute-start | bytes 196616 | tf_op jit(solution)/shard_map/ppermute | solution.py:436
  31.7 0.9 copy-start.7
  35.3 19.2 %all-to-all-start.1 = ((bf16[8,2,192,128]{3,2,1,0:T(8,128)(2,1)}), bf16[8,2,192,128]{3,2,1,0:T(8,128)(2,1)S(1)}, u32[]{:S(2)}, u32[]{:S(2)}) async-start(bf16[8,2,192,128]{3,2,1,0:T(8,128)(2,1)} %shard_map.141), calls=%async_computation.1 | async-start | bytes 1572864 | tf_op jit(solution)/shard_map/all_to_all | solution.py:447
  42.6 0.7 copy-start.8
  42.6 0.7 copy-start.9
  43.2 0.9 copy-start.1
  99.3 7.4 %copy-start = (bf16[8,128,128]{2,1,0:T(8,128)(2,1)S(1)}, bf16[8,128,128]{2,1,0:T(8,128)(2,1)}, u32[]{:S(2)}) copy-start(bf16[8,128,128]{2,1,0:T(8,128)(2,1)} %weights_ref.1) | copy-start | bytes 786436
  100.1 6.7 %copy-start.3 = (s32[8,8]{1,0:T(8,128)S(1)}, s32[8,8]{1,0:T(8,128)}, u32[]{:S(2)}) copy-start(s32[8,8]{1,0:T(8,128)} %bricks_ref.3) | copy-start | bytes 772
  100.1 6.7 %copy-start.4 = (s32[8,8]{1,0:T(8,128)S(1)}, s32[8,8]{1,0:T(8,128)}, u32[]{:S(2)}) copy-start(s32[8,8]{1,0:T(8,128)} %rows_ref.3) | copy-start | bytes 772
  100.1 11.6 %all-to-all-start.4 = ((f32[8,24,128]{2,1,0:T(8,128)}), f32[8,24,128]{2,1,0:T(8,128)S(1)}, u32[]{:S(2)}, u32[]{:S(2)}) async-start(f32[8,24,128]{2,1,0:T(8,128)} %shard_map.146), calls=%async_computation.4 | async-start | bytes 196608 | tf_op jit(solution)/shard_map/all_to_all | solution.py:470

commit v6 on v5

--- a/solution.py
+++ b/solution.py
@@ -104,7 +104,7 @@
         for t in range(tiles):
             at = pl.multiple_of(rows_ref[t, k] * C, C)
             chosen[t * C : (t + 1) * C, k * X : (k + 1) * X] = arrived_ref[
-                bricks_ref[t, k], pl.ds(at, C), :
+                jnp.bitwise_xor(bricks_ref[t, k], lax.axis_index("view")), pl.ds(at, C), :
             ]
     out_ref[...] = jnp.dot(
         chosen[...], weights_ref[...].reshape(slots * X, X), preferred_element_type=F32
@@ -112,7 +112,7 @@
 
 
 def first_sum_kernel(arrived_ref, out_ref):
-    sums = arrived_ref[:, HALF:, :].astype(F32).sum(axis=0)
+    sums = arrived_ref[...].astype(F32).sum(axis=0)
     sums = sums[:24] + sums[24:]
     lost = sums - sums.astype(BF16).astype(F32)
     group = lax.broadcasted_iota(jnp.int32, sums.shape, 1) >> 4
@@ -149,7 +149,8 @@
     block_hbm,
     bias_ref,
     field_ref,
-    payload_ref,
+    lift_ref,
+    sums_ref,
     s_lift,
     s_grad,
     s_act1,
@@ -268,8 +269,7 @@
         return jnp.where(low, plane[:HALF], plane[RIM:])
 
     lift_grad = conv_own(5, s_back1).astype(BF16)
-    for v in range(VIEWS):
-        payload_ref[v, :HALF, :] = lift_grad
+    lift_ref[0] = lift_grad
     field_ref[...] = conv_own(2, s_act2).astype(BF16)
 
     wide = (HALF, K3)
@@ -319,19 +319,20 @@
         rows = packed[v // 2][start : start + 24]
         high = rows.astype(BF16).astype(F32)
         both = jnp.concatenate([high, rows - high], axis=0)
-        payload_ref[v, HALF:, :] = both.astype(BF16)
+        sums_ref[v] = both.astype(BF16)
 
 
 def main_call(arrived, blocks, bias):
     return pl.pallas_call(
         main_kernel,
         in_specs=[vmem_spec(), hbm_spec(), vmem_spec()],
-        out_specs=[vmem_spec()] * 2,
+        out_specs=[vmem_spec()] * 3,
         **call(
             main_kernel,
             (
                 jax.ShapeDtypeStruct((HALF, X), BF16),
-                jax.ShapeDtypeStruct((VIEWS, HALF + 48, X), BF16),
+                jax.ShapeDtypeStruct((1, HALF, X), BF16),
+                jax.ShapeDtypeStruct((VIEWS, 48, X), BF16),
             ),
             [pltpu.VMEM((K3, n * X), BF16) for n in (9, 7, 7, 3, 5, 3)]
             + [
@@ -446,11 +447,15 @@
     )(own, far, rim)
     arrived = lax.all_to_all(parts, "view", 0, 0, tiled=True)
 
-    field, payload = main_call(arrived, blocks, bias)
-    arrived = lax.all_to_all(payload, "view", 0, 0, tiled=True)
+    field, lift_grad, sums = main_call(arrived, blocks, bias)
+    sums = lax.all_to_all(sums, "view", 0, 0, tiled=True)
 
     across = ("depth", "height")
-    sums = for_each_sum(first_sum_kernel, arrived, depths * heights, BF16)
+    sums = for_each_sum(first_sum_kernel, sums, depths * heights, BF16)
+    sums, lift_grad = lax.optimization_barrier((sums, lift_grad))
+    for step in (1, 2, 4):
+        pairs = [(v, v ^ step) for v in range(views)]
+        lift_grad = jnp.concatenate([lift_grad, lax.ppermute(lift_grad, "view", pairs)])
     sums = lax.all_to_all(sums, across, 0, 0, tiled=True)
     sums = for_each_sum(next_sum_kernel, sums, views, F32)
 
@@ -465,7 +470,7 @@
             flops=10**8,
             moved=10**6,
         ),
-    )(tile_bricks, tile_rows, arrived, footprint_slot_weights)
+    )(tile_bricks, tile_rows, lift_grad, footprint_slot_weights)
 
     sums = lax.all_to_all(sums, "view", 0, 0, tiled=True).reshape(12 * C, X)
     scale = 1.0 / math.sqrt(YB * X * depths * heights * views)

time: 113 us -> 112 us (level)
  blocking collectives: 55.8 us -> 24.9 us
  starting transfers between devices: 21 us -> 41.3 us
  waiting for transfers between devices: 18.3 us -> 25.1 us
    all_to_all x2 -> x1, blocking collectives: 39.1 us -> 8.23 us  [body(): sums = lax.all_to_all(sums, 'view', 0, 0, tiled=True)]
    all_to_all x0 -> x1, starting transfers between devices: none -> 12.7 us  [body(): sums = lax.all_to_all(sums, across, 0, 0, tiled=True)]
    ppermute x0 -> x3, starting transfers between devices: none -> 7.74 us  [body(): lax.ppermute(lift_grad, 'view', pairs)]
    ppermute x0 -> x3, waiting for transfers between devices: none -> 3.94 us  [body(): lax.ppermute(lift_grad, 'view', pairs)]
    all_to_all x0 -> x1, waiting for transfers between devices: none -> 3.87 us  [body(): sums = lax.all_to_all(sums, across, 0, 0, tiled=True)]
  transfers between devices with their start and end apart: 4 -> 8, of which waited for: 4 -> 7; matrix products, arithmetic and copies ran while one was open for 1% -> 1% of each run, Pallas kernels for 2% -> 3%
where the time goes in v6:
time: 112 us; the launch traced here: 111 us
  starting transfers between devices  41.3 us (37%)
  waiting for transfers between devices  25.1 us (22%)
  blocking collectives  24.9 us (22%)
  Pallas kernels  14.4 us (13%)
  local copies, waits for them, and re-layouts  4.03 us (4%)
    all_to_all x1, blocking collectives, body(): pieces = lax.all_to_all(partial, 'view', 0, 0, tiled=True)  16.7 us
    all_to_all x1, starting transfers between devices, body(): sums = lax.all_to_all(sums, across, 0, 0, tiled=True)  12.7 us
    all_to_all x1, waiting for transfers between devices, body(): arrived = lax.all_to_all(parts, 'view', 0, 0, tiled=True)  9.72 us
    all_to_all x1, blocking collectives, body(): sums = lax.all_to_all(sums, 'view', 0, 0, tiled=True)  8.23 us
    ppermute x3, starting transfers between devices, body(): lax.ppermute(lift_grad, 'view', pairs)  7.74 us
    all_to_all x1, starting transfers between devices, body(): arrived = lax.all_to_all(parts, 'view', 0, 0, tiled=True)  6.85 us
    all_to_all x1, starting transfers between devices, body(): sums = lax.all_to_all(sums, 'view', 0, 0, tiled=True).reshape(12 * C, X)  6.52 us
    ppermute x1, starting transfers between devices, body(): rim = lax.ppermute(facing, 'height', [(0, 1), (1, 0)])  6.23 us
  transfers between devices with their start and end apart: 8, of which 7 were waited for; matrix products, arithmetic and copies ran while one was open for 1% of the time, Pallas kernels for 3%

profile of v6, /device:TPU:1, one launch (start us, length us, event | category | flops | bytes accessed | tf_op | source)
XLA Modules:
  0.0 110.8 jit_solution(12303097065134559013)
XLA Ops:
  0.6 2.9 %shard_map.138 = bf16[8,128,128]{2,1,0:T(8,128)(2,1)} custom-call(s32[8,8]{1,0:T(8,128)} %bricks_ref.3, s32[8,8]{1,0:T(8,128)} %rows_ref.3, bf16[128,128]{1,0:T(8,128)(2,1)} %bitcast.33, bf16[8,128,128]{2,1,0:T(8,128)(2,1)} %weights_ref.1), custom_call_target="tpu_custom_call" | custom-call | flops 100000000 | bytes 1000000 | tf_op jit(solution)/shard_map/pallas_call | solution.py:381
  3.6 16.7 %all_to_all.25.pieces_ref = bf16[8,128,128]{2,1,0:T(8,128)(2,1)S(1)} all-to-all(bf16[8,128,128]{2,1,0:T(8,128)(2,1)} %shard_map.138), channel_id=1, replica_groups=mesh['depth'=32,'height'=2,'view'=8] {'view'}, dimensions={0} | all-to-all | bytes 524288 | tf_op jit(solution)/shard_map/all_to_all | solution.py:399
  20.3 1.3 %collective-permute-start = (bf16[2,128,128]{2,1,0:T(8,128)(2,1)S(1)}, bf16[2,128,128]{2,1,0:T(8,128)(2,1)S(1)}, u32[]{:S(2)}, u32[]{:S(2)}) collective-permute-start(bf16[2,128,128]{2,1,0:T(8,128)(2,1)S(1)} %shard_map.139.own_ref), channel_id=1, source_target_pairs={{4,20},{5,21},{6,22},{7,23},{16,0},{17,1},{18,2},{19,3},{20,36},{2... | collective-permute-start | bytes 196616 | tf_op jit(solution)/shard_map/ppermute | solution.py:430
  21.7 3.7 %collective-permute-done.far_ref = bf16[2,128,128]{2,1,0:T(8,128)(2,1)S(1)} collective-permute-done((bf16[2,128,128]{2,1,0:T(8,128)(2,1)S(1)}, bf16[2,128,128]{2,1,0:T(8,128)(2,1)S(1)}, u32[]{:S(2)}, u32[]{:S(2)}) %collective-permute-start) | collective-permute-done | bytes 65568 | tf_op jit(solution)/shard_map/ppermute | solution.py:430
  25.3 6.2 %collective-permute-start.1 = (bf16[4,64,128]{2,1,0:T(8,128)(2,1)S(1)}, bf16[4,64,128]{2,1,0:T(8,128)(2,1)S(1)}, u32[]{:S(2)}, u32[]{:S(2)}) collective-permute-start(bf16[4,64,128]{2,1,0:T(8,128)(2,1)S(1)} %shard_map.140), channel_id=1, source_target_pairs={{0,8},{8,0},{1,9},{9,1},{2,10},{10,2},{3,11},{11,3},{4,12},{12,4},... | collective-permute-start | bytes 196616 | tf_op jit(solution)/shard_map/ppermute | solution.py:437
  32.8 1.5 %collective-permute-done.1.rim_ref = bf16[4,64,128]{2,1,0:T(8,128)(2,1)S(1)} collective-permute-done((bf16[4,64,128]{2,1,0:T(8,128)(2,1)S(1)}, bf16[4,64,128]{2,1,0:T(8,128)(2,1)S(1)}, u32[]{:S(2)}, u32[]{:S(2)}) %collective-permute-start.1) | collective-permute-done | bytes 65568 | tf_op jit(solution)/shard_map/ppermute | solution.py:437
  34.3 1.0 shard_map.141
  35.3 6.9 %all-to-all-start.1 = ((bf16[8,2,192,128]{3,2,1,0:T(8,128)(2,1)}), bf16[8,2,192,128]{3,2,1,0:T(8,128)(2,1)S(1)}, u32[]{:S(2)}, u32[]{:S(2)}) async-start(bf16[8,2,192,128]{3,2,1,0:T(8,128)(2,1)} %shard_map.141), calls=%async_computation.1 | async-start | bytes 1572864 | tf_op jit(solution)/shard_map/all_to_all | solution.py:448
  44.7 9.7 %all-to-all-done.1.arrived_ref = bf16[8,2,192,128]{3,2,1,0:T(8,128)(2,1)S(1)} async-done(((bf16[8,2,192,128]{3,2,1,0:T(8,128)(2,1)}), bf16[8,2,192,128]{3,2,1,0:T(8,128)(2,1)S(1)}, u32[]{:S(2)}, u32[]{:S(2)}) %all-to-all-start.1) | async-done | bytes 786464 | tf_op jit(solution)/shard_map/all_to_all | solution.py:448
  54.4 5.7 %shard_map.143 = (bf16[128,128]{1,0:T(8,128)(2,1)}, bf16[1,128,128]{2,1,0:T(8,128)(2,1)S(1)}, bf16[8,48,128]{2,1,0:T(8,128)(2,1)S(1)}) custom-call(bf16[8,2,192,128]{3,2,1,0:T(8,128)(2,1)S(1)} %all-to-all-done.1.arrived_ref, bf16[96,1792]{1,0:T(8,128)(2,1)S(1)} %shard_map.142.block_hbm, f32[2,192,1]{2,1,0:T(8,128)S(1)} %copy.23.bias_ref), custom_call_target="tpu_custom_call" | custom-call | flops 10000000000 | bytes 10000000 | tf_op jit(solution)/shard_map/pallas_call | solution.py:326
  60.1 8.2 %all_to_all.26.arrived_ref = bf16[8,48,128]{2,1,0:T(8,128)(2,1)S(1)} all-to-all(bf16[8,48,128]{2,1,0:T(8,128)(2,1)S(1)} %get-tuple-element.12), channel_id=1, replica_groups=mesh['depth'=32,'height'=2,'view'=8] {'view'}, dimensions={0} | all-to-all | bytes 196608 | tf_op jit(solution)/shard_map/all_to_all | solution.py:451
  68.3 0.9 shard_map.144
  69.2 12.7 %all-to-all-start.3 = ((bf16[64,24,128]{2,1,0:T(8,128)(2,1)}), bf16[64,24,128]{2,1,0:T(8,128)(2,1)S(1)}, u32[]{:S(2)}, u32[]{:S(2)}) async-start(bf16[64,24,128]{2,1,0:T(8,128)(2,1)} %shard_map.144), calls=%async_computation.3 | async-start | bytes 786432 | tf_op jit(solution)/shard_map/all_to_all | solution.py:459
  81.9 3.0 %collective-permute-start.2 = (bf16[1,128,128]{2,1,0:T(8,128)(2,1)S(1)}, bf16[1,128,128]{2,1,0:T(8,128)(2,1)S(1)}, u32[]{:S(2)}, u32[]{:S(2)}) collective-permute-start(bf16[1,128,128]{2,1,0:T(8,128)(2,1)S(1)} %get-tuple-element.14), channel_id=1, source_target_pairs={{0,1},{1,0},{2,3},{3,2},{4,5},{5,4},{6,7},{7,6},{8,9},{9,8},{10,11... | collective-permute-start | bytes 98312 | tf_op jit(solution)/shard_map/ppermute | solution.py:458
  84.9 0.8 collective-permute-done.2
  85.7 2.2 %collective-permute-start.3 = (bf16[2,128,128]{2,1,0:T(8,128)(2,1)S(1)}, bf16[2,128,128]{2,1,0:T(8,128)(2,1)S(1)}, u32[]{:S(2)}, u32[]{:S(2)}) collective-permute-start(bf16[2,128,128]{2,1,0:T(8,128)(2,1)S(1)} %pad_maximum_fusion.2), channel_id=1, source_target_pairs={{0,2},{1,3},{2,0},{3,1},{4,6},{5,7},{6,4},{7,5},{8,10},{9,11},{10,... | collective-permute-start | bytes 196616 | tf_op jit(solution)/shard_map/ppermute | solution.py:458
  87.9 3.1 %collective-permute-done.3 = bf16[2,128,128]{2,1,0:T(8,128)(2,1)S(1)} collective-permute-done((bf16[2,128,128]{2,1,0:T(8,128)(2,1)S(1)}, bf16[2,128,128]{2,1,0:T(8,128)(2,1)S(1)}, u32[]{:S(2)}, u32[]{:S(2)}) %collective-permute-start.3) | collective-permute-done | bytes 65568 | tf_op jit(solution)/shard_map/ppermute | solution.py:458
  91.1 2.5 %collective-permute-start.4 = (bf16[4,128,128]{2,1,0:T(8,128)(2,1)S(1)}, bf16[4,128,128]{2,1,0:T(8,128)(2,1)S(1)}, u32[]{:S(2)}, u32[]{:S(2)}) collective-permute-start(bf16[4,128,128]{2,1,0:T(8,128)(2,1)S(1)} %pad_maximum_fusion.1), channel_id=1, source_target_pairs={{0,4},{1,5},{2,6},{3,7},{4,0},{5,1},{6,2},{7,3},{8,12},{9,13},{10,... | collective-permute-start | bytes 393224 | tf_op jit(solution)/shard_map/ppermute | solution.py:458
  93.6 3.9 %all-to-all-done.3.arrived_ref = bf16[64,24,128]{2,1,0:T(8,128)(2,1)S(1)} async-done(((bf16[64,24,128]{2,1,0:T(8,128)(2,1)}), bf16[64,24,128]{2,1,0:T(8,128)(2,1)S(1)}, u32[]{:S(2)}, u32[]{:S(2)}) %all-to-all-start.3) | async-done | bytes 393248 | tf_op jit(solution)/shard_map/all_to_all | solution.py:459
  98.2 6.5 %all-to-all-start.4 = ((f32[8,24,128]{2,1,0:T(8,128)}), f32[8,24,128]{2,1,0:T(8,128)S(1)}, u32[]{:S(2)}, u32[]{:S(2)}) async-start(f32[8,24,128]{2,1,0:T(8,128)} %shard_map.146), calls=%async_computation.4 | async-start | bytes 196608 | tf_op jit(solution)/shard_map/all_to_all | solution.py:475
  104.8 0.9 copy-done
  105.7 1.6 %shard_map.145 = f32[128,128]{1,0:T(8,128)} custom-call(s32[8,8]{1,0:T(8,128)S(1)} %copy-done.3, s32[8,8]{1,0:T(8,128)S(1)} %copy-done.4, bf16[8,128,128]{2,1,0:T(8,128)(2,1)S(1)} %pad_maximum_fusion.arrived_ref, bf16[8,128,128]{2,1,0:T(8,128)(2,1)S(1)} %copy-done), custom_call_target="tpu_custom_call" | custom-call | flops 100000000 | bytes 1000000 | tf_op jit(solution)/shard_map/pallas_call | solution.py:462
  107.3 2.4 %all-to-all-done.4 = f32[8,24,128]{2,1,0:T(8,128)S(1)} async-done(((f32[8,24,128]{2,1,0:T(8,128)}), f32[8,24,128]{2,1,0:T(8,128)S(1)}, u32[]{:S(2)}, u32[]{:S(2)}) %all-to-all-start.4) | async-done | bytes 98336 | tf_op jit(solution)/shard_map/all_to_all | solution.py:475
  109.7 1.1 shard_map.147
  (45 shorter events, 4.5 us)
Async XLA Ops:
  3.6 16.7 %copy-start.2 = (bf16[1,8,16,128]{3,2,1,0:T(8,128)(2,1)S(1)}, bf16[1,8,16,128]{3,2,1,0:T(8,128)(2,1)}, u32[]{:S(2)}) copy-start(bf16[1,8,16,128]{3,2,1,0:T(8,128)(2,1)} %param.20) | copy-start | bytes 98308
  20.3 1.3 %copy-start.6 = (bf16[16,16,3,3,3]{1,0,4,3,2:T(8,128)(2,1)S(1)}, bf16[16,16,3,3,3]{1,0,4,3,2:T(8,128)(2,1)}, u32[]{:S(2)}) copy-start(bf16[16,16,3,3,3]{1,0,4,3,2:T(8,128)(2,1)} %param.15) | copy-start | bytes 41476
  20.3 5.0 %collective-permute-start = (bf16[2,128,128]{2,1,0:T(8,128)(2,1)S(1)}, bf16[2,128,128]{2,1,0:T(8,128)(2,1)S(1)}, u32[]{:S(2)}, u32[]{:S(2)}) collective-permute-start(bf16[2,128,128]{2,1,0:T(8,128)(2,1)S(1)} %shard_map.139.own_ref), channel_id=1, source_target_pairs={{4,20},{5,21},{6,22},{7,23},{16,0},{17,1},{18,2},{19,3},{20,36},{2... | collective-permute-start | bytes 196616 | tf_op jit(solution)/shard_map/ppermute | solution.py:430
  21.7 9.9 %copy-start.5 = (bf16[16,16,3,3,3]{1,0,4,3,2:T(8,128)(2,1)S(1)}, bf16[16,16,3,3,3]{1,0,4,3,2:T(8,128)(2,1)}, u32[]{:S(2)}) copy-start(bf16[16,16,3,3,3]{1,0,4,3,2:T(8,128)(2,1)} %param.16) | copy-start | bytes 41476
  25.3 8.9 %collective-permute-start.1 = (bf16[4,64,128]{2,1,0:T(8,128)(2,1)S(1)}, bf16[4,64,128]{2,1,0:T(8,128)(2,1)S(1)}, u32[]{:S(2)}, u32[]{:S(2)}) collective-permute-start(bf16[4,64,128]{2,1,0:T(8,128)(2,1)S(1)} %shard_map.140), channel_id=1, source_target_pairs={{0,8},{8,0},{1,9},{9,1},{2,10},{10,2},{3,11},{11,3},{4,12},{12,4},... | collective-permute-start | bytes 196616 | tf_op jit(solution)/shard_map/ppermute | solution.py:437
  31.7 0.9 copy-start.7
  35.3 19.2 %all-to-all-start.1 = ((bf16[8,2,192,128]{3,2,1,0:T(8,128)(2,1)}), bf16[8,2,192,128]{3,2,1,0:T(8,128)(2,1)S(1)}, u32[]{:S(2)}, u32[]{:S(2)}) async-start(bf16[8,2,192,128]{3,2,1,0:T(8,128)(2,1)} %shard_map.141), calls=%async_computation.1 | async-start | bytes 1572864 | tf_op jit(solution)/shard_map/all_to_all | solution.py:448
  42.5 0.7 copy-start.8
  42.6 0.7 copy-start.9
  43.2 0.9 copy-start.1
  69.2 28.3 %all-to-all-start.3 = ((bf16[64,24,128]{2,1,0:T(8,128)(2,1)}), bf16[64,24,128]{2,1,0:T(8,128)(2,1)S(1)}, u32[]{:S(2)}, u32[]{:S(2)}) async-start(bf16[64,24,128]{2,1,0:T(8,128)(2,1)} %shard_map.144), calls=%async_computation.3 | async-start | bytes 786432 | tf_op jit(solution)/shard_map/all_to_all | solution.py:459
  81.9 3.9 %collective-permute-start.2 = (bf16[1,128,128]{2,1,0:T(8,128)(2,1)S(1)}, bf16[1,128,128]{2,1,0:T(8,128)(2,1)S(1)}, u32[]{:S(2)}, u32[]{:S(2)}) collective-permute-start(bf16[1,128,128]{2,1,0:T(8,128)(2,1)S(1)} %get-tuple-element.14), channel_id=1, source_target_pairs={{0,1},{1,0},{2,3},{3,2},{4,5},{5,4},{6,7},{7,6},{8,9},{9,8},{10,11... | collective-permute-start | bytes 98312 | tf_op jit(solution)/shard_map/ppermute | solution.py:458
  85.7 5.3 %collective-permute-start.3 = (bf16[2,128,128]{2,1,0:T(8,128)(2,1)S(1)}, bf16[2,128,128]{2,1,0:T(8,128)(2,1)S(1)}, u32[]{:S(2)}, u32[]{:S(2)}) collective-permute-start(bf16[2,128,128]{2,1,0:T(8,128)(2,1)S(1)} %pad_maximum_fusion.2), channel_id=1, source_target_pairs={{0,2},{1,3},{2,0},{3,1},{4,6},{5,7},{6,4},{7,5},{8,10},{9,11},{10,... | collective-permute-start | bytes 196616 | tf_op jit(solution)/shard_map/ppermute | solution.py:458
  91.1 13.7 %collective-permute-start.4 = (bf16[4,128,128]{2,1,0:T(8,128)(2,1)S(1)}, bf16[4,128,128]{2,1,0:T(8,128)(2,1)S(1)}, u32[]{:S(2)}, u32[]{:S(2)}) collective-permute-start(bf16[4,128,128]{2,1,0:T(8,128)(2,1)S(1)} %pad_maximum_fusion.1), channel_id=1, source_target_pairs={{0,4},{1,5},{2,6},{3,7},{4,0},{5,1},{6,2},{7,3},{8,12},{9,13},{10,... | collective-permute-start | bytes 393224 | tf_op jit(solution)/shard_map/ppermute | solution.py:458
  98.2 11.5 %all-to-all-start.4 = ((f32[8,24,128]{2,1,0:T(8,128)}), f32[8,24,128]{2,1,0:T(8,128)S(1)}, u32[]{:S(2)}, u32[]{:S(2)}) async-start(f32[8,24,128]{2,1,0:T(8,128)} %shard_map.146), calls=%async_computation.4 | async-start | bytes 196608 | tf_op jit(solution)/shard_map/all_to_all | solution.py:475
  104.7 0.9 copy-start
  104.7 1.0 copy-start.3
  104.7 1.0 copy-start.4

commit v7 on v6

--- a/solution.py
+++ b/solution.py
@@ -80,15 +80,27 @@
         parts_ref[v, 1] = planes[jnp.where(away == half, 2, jnp.where(away < half, 1, 3))]
 
 
-def lift_kernel(bricks_ref, rows_ref, feats_hbm, weights_hbm, out_ref, feats, weights, total, sems):
-    fetch_feats = pltpu.make_async_copy(feats_hbm, feats, sems.at[0])
-    fetch_weights = pltpu.make_async_copy(weights_hbm, weights, sems.at[1])
-    fetch_feats.start()
-    fetch_weights.start()
+def lift_kernel(
+    bricks_hbm,
+    rows_hbm,
+    feats_hbm,
+    weights_hbm,
+    out_ref,
+    bricks_ref,
+    rows_ref,
+    feats,
+    weights,
+    total,
+    sems,
+):
+    pairs = (bricks_hbm, bricks_ref), (rows_hbm, rows_ref), (feats_hbm, feats), (weights_hbm, weights)
+    fetches = [pltpu.make_async_copy(*pair, sems.at[n]) for n, pair in enumerate(pairs)]
+    for fetch in fetches:
+        fetch.start()
     total[...] = jnp.zeros_like(total)
     tiles, slots = bricks_ref.shape
-    fetch_feats.wait()
-    fetch_weights.wait()
+    for fetch in fetches:
+        fetch.wait()
     for k in range(slots):
         blocks = lax.dot_general(
             feats[...], weights[k], (((1,), (1,)), ((), ())), preferred_element_type=F32
@@ -380,16 +392,18 @@
 
     partial = pl.pallas_call(
         lift_kernel,
-        in_specs=[smem_spec(), smem_spec(), hbm_spec(), hbm_spec()],
+        in_specs=[hbm_spec()] * 4,
         out_specs=vmem_spec(),
         **call(
             lift_kernel,
             jax.ShapeDtypeStruct((views, HALF, X), BF16),
             [
+                pltpu.SMEM((tiles, slots), jnp.int32),
+                pltpu.SMEM((tiles, slots), jnp.int32),
                 pltpu.VMEM((tiles * C, X), BF16),
                 pltpu.VMEM((slots, X, X), BF16),
                 pltpu.VMEM((views * YB, C, X), F32),
-                pltpu.SemaphoreType.DMA((2,)),
+                pltpu.SemaphoreType.DMA((4,)),
             ],
             vmem=62,
             flops=10**8,

time: 112 us -> 111 us (level)
  no operation moved by 1% of the time
where the time goes in v7:
time: 111 us; the launch traced here: 110 us
  starting transfers between devices  41.3 us (37%)
  waiting for transfers between devices  25.1 us (23%)
  blocking collectives  24.9 us (22%)
  Pallas kernels  13.7 us (12%)
  local copies, waits for them, and re-layouts  4.03 us (4%)
    all_to_all x1, blocking collectives, body(): pieces = lax.all_to_all(partial, 'view', 0, 0, tiled=True)  16.7 us
    all_to_all x1, starting transfers between devices, body(): sums = lax.all_to_all(sums, across, 0, 0, tiled=True)  12.7 us
    all_to_all x1, waiting for transfers between devices, body(): arrived = lax.all_to_all(parts, 'view', 0, 0, tiled=True)  9.72 us
    all_to_all x1, blocking collectives, body(): sums = lax.all_to_all(sums, 'view', 0, 0, tiled=True)  8.23 us
    ppermute x3, starting transfers between devices, body(): lax.ppermute(lift_grad, 'view', pairs)  7.74 us
    all_to_all x1, starting transfers between devices, body(): arrived = lax.all_to_all(parts, 'view', 0, 0, tiled=True)  6.86 us
    all_to_all x1, starting transfers between devices, body(): sums = lax.all_to_all(sums, 'view', 0, 0, tiled=True).reshape(12 * C, X)  6.52 us
    ppermute x1, starting transfers between devices, body(): rim = lax.ppermute(facing, 'height', [(0, 1), (1, 0)])  6.24 us
  transfers between devices with their start and end apart: 8, of which 7 were waited for; matrix products, arithmetic and copies ran while one was open for 1% of the time, Pallas kernels for 3%

profile of v7, /device:TPU:1, one launch (start us, length us, event | category | flops | bytes accessed | tf_op | source)
XLA Modules:
  0.0 110.0 jit_solution(4291236747021363140)
XLA Ops:
  0.6 2.2 %shard_map.138 = bf16[8,128,128]{2,1,0:T(8,128)(2,1)} custom-call(s32[8,8]{1,0:T(8,128)} %bricks_ref.1, s32[8,8]{1,0:T(8,128)} %rows_ref.1, bf16[128,128]{1,0:T(8,128)(2,1)} %bitcast.33, bf16[8,128,128]{2,1,0:T(8,128)(2,1)} %weights_ref.1), custom_call_target="tpu_custom_call" | custom-call | flops 100000000 | bytes 1000000 | tf_op jit(solution)/shard_map/pallas_call | solution.py:393
  2.8 16.7 %all_to_all.25.pieces_ref = bf16[8,128,128]{2,1,0:T(8,128)(2,1)S(1)} all-to-all(bf16[8,128,128]{2,1,0:T(8,128)(2,1)} %shard_map.138), channel_id=1, replica_groups=mesh['depth'=32,'height'=2,'view'=8] {'view'}, dimensions={0} | all-to-all | bytes 524288 | tf_op jit(solution)/shard_map/all_to_all | solution.py:413
  19.6 1.3 %collective-permute-start = (bf16[2,128,128]{2,1,0:T(8,128)(2,1)S(1)}, bf16[2,128,128]{2,1,0:T(8,128)(2,1)S(1)}, u32[]{:S(2)}, u32[]{:S(2)}) collective-permute-start(bf16[2,128,128]{2,1,0:T(8,128)(2,1)S(1)} %shard_map.139.own_ref), channel_id=1, source_target_pairs={{4,20},{5,21},{6,22},{7,23},{16,0},{17,1},{18,2},{19,3},{20,36},{2... | collective-permute-start | bytes 196616 | tf_op jit(solution)/shard_map/ppermute | solution.py:444
  20.9 3.7 %collective-permute-done.far_ref = bf16[2,128,128]{2,1,0:T(8,128)(2,1)S(1)} collective-permute-done((bf16[2,128,128]{2,1,0:T(8,128)(2,1)S(1)}, bf16[2,128,128]{2,1,0:T(8,128)(2,1)S(1)}, u32[]{:S(2)}, u32[]{:S(2)}) %collective-permute-start) | collective-permute-done | bytes 65568 | tf_op jit(solution)/shard_map/ppermute | solution.py:444
  24.6 6.2 %collective-permute-start.1 = (bf16[4,64,128]{2,1,0:T(8,128)(2,1)S(1)}, bf16[4,64,128]{2,1,0:T(8,128)(2,1)S(1)}, u32[]{:S(2)}, u32[]{:S(2)}) collective-permute-start(bf16[4,64,128]{2,1,0:T(8,128)(2,1)S(1)} %shard_map.140), channel_id=1, source_target_pairs={{0,8},{8,0},{1,9},{9,1},{2,10},{10,2},{3,11},{11,3},{4,12},{12,4},... | collective-permute-start | bytes 196616 | tf_op jit(solution)/shard_map/ppermute | solution.py:451
  32.0 1.5 %collective-permute-done.1.rim_ref = bf16[4,64,128]{2,1,0:T(8,128)(2,1)S(1)} collective-permute-done((bf16[4,64,128]{2,1,0:T(8,128)(2,1)S(1)}, bf16[4,64,128]{2,1,0:T(8,128)(2,1)S(1)}, u32[]{:S(2)}, u32[]{:S(2)}) %collective-permute-start.1) | collective-permute-done | bytes 65568 | tf_op jit(solution)/shard_map/ppermute | solution.py:451
  33.5 1.0 shard_map.141
  34.5 6.9 %all-to-all-start.1 = ((bf16[8,2,192,128]{3,2,1,0:T(8,128)(2,1)}), bf16[8,2,192,128]{3,2,1,0:T(8,128)(2,1)S(1)}, u32[]{:S(2)}, u32[]{:S(2)}) async-start(bf16[8,2,192,128]{3,2,1,0:T(8,128)(2,1)} %shard_map.141), calls=%async_computation.1 | async-start | bytes 1572864 | tf_op jit(solution)/shard_map/all_to_all | solution.py:462
  43.9 9.7 %all-to-all-done.1.arrived_ref = bf16[8,2,192,128]{3,2,1,0:T(8,128)(2,1)S(1)} async-done(((bf16[8,2,192,128]{3,2,1,0:T(8,128)(2,1)}), bf16[8,2,192,128]{3,2,1,0:T(8,128)(2,1)S(1)}, u32[]{:S(2)}, u32[]{:S(2)}) %all-to-all-start.1) | async-done | bytes 786464 | tf_op jit(solution)/shard_map/all_to_all | solution.py:462
  53.6 5.7 %shard_map.143 = (bf16[128,128]{1,0:T(8,128)(2,1)}, bf16[1,128,128]{2,1,0:T(8,128)(2,1)S(1)}, bf16[8,48,128]{2,1,0:T(8,128)(2,1)S(1)}) custom-call(bf16[8,2,192,128]{3,2,1,0:T(8,128)(2,1)S(1)} %all-to-all-done.1.arrived_ref, bf16[96,1792]{1,0:T(8,128)(2,1)S(1)} %shard_map.142.block_hbm, f32[2,192,1]{2,1,0:T(8,128)S(1)} %copy.23.bias_ref), custom_call_target="tpu_custom_call" | custom-call | flops 10000000000 | bytes 10000000 | tf_op jit(solution)/shard_map/pallas_call | solution.py:338
  59.3 8.2 %all_to_all.26.arrived_ref = bf16[8,48,128]{2,1,0:T(8,128)(2,1)S(1)} all-to-all(bf16[8,48,128]{2,1,0:T(8,128)(2,1)S(1)} %get-tuple-element.12), channel_id=1, replica_groups=mesh['depth'=32,'height'=2,'view'=8] {'view'}, dimensions={0} | all-to-all | bytes 196608 | tf_op jit(solution)/shard_map/all_to_all | solution.py:465
  67.6 0.9 shard_map.144
  68.4 12.7 %all-to-all-start.3 = ((bf16[64,24,128]{2,1,0:T(8,128)(2,1)}), bf16[64,24,128]{2,1,0:T(8,128)(2,1)S(1)}, u32[]{:S(2)}, u32[]{:S(2)}) async-start(bf16[64,24,128]{2,1,0:T(8,128)(2,1)} %shard_map.144), calls=%async_computation.3 | async-start | bytes 786432 | tf_op jit(solution)/shard_map/all_to_all | solution.py:473
  81.1 3.0 %collective-permute-start.2 = (bf16[1,128,128]{2,1,0:T(8,128)(2,1)S(1)}, bf16[1,128,128]{2,1,0:T(8,128)(2,1)S(1)}, u32[]{:S(2)}, u32[]{:S(2)}) collective-permute-start(bf16[1,128,128]{2,1,0:T(8,128)(2,1)S(1)} %get-tuple-element.14), channel_id=1, source_target_pairs={{0,1},{1,0},{2,3},{3,2},{4,5},{5,4},{6,7},{7,6},{8,9},{9,8},{10,11... | collective-permute-start | bytes 98312 | tf_op jit(solution)/shard_map/ppermute | solution.py:472
  84.1 0.8 collective-permute-done.2
  85.0 2.2 %collective-permute-start.3 = (bf16[2,128,128]{2,1,0:T(8,128)(2,1)S(1)}, bf16[2,128,128]{2,1,0:T(8,128)(2,1)S(1)}, u32[]{:S(2)}, u32[]{:S(2)}) collective-permute-start(bf16[2,128,128]{2,1,0:T(8,128)(2,1)S(1)} %pad_maximum_fusion.2), channel_id=1, source_target_pairs={{0,2},{1,3},{2,0},{3,1},{4,6},{5,7},{6,4},{7,5},{8,10},{9,11},{10,... | collective-permute-start | bytes 196616 | tf_op jit(solution)/shard_map/ppermute | solution.py:472
  87.2 3.1 %collective-permute-done.3 = bf16[2,128,128]{2,1,0:T(8,128)(2,1)S(1)} collective-permute-done((bf16[2,128,128]{2,1,0:T(8,128)(2,1)S(1)}, bf16[2,128,128]{2,1,0:T(8,128)(2,1)S(1)}, u32[]{:S(2)}, u32[]{:S(2)}) %collective-permute-start.3) | collective-permute-done | bytes 65568 | tf_op jit(solution)/shard_map/ppermute | solution.py:472
  90.3 2.5 %collective-permute-start.4 = (bf16[4,128,128]{2,1,0:T(8,128)(2,1)S(1)}, bf16[4,128,128]{2,1,0:T(8,128)(2,1)S(1)}, u32[]{:S(2)}, u32[]{:S(2)}) collective-permute-start(bf16[4,128,128]{2,1,0:T(8,128)(2,1)S(1)} %pad_maximum_fusion.1), channel_id=1, source_target_pairs={{0,4},{1,5},{2,6},{3,7},{4,0},{5,1},{6,2},{7,3},{8,12},{9,13},{10,... | collective-permute-start | bytes 393224 | tf_op jit(solution)/shard_map/ppermute | solution.py:472
  92.8 3.9 %all-to-all-done.3.arrived_ref = bf16[64,24,128]{2,1,0:T(8,128)(2,1)S(1)} async-done(((bf16[64,24,128]{2,1,0:T(8,128)(2,1)}), bf16[64,24,128]{2,1,0:T(8,128)(2,1)S(1)}, u32[]{:S(2)}, u32[]{:S(2)}) %all-to-all-start.3) | async-done | bytes 393248 | tf_op jit(solution)/shard_map/all_to_all | solution.py:473
  97.4 6.5 %all-to-all-start.4 = ((f32[8,24,128]{2,1,0:T(8,128)}), f32[8,24,128]{2,1,0:T(8,128)S(1)}, u32[]{:S(2)}, u32[]{:S(2)}) async-start(f32[8,24,128]{2,1,0:T(8,128)} %shard_map.146), calls=%async_computation.4 | async-start | bytes 196608 | tf_op jit(solution)/shard_map/all_to_all | solution.py:489
  104.0 0.9 copy-done
  104.9 1.6 %shard_map.145 = f32[128,128]{1,0:T(8,128)} custom-call(s32[8,8]{1,0:T(8,128)S(1)} %copy-done.3, s32[8,8]{1,0:T(8,128)S(1)} %copy-done.4, bf16[8,128,128]{2,1,0:T(8,128)(2,1)S(1)} %pad_maximum_fusion.arrived_ref, bf16[8,128,128]{2,1,0:T(8,128)(2,1)S(1)} %copy-done), custom_call_target="tpu_custom_call" | custom-call | flops 100000000 | bytes 1000000 | tf_op jit(solution)/shard_map/pallas_call | solution.py:476
  106.5 2.4 %all-to-all-done.4 = f32[8,24,128]{2,1,0:T(8,128)S(1)} async-done(((f32[8,24,128]{2,1,0:T(8,128)}), f32[8,24,128]{2,1,0:T(8,128)S(1)}, u32[]{:S(2)}, u32[]{:S(2)}) %all-to-all-start.4) | async-done | bytes 98336 | tf_op jit(solution)/shard_map/all_to_all | solution.py:489
  109.0 1.1 shard_map.147
  (45 shorter events, 4.5 us)
Async XLA Ops:
  2.8 16.7 %copy-start.2 = (bf16[1,8,16,128]{3,2,1,0:T(8,128)(2,1)S(1)}, bf16[1,8,16,128]{3,2,1,0:T(8,128)(2,1)}, u32[]{:S(2)}) copy-start(bf16[1,8,16,128]{3,2,1,0:T(8,128)(2,1)} %param.20) | copy-start | bytes 98308
  19.5 1.3 %copy-start.6 = (bf16[16,16,3,3,3]{1,0,4,3,2:T(8,128)(2,1)S(1)}, bf16[16,16,3,3,3]{1,0,4,3,2:T(8,128)(2,1)}, u32[]{:S(2)}) copy-start(bf16[16,16,3,3,3]{1,0,4,3,2:T(8,128)(2,1)} %param.15) | copy-start | bytes 41476
  19.6 5.0 %collective-permute-start = (bf16[2,128,128]{2,1,0:T(8,128)(2,1)S(1)}, bf16[2,128,128]{2,1,0:T(8,128)(2,1)S(1)}, u32[]{:S(2)}, u32[]{:S(2)}) collective-permute-start(bf16[2,128,128]{2,1,0:T(8,128)(2,1)S(1)} %shard_map.139.own_ref), channel_id=1, source_target_pairs={{4,20},{5,21},{6,22},{7,23},{16,0},{17,1},{18,2},{19,3},{20,36},{2... | collective-permute-start | bytes 196616 | tf_op jit(solution)/shard_map/ppermute | solution.py:444
  20.9 9.9 %copy-start.5 = (bf16[16,16,3,3,3]{1,0,4,3,2:T(8,128)(2,1)S(1)}, bf16[16,16,3,3,3]{1,0,4,3,2:T(8,128)(2,1)}, u32[]{:S(2)}) copy-start(bf16[16,16,3,3,3]{1,0,4,3,2:T(8,128)(2,1)} %param.16) | copy-start | bytes 41476
  24.6 8.9 %collective-permute-start.1 = (bf16[4,64,128]{2,1,0:T(8,128)(2,1)S(1)}, bf16[4,64,128]{2,1,0:T(8,128)(2,1)S(1)}, u32[]{:S(2)}, u32[]{:S(2)}) collective-permute-start(bf16[4,64,128]{2,1,0:T(8,128)(2,1)S(1)} %shard_map.140), channel_id=1, source_target_pairs={{0,8},{8,0},{1,9},{9,1},{2,10},{10,2},{3,11},{11,3},{4,12},{12,4},... | collective-permute-start | bytes 196616 | tf_op jit(solution)/shard_map/ppermute | solution.py:451
  31.0 0.9 copy-start.7
  34.5 19.2 %all-to-all-start.1 = ((bf16[8,2,192,128]{3,2,1,0:T(8,128)(2,1)}), bf16[8,2,192,128]{3,2,1,0:T(8,128)(2,1)S(1)}, u32[]{:S(2)}, u32[]{:S(2)}) async-start(bf16[8,2,192,128]{3,2,1,0:T(8,128)(2,1)} %shard_map.141), calls=%async_computation.1 | async-start | bytes 1572864 | tf_op jit(solution)/shard_map/all_to_all | solution.py:462
  41.8 0.7 copy-start.8
  41.8 0.7 copy-start.9
  42.4 0.9 copy-start.1
  68.4 28.3 %all-to-all-start.3 = ((bf16[64,24,128]{2,1,0:T(8,128)(2,1)}), bf16[64,24,128]{2,1,0:T(8,128)(2,1)S(1)}, u32[]{:S(2)}, u32[]{:S(2)}) async-start(bf16[64,24,128]{2,1,0:T(8,128)(2,1)} %shard_map.144), calls=%async_computation.3 | async-start | bytes 786432 | tf_op jit(solution)/shard_map/all_to_all | solution.py:473
  81.1 3.9 %collective-permute-start.2 = (bf16[1,128,128]{2,1,0:T(8,128)(2,1)S(1)}, bf16[1,128,128]{2,1,0:T(8,128)(2,1)S(1)}, u32[]{:S(2)}, u32[]{:S(2)}) collective-permute-start(bf16[1,128,128]{2,1,0:T(8,128)(2,1)S(1)} %get-tuple-element.14), channel_id=1, source_target_pairs={{0,1},{1,0},{2,3},{3,2},{4,5},{5,4},{6,7},{7,6},{8,9},{9,8},{10,11... | collective-permute-start | bytes 98312 | tf_op jit(solution)/shard_map/ppermute | solution.py:472
  85.0 5.3 %collective-permute-start.3 = (bf16[2,128,128]{2,1,0:T(8,128)(2,1)S(1)}, bf16[2,128,128]{2,1,0:T(8,128)(2,1)S(1)}, u32[]{:S(2)}, u32[]{:S(2)}) collective-permute-start(bf16[2,128,128]{2,1,0:T(8,128)(2,1)S(1)} %pad_maximum_fusion.2), channel_id=1, source_target_pairs={{0,2},{1,3},{2,0},{3,1},{4,6},{5,7},{6,4},{7,5},{8,10},{9,11},{10,... | collective-permute-start | bytes 196616 | tf_op jit(solution)/shard_map/ppermute | solution.py:472
  90.3 13.7 %collective-permute-start.4 = (bf16[4,128,128]{2,1,0:T(8,128)(2,1)S(1)}, bf16[4,128,128]{2,1,0:T(8,128)(2,1)S(1)}, u32[]{:S(2)}, u32[]{:S(2)}) collective-permute-start(bf16[4,128,128]{2,1,0:T(8,128)(2,1)S(1)} %pad_maximum_fusion.1), channel_id=1, source_target_pairs={{0,4},{1,5},{2,6},{3,7},{4,0},{5,1},{6,2},{7,3},{8,12},{9,13},{10,... | collective-permute-start | bytes 393224 | tf_op jit(solution)/shard_map/ppermute | solution.py:472
  97.4 11.5 %all-to-all-start.4 = ((f32[8,24,128]{2,1,0:T(8,128)}), f32[8,24,128]{2,1,0:T(8,128)S(1)}, u32[]{:S(2)}, u32[]{:S(2)}) async-start(f32[8,24,128]{2,1,0:T(8,128)} %shard_map.146), calls=%async_computation.4 | async-start | bytes 196608 | tf_op jit(solution)/shard_map/all_to_all | solution.py:489
  104.0 0.9 copy-start
  104.0 1.0 copy-start.3
  104.0 1.0 copy-start.4

commit v8 on v7

--- a/solution.py
+++ b/solution.py
@@ -110,13 +110,17 @@
     out_ref[...] = total[...].astype(BF16).reshape(out_ref.shape)
 
 
+def reversed_bits(n):
+    return ((n & 1) << 2) | (n & 2) | ((n >> 2) & 1)
+
+
 def camera_kernel(bricks_ref, rows_ref, arrived_ref, weights_ref, out_ref, chosen):
     tiles, slots = bricks_ref.shape
     for k in range(slots):
         for t in range(tiles):
             at = pl.multiple_of(rows_ref[t, k] * C, C)
             chosen[t * C : (t + 1) * C, k * X : (k + 1) * X] = arrived_ref[
-                jnp.bitwise_xor(bricks_ref[t, k], lax.axis_index("view")), pl.ds(at, C), :
+                reversed_bits(bricks_ref[t, k] ^ lax.axis_index("view")), pl.ds(at, C), :
             ]
     out_ref[...] = jnp.dot(
         chosen[...], weights_ref[...].reshape(slots * X, X), preferred_element_type=F32
@@ -221,13 +225,11 @@
             preferred_element_type=F32,
         )
 
-    def pairs(count):
-        return [(i, min(2, count - i)) for i in range(0, count, 2)]
+    def runs(count):
+        return [(i, min(4, count - i)) for i in range(0, count, 4)]
 
     for i in range(9):
         put(s_lift, i, fetch(i - 4, 0))
-    for i in range(7):
-        put(s_grad, i, fetch(i - 3, 1))
 
     fetch_blocks.wait()
     at = lax.broadcasted_iota(jnp.int32, (C, 14 * X), 1)
@@ -249,16 +251,18 @@
             band_ref[n, y * C : (y + 1) * C, :] = rows[:, : 3 * K3].astype(BF16)
 
     bias1, bias2 = bias_ref[0], bias_ref[1]
-    for i, n in pairs(7):
+    for i, n in runs(7):
         for j, pre in enumerate(conv(0, s_lift, i, n)):
             act, slope = silu_and_slope(pre + bias1)
             put(s_act1, i + j, masked(i + j - 3, act))
             if abs(i + j - 3) <= 1:
                 slope1[i + j - 2] = slope
-    for i, n in pairs(5):
+    for i in range(7):
+        put(s_grad, i, fetch(i - 3, 1))
+    for i, n in runs(5):
         for j, up in enumerate(conv(3, s_grad, i, n)):
             up2[i + j] = up
-    for i, n in pairs(5):
+    for i, n in runs(5):
         for j, pre in enumerate(conv(1, s_act1, i, n)):
             at = i + j
             act, slope = silu_and_slope(pre + bias2)
@@ -269,7 +273,7 @@
             if abs(at - 2) <= 1:
                 before = s_act1[YC : 2 * YC, (at + 1) * X : (at + 2) * X].astype(F32)
                 put(s_act2, at - 1, masked(at - 2, act + before))
-    for i, n in pairs(3):
+    for i, n in runs(3):
         for j, up in enumerate(conv(4, s_back2, i, n)):
             at = i + j
             back = (up2[at + 1] + up) * slope1[at]
@@ -467,7 +471,7 @@
     across = ("depth", "height")
     sums = for_each_sum(first_sum_kernel, sums, depths * heights, BF16)
     sums, lift_grad = lax.optimization_barrier((sums, lift_grad))
-    for step in (1, 2, 4):
+    for step in (4, 2, 1):
         pairs = [(v, v ^ step) for v in range(views)]
         lift_grad = jnp.concatenate([lift_grad, lax.ppermute(lift_grad, "view", pairs)])
     sums = lax.all_to_all(sums, across, 0, 0, tiled=True)

time: 111 us -> 111 us (level)
    all_to_all x1, waiting for transfers between devices: 3.87 us -> 0.01 us  [body(): sums = lax.all_to_all(sums, across, 0, 0, tiled=True)]
    ppermute x3, waiting for transfers between devices: 3.94 us -> 6.9 us  [body(): lax.ppermute(lift_grad, 'view', pairs)]
    ppermute x3, starting transfers between devices: 7.74 us -> 9.57 us  [body(): lax.ppermute(lift_grad, 'view', pairs)]
  transfers between devices with their start and end apart: 8 -> 8, of which waited for: 7 -> 6; matrix products, arithmetic and copies ran while one was open for 1% -> 1% of each run, Pallas kernels for 3% -> 3%
where the time goes in v8:
time: 111 us; the launch traced here: 110 us
  starting transfers between devices  42.2 us (38%)
  blocking collectives  24.9 us (22%)
  waiting for transfers between devices  24.1 us (22%)
  Pallas kernels  13.8 us (12%)
  local copies, waits for them, and re-layouts  4.03 us (4%)
    all_to_all x1, blocking collectives, body(): pieces = lax.all_to_all(partial, 'view', 0, 0, tiled=True)  16.7 us
    all_to_all x1, starting transfers between devices, body(): sums = lax.all_to_all(sums, across, 0, 0, tiled=True)  12.7 us
    all_to_all x1, waiting for transfers between devices, body(): arrived = lax.all_to_all(parts, 'view', 0, 0, tiled=True)  9.72 us
    ppermute x3, starting transfers between devices, body(): lax.ppermute(lift_grad, 'view', pairs)  9.57 us
    all_to_all x1, blocking collectives, body(): sums = lax.all_to_all(sums, 'view', 0, 0, tiled=True)  8.22 us
    ppermute x3, waiting for transfers between devices, body(): lax.ppermute(lift_grad, 'view', pairs)  6.9 us
    all_to_all x1, starting transfers between devices, body(): arrived = lax.all_to_all(parts, 'view', 0, 0, tiled=True)  6.86 us
    ppermute x1, starting transfers between devices, body(): rim = lax.ppermute(facing, 'height', [(0, 1), (1, 0)])  6.24 us
  transfers between devices with their start and end apart: 8, of which 6 were waited for; matrix products, arithmetic and copies ran while one was open for 1% of the time, Pallas kernels for 3%

profile of v8, /device:TPU:1, one launch (start us, length us, event | category | flops | bytes accessed | tf_op | source)
XLA Modules:
  0.0 110.0 jit_solution(6814625317219110913)
XLA Ops:
  0.6 2.2 %shard_map.138 = bf16[8,128,128]{2,1,0:T(8,128)(2,1)} custom-call(s32[8,8]{1,0:T(8,128)} %bricks_ref.1, s32[8,8]{1,0:T(8,128)} %rows_ref.1, bf16[128,128]{1,0:T(8,128)(2,1)} %bitcast.33, bf16[8,128,128]{2,1,0:T(8,128)(2,1)} %weights_ref.1), custom_call_target="tpu_custom_call" | custom-call | flops 100000000 | bytes 1000000 | tf_op jit(solution)/shard_map/pallas_call | solution.py:397
  2.8 16.7 %all_to_all.25.pieces_ref = bf16[8,128,128]{2,1,0:T(8,128)(2,1)S(1)} all-to-all(bf16[8,128,128]{2,1,0:T(8,128)(2,1)} %shard_map.138), channel_id=1, replica_groups=mesh['depth'=32,'height'=2,'view'=8] {'view'}, dimensions={0} | all-to-all | bytes 524288 | tf_op jit(solution)/shard_map/all_to_all | solution.py:417
  19.6 1.3 %collective-permute-start = (bf16[2,128,128]{2,1,0:T(8,128)(2,1)S(1)}, bf16[2,128,128]{2,1,0:T(8,128)(2,1)S(1)}, u32[]{:S(2)}, u32[]{:S(2)}) collective-permute-start(bf16[2,128,128]{2,1,0:T(8,128)(2,1)S(1)} %shard_map.139.own_ref), channel_id=1, source_target_pairs={{4,20},{5,21},{6,22},{7,23},{16,0},{17,1},{18,2},{19,3},{20,36},{2... | collective-permute-start | bytes 196616 | tf_op jit(solution)/shard_map/ppermute | solution.py:448
  20.9 3.7 %collective-permute-done.far_ref = bf16[2,128,128]{2,1,0:T(8,128)(2,1)S(1)} collective-permute-done((bf16[2,128,128]{2,1,0:T(8,128)(2,1)S(1)}, bf16[2,128,128]{2,1,0:T(8,128)(2,1)S(1)}, u32[]{:S(2)}, u32[]{:S(2)}) %collective-permute-start) | collective-permute-done | bytes 65568 | tf_op jit(solution)/shard_map/ppermute | solution.py:448
  24.6 6.2 %collective-permute-start.1 = (bf16[4,64,128]{2,1,0:T(8,128)(2,1)S(1)}, bf16[4,64,128]{2,1,0:T(8,128)(2,1)S(1)}, u32[]{:S(2)}, u32[]{:S(2)}) collective-permute-start(bf16[4,64,128]{2,1,0:T(8,128)(2,1)S(1)} %shard_map.140), channel_id=1, source_target_pairs={{0,8},{8,0},{1,9},{9,1},{2,10},{10,2},{3,11},{11,3},{4,12},{12,4},... | collective-permute-start | bytes 196616 | tf_op jit(solution)/shard_map/ppermute | solution.py:455
  31.1 0.8 copy-done.7
  32.0 1.5 %collective-permute-done.1.rim_ref = bf16[4,64,128]{2,1,0:T(8,128)(2,1)S(1)} collective-permute-done((bf16[4,64,128]{2,1,0:T(8,128)(2,1)S(1)}, bf16[4,64,128]{2,1,0:T(8,128)(2,1)S(1)}, u32[]{:S(2)}, u32[]{:S(2)}) %collective-permute-start.1) | collective-permute-done | bytes 65568 | tf_op jit(solution)/shard_map/ppermute | solution.py:455
  33.5 1.0 shard_map.141
  34.5 6.9 %all-to-all-start.1 = ((bf16[8,2,192,128]{3,2,1,0:T(8,128)(2,1)}), bf16[8,2,192,128]{3,2,1,0:T(8,128)(2,1)S(1)}, u32[]{:S(2)}, u32[]{:S(2)}) async-start(bf16[8,2,192,128]{3,2,1,0:T(8,128)(2,1)} %shard_map.141), calls=%async_computation.1 | async-start | bytes 1572864 | tf_op jit(solution)/shard_map/all_to_all | solution.py:466
  43.9 9.7 %all-to-all-done.1.arrived_ref = bf16[8,2,192,128]{3,2,1,0:T(8,128)(2,1)S(1)} async-done(((bf16[8,2,192,128]{3,2,1,0:T(8,128)(2,1)}), bf16[8,2,192,128]{3,2,1,0:T(8,128)(2,1)S(1)}, u32[]{:S(2)}, u32[]{:S(2)}) %all-to-all-start.1) | async-done | bytes 786464 | tf_op jit(solution)/shard_map/all_to_all | solution.py:466
  53.6 5.7 %shard_map.143 = (bf16[128,128]{1,0:T(8,128)(2,1)}, bf16[1,128,128]{2,1,0:T(8,128)(2,1)S(1)}, bf16[8,48,128]{2,1,0:T(8,128)(2,1)S(1)}) custom-call(bf16[8,2,192,128]{3,2,1,0:T(8,128)(2,1)S(1)} %all-to-all-done.1.arrived_ref, bf16[96,1792]{1,0:T(8,128)(2,1)S(1)} %shard_map.142.block_hbm, f32[2,192,1]{2,1,0:T(8,128)S(1)} %copy.23.bias_ref), custom_call_target="tpu_custom_call" | custom-call | flops 10000000000 | bytes 10000000 | tf_op jit(solution)/shard_map/pallas_call | solution.py:342
  59.4 8.2 %all_to_all.26.arrived_ref = bf16[8,48,128]{2,1,0:T(8,128)(2,1)S(1)} all-to-all(bf16[8,48,128]{2,1,0:T(8,128)(2,1)S(1)} %get-tuple-element.12), channel_id=1, replica_groups=mesh['depth'=32,'height'=2,'view'=8] {'view'}, dimensions={0} | all-to-all | bytes 196608 | tf_op jit(solution)/shard_map/all_to_all | solution.py:469
  67.6 0.9 shard_map.144
  68.5 12.7 %all-to-all-start.3 = ((bf16[64,24,128]{2,1,0:T(8,128)(2,1)}), bf16[64,24,128]{2,1,0:T(8,128)(2,1)S(1)}, u32[]{:S(2)}, u32[]{:S(2)}) async-start(bf16[64,24,128]{2,1,0:T(8,128)(2,1)} %shard_map.144), calls=%async_computation.3 | async-start | bytes 786432 | tf_op jit(solution)/shard_map/all_to_all | solution.py:477
  81.1 2.7 %collective-permute-start.2 = (bf16[1,128,128]{2,1,0:T(8,128)(2,1)S(1)}, bf16[1,128,128]{2,1,0:T(8,128)(2,1)S(1)}, u32[]{:S(2)}, u32[]{:S(2)}) collective-permute-start(bf16[1,128,128]{2,1,0:T(8,128)(2,1)S(1)} %get-tuple-element.14), channel_id=1, source_target_pairs={{0,4},{1,5},{2,6},{3,7},{4,0},{5,1},{6,2},{7,3},{8,12},{9,13},{10,... | collective-permute-start | bytes 98312 | tf_op jit(solution)/shard_map/ppermute | solution.py:476
  83.8 3.8 %collective-permute-done.2 = bf16[1,128,128]{2,1,0:T(8,128)(2,1)S(1)} collective-permute-done((bf16[1,128,128]{2,1,0:T(8,128)(2,1)S(1)}, bf16[1,128,128]{2,1,0:T(8,128)(2,1)S(1)}, u32[]{:S(2)}, u32[]{:S(2)}) %collective-permute-start.2) | collective-permute-done | bytes 32800 | tf_op jit(solution)/shard_map/ppermute | solution.py:476
  87.6 2.2 %collective-permute-start.3 = (bf16[2,128,128]{2,1,0:T(8,128)(2,1)S(1)}, bf16[2,128,128]{2,1,0:T(8,128)(2,1)S(1)}, u32[]{:S(2)}, u32[]{:S(2)}) collective-permute-start(bf16[2,128,128]{2,1,0:T(8,128)(2,1)S(1)} %pad_maximum_fusion.2), channel_id=1, source_target_pairs={{0,2},{1,3},{2,0},{3,1},{4,6},{5,7},{6,4},{7,5},{8,10},{9,11},{10,... | collective-permute-start | bytes 196616 | tf_op jit(solution)/shard_map/ppermute | solution.py:476
  89.8 3.1 %collective-permute-done.3 = bf16[2,128,128]{2,1,0:T(8,128)(2,1)S(1)} collective-permute-done((bf16[2,128,128]{2,1,0:T(8,128)(2,1)S(1)}, bf16[2,128,128]{2,1,0:T(8,128)(2,1)S(1)}, u32[]{:S(2)}, u32[]{:S(2)}) %collective-permute-start.3) | collective-permute-done | bytes 65568 | tf_op jit(solution)/shard_map/ppermute | solution.py:476
  92.9 4.7 %collective-permute-start.4 = (bf16[4,128,128]{2,1,0:T(8,128)(2,1)S(1)}, bf16[4,128,128]{2,1,0:T(8,128)(2,1)S(1)}, u32[]{:S(2)}, u32[]{:S(2)}) collective-permute-start(bf16[4,128,128]{2,1,0:T(8,128)(2,1)S(1)} %pad_maximum_fusion.1), channel_id=1, source_target_pairs={{0,1},{1,0},{2,3},{3,2},{4,5},{5,4},{6,7},{7,6},{8,9},{9,8},{10,11... | collective-permute-start | bytes 393224 | tf_op jit(solution)/shard_map/ppermute | solution.py:476
  98.4 5.6 %all-to-all-start.4 = ((f32[8,24,128]{2,1,0:T(8,128)}), f32[8,24,128]{2,1,0:T(8,128)S(1)}, u32[]{:S(2)}, u32[]{:S(2)}) async-start(f32[8,24,128]{2,1,0:T(8,128)} %shard_map.146), calls=%async_computation.4 | async-start | bytes 196608 | tf_op jit(solution)/shard_map/all_to_all | solution.py:493
  104.0 0.9 copy-done
  104.9 1.7 %shard_map.145 = f32[128,128]{1,0:T(8,128)} custom-call(s32[8,8]{1,0:T(8,128)S(1)} %copy-done.3, s32[8,8]{1,0:T(8,128)S(1)} %copy-done.4, bf16[8,128,128]{2,1,0:T(8,128)(2,1)S(1)} %pad_maximum_fusion.arrived_ref, bf16[8,128,128]{2,1,0:T(8,128)(2,1)S(1)} %copy-done), custom_call_target="tpu_custom_call" | custom-call | flops 100000000 | bytes 1000000 | tf_op jit(solution)/shard_map/pallas_call | solution.py:480
  106.7 2.3 %all-to-all-done.4 = f32[8,24,128]{2,1,0:T(8,128)S(1)} async-done(((f32[8,24,128]{2,1,0:T(8,128)}), f32[8,24,128]{2,1,0:T(8,128)S(1)}, u32[]{:S(2)}, u32[]{:S(2)}) %all-to-all-start.4) | async-done | bytes 98336 | tf_op jit(solution)/shard_map/all_to_all | solution.py:493
  109.0 1.1 shard_map.147
  (45 shorter events, 3.8 us)
Async XLA Ops:
  2.8 16.7 %copy-start.2 = (bf16[1,8,16,128]{3,2,1,0:T(8,128)(2,1)S(1)}, bf16[1,8,16,128]{3,2,1,0:T(8,128)(2,1)}, u32[]{:S(2)}) copy-start(bf16[1,8,16,128]{3,2,1,0:T(8,128)(2,1)} %param.20) | copy-start | bytes 98308
  19.5 1.3 %copy-start.6 = (bf16[16,16,3,3,3]{1,0,4,3,2:T(8,128)(2,1)S(1)}, bf16[16,16,3,3,3]{1,0,4,3,2:T(8,128)(2,1)}, u32[]{:S(2)}) copy-start(bf16[16,16,3,3,3]{1,0,4,3,2:T(8,128)(2,1)} %param.15) | copy-start | bytes 41476
  19.6 5.0 %collective-permute-start = (bf16[2,128,128]{2,1,0:T(8,128)(2,1)S(1)}, bf16[2,128,128]{2,1,0:T(8,128)(2,1)S(1)}, u32[]{:S(2)}, u32[]{:S(2)}) collective-permute-start(bf16[2,128,128]{2,1,0:T(8,128)(2,1)S(1)} %shard_map.139.own_ref), channel_id=1, source_target_pairs={{4,20},{5,21},{6,22},{7,23},{16,0},{17,1},{18,2},{19,3},{20,36},{2... | collective-permute-start | bytes 196616 | tf_op jit(solution)/shard_map/ppermute | solution.py:448
  20.9 9.9 %copy-start.5 = (bf16[16,16,3,3,3]{1,0,4,3,2:T(8,128)(2,1)S(1)}, bf16[16,16,3,3,3]{1,0,4,3,2:T(8,128)(2,1)}, u32[]{:S(2)}) copy-start(bf16[16,16,3,3,3]{1,0,4,3,2:T(8,128)(2,1)} %param.16) | copy-start | bytes 41476
  24.6 8.9 %collective-permute-start.1 = (bf16[4,64,128]{2,1,0:T(8,128)(2,1)S(1)}, bf16[4,64,128]{2,1,0:T(8,128)(2,1)S(1)}, u32[]{:S(2)}, u32[]{:S(2)}) collective-permute-start(bf16[4,64,128]{2,1,0:T(8,128)(2,1)S(1)} %shard_map.140), channel_id=1, source_target_pairs={{0,8},{8,0},{1,9},{9,1},{2,10},{10,2},{3,11},{11,3},{4,12},{12,4},... | collective-permute-start | bytes 196616 | tf_op jit(solution)/shard_map/ppermute | solution.py:455
  31.0 0.9 copy-start.7
  34.5 19.2 %all-to-all-start.1 = ((bf16[8,2,192,128]{3,2,1,0:T(8,128)(2,1)}), bf16[8,2,192,128]{3,2,1,0:T(8,128)(2,1)S(1)}, u32[]{:S(2)}, u32[]{:S(2)}) async-start(bf16[8,2,192,128]{3,2,1,0:T(8,128)(2,1)} %shard_map.141), calls=%async_computation.1 | async-start | bytes 1572864 | tf_op jit(solution)/shard_map/all_to_all | solution.py:466
  41.8 0.7 copy-start.8
  41.8 0.7 copy-start.9
  42.4 0.9 copy-start.1
  68.5 29.2 %all-to-all-start.3 = ((bf16[64,24,128]{2,1,0:T(8,128)(2,1)}), bf16[64,24,128]{2,1,0:T(8,128)(2,1)S(1)}, u32[]{:S(2)}, u32[]{:S(2)}) async-start(bf16[64,24,128]{2,1,0:T(8,128)(2,1)} %shard_map.144), calls=%async_computation.3 | async-start | bytes 786432 | tf_op jit(solution)/shard_map/all_to_all | solution.py:477
  81.1 6.5 %collective-permute-start.2 = (bf16[1,128,128]{2,1,0:T(8,128)(2,1)S(1)}, bf16[1,128,128]{2,1,0:T(8,128)(2,1)S(1)}, u32[]{:S(2)}, u32[]{:S(2)}) collective-permute-start(bf16[1,128,128]{2,1,0:T(8,128)(2,1)S(1)} %get-tuple-element.14), channel_id=1, source_target_pairs={{0,4},{1,5},{2,6},{3,7},{4,0},{5,1},{6,2},{7,3},{8,12},{9,13},{10,... | collective-permute-start | bytes 98312 | tf_op jit(solution)/shard_map/ppermute | solution.py:476
  87.6 5.3 %collective-permute-start.3 = (bf16[2,128,128]{2,1,0:T(8,128)(2,1)S(1)}, bf16[2,128,128]{2,1,0:T(8,128)(2,1)S(1)}, u32[]{:S(2)}, u32[]{:S(2)}) collective-permute-start(bf16[2,128,128]{2,1,0:T(8,128)(2,1)S(1)} %pad_maximum_fusion.2), channel_id=1, source_target_pairs={{0,2},{1,3},{2,0},{3,1},{4,6},{5,7},{6,4},{7,5},{8,10},{9,11},{10,... | collective-permute-start | bytes 196616 | tf_op jit(solution)/shard_map/ppermute | solution.py:476
  92.9 11.1 %collective-permute-start.4 = (bf16[4,128,128]{2,1,0:T(8,128)(2,1)S(1)}, bf16[4,128,128]{2,1,0:T(8,128)(2,1)S(1)}, u32[]{:S(2)}, u32[]{:S(2)}) collective-permute-start(bf16[4,128,128]{2,1,0:T(8,128)(2,1)S(1)} %pad_maximum_fusion.1), channel_id=1, source_target_pairs={{0,1},{1,0},{2,3},{3,2},{4,5},{5,4},{6,7},{7,6},{8,9},{9,8},{10,11... | collective-permute-start | bytes 393224 | tf_op jit(solution)/shard_map/ppermute | solution.py:476
  98.4 10.6 %all-to-all-start.4 = ((f32[8,24,128]{2,1,0:T(8,128)}), f32[8,24,128]{2,1,0:T(8,128)S(1)}, u32[]{:S(2)}, u32[]{:S(2)}) async-start(f32[8,24,128]{2,1,0:T(8,128)} %shard_map.146), calls=%async_computation.4 | async-start | bytes 196608 | tf_op jit(solution)/shard_map/all_to_all | solution.py:493
  104.0 0.9 copy-start
  104.0 1.0 copy-start.3
  104.0 1.0 copy-start.4

commit v9 on v7

--- a/solution.py
+++ b/solution.py
@@ -466,12 +466,14 @@
 
     across = ("depth", "height")
     sums = for_each_sum(first_sum_kernel, sums, depths * heights, BF16)
-    sums, lift_grad = lax.optimization_barrier((sums, lift_grad))
+    pieces = lift_grad
     for step in (1, 2, 4):
+        if step == 2:
+            sums, pieces = lax.optimization_barrier((sums, pieces))
         pairs = [(v, v ^ step) for v in range(views)]
-        lift_grad = jnp.concatenate([lift_grad, lax.ppermute(lift_grad, "view", pairs)])
+        pieces = jnp.concatenate([pieces, lax.ppermute(pieces, "view", pairs)])
+    lift_grad = pieces
     sums = lax.all_to_all(sums, across, 0, 0, tiled=True)
-    sums = for_each_sum(next_sum_kernel, sums, views, F32)
 
     camera_grad = pl.pallas_call(
         camera_kernel,
@@ -486,6 +488,8 @@
         ),
     )(tile_bricks, tile_rows, lift_grad, footprint_slot_weights)
 
+    sums, camera_grad = lax.optimization_barrier((sums, camera_grad))
+    sums = for_each_sum(next_sum_kernel, sums, views, F32)
     sums = lax.all_to_all(sums, "view", 0, 0, tiled=True).reshape(12 * C, X)
     scale = 1.0 / math.sqrt(YB * X * depths * heights * views)
     weight_grads, bias_gradient_pair = pl.pallas_call(

time: 111 us -> 112 us (level)
  waiting for transfers between devices: 25.1 us -> 28.7 us
  starting transfers between devices: 41.3 us -> 38.1 us
  blocking collectives: 24.9 us -> 27.3 us
    ppermute x3, waiting for transfers between devices: 3.94 us -> 7.96 us  [body(): pieces = jnp.concatenate([pieces, lax.ppermute(pieces, 'view', pairs)])]
    all_to_all x1, starting transfers between devices: 6.52 us -> 3.32 us  [body(): sums = lax.all_to_all(sums, 'view', 0, 0, tiled=True)]
    all_to_all x1, waiting for transfers between devices: 3.87 us -> 0.91 us  [body(): sums = lax.all_to_all(sums, across, 0, 0, tiled=True)]
    all_to_all x1, waiting for transfers between devices: 2.42 us -> 4.93 us  [body(): sums = lax.all_to_all(sums, 'view', 0, 0, tiled=True)]
    all_to_all x1, blocking collectives: 8.23 us -> 10.6 us  [body(): sums = lax.all_to_all(sums, 'view', 0, 0, tiled=True).reshape(12 * C, X)]
  transfers between devices with their start and end apart: 8 -> 8, of which waited for: 7 -> 7; matrix products, arithmetic and copies ran while one was open for 1% -> 1% of each run, Pallas kernels for 3% -> 2%
where the time goes in v9:
time: 112 us; the launch traced here: 111 us
  starting transfers between devices  38.1 us (34%)
  waiting for transfers between devices  28.7 us (26%)
  blocking collectives  27.3 us (24%)
  Pallas kernels  13.2 us (12%)
  local copies, waits for them, and re-layouts  3.15 us (3%)
    all_to_all x1, blocking collectives, body(): pieces = lax.all_to_all(partial, 'view', 0, 0, tiled=True)  16.7 us
    all_to_all x1, starting transfers between devices, body(): sums = lax.all_to_all(sums, across, 0, 0, tiled=True)  12.7 us
    all_to_all x1, blocking collectives, body(): sums = lax.all_to_all(sums, 'view', 0, 0, tiled=True).reshape(12 * C, X)  10.6 us
    all_to_all x1, waiting for transfers between devices, body(): arrived = lax.all_to_all(parts, 'view', 0, 0, tiled=True)  9.72 us
    ppermute x3, waiting for transfers between devices, body(): pieces = jnp.concatenate([pieces, lax.ppermute(pieces, 'view', pairs)])  7.96 us
    ppermute x3, starting transfers between devices, body(): pieces = jnp.concatenate([pieces, lax.ppermute(pieces, 'view', pairs)])  7.75 us
    all_to_all x1, starting transfers between devices, body(): arrived = lax.all_to_all(parts, 'view', 0, 0, tiled=True)  6.86 us
    ppermute x1, starting transfers between devices, body(): rim = lax.ppermute(facing, 'height', [(0, 1), (1, 0)])  6.23 us
  transfers between devices with their start and end apart: 8, of which 7 were waited for; matrix products, arithmetic and copies ran while one was open for 1% of the time, Pallas kernels for 2%

profile of v9, /device:TPU:1, one launch (start us, length us, event | category | flops | bytes accessed | tf_op | source)
XLA Modules:
  0.0 111.5 jit_solution(17615571747168134408)
XLA Ops:
  0.6 2.2 %shard_map.138 = bf16[8,128,128]{2,1,0:T(8,128)(2,1)} custom-call(s32[8,8]{1,0:T(8,128)} %bricks_ref.1, s32[8,8]{1,0:T(8,128)} %rows_ref.1, bf16[128,128]{1,0:T(8,128)(2,1)} %bitcast.33, bf16[8,128,128]{2,1,0:T(8,128)(2,1)} %weights_ref.1), custom_call_target="tpu_custom_call" | custom-call | flops 100000000 | bytes 1000000 | tf_op jit(solution)/shard_map/pallas_call | solution.py:393
  2.8 16.7 %all_to_all.25.pieces_ref = bf16[8,128,128]{2,1,0:T(8,128)(2,1)S(1)} all-to-all(bf16[8,128,128]{2,1,0:T(8,128)(2,1)} %shard_map.138), channel_id=1, replica_groups=mesh['depth'=32,'height'=2,'view'=8] {'view'}, dimensions={0} | all-to-all | bytes 524288 | tf_op jit(solution)/shard_map/all_to_all | solution.py:413
  19.6 1.3 %collective-permute-start = (bf16[2,128,128]{2,1,0:T(8,128)(2,1)S(1)}, bf16[2,128,128]{2,1,0:T(8,128)(2,1)S(1)}, u32[]{:S(2)}, u32[]{:S(2)}) collective-permute-start(bf16[2,128,128]{2,1,0:T(8,128)(2,1)S(1)} %shard_map.139.own_ref), channel_id=1, source_target_pairs={{4,20},{5,21},{6,22},{7,23},{16,0},{17,1},{18,2},{19,3},{20,36},{2... | collective-permute-start | bytes 196616 | tf_op jit(solution)/shard_map/ppermute | solution.py:444
  20.9 3.7 %collective-permute-done.far_ref = bf16[2,128,128]{2,1,0:T(8,128)(2,1)S(1)} collective-permute-done((bf16[2,128,128]{2,1,0:T(8,128)(2,1)S(1)}, bf16[2,128,128]{2,1,0:T(8,128)(2,1)S(1)}, u32[]{:S(2)}, u32[]{:S(2)}) %collective-permute-start) | collective-permute-done | bytes 65568 | tf_op jit(solution)/shard_map/ppermute | solution.py:444
  24.6 6.2 %collective-permute-start.1 = (bf16[4,64,128]{2,1,0:T(8,128)(2,1)S(1)}, bf16[4,64,128]{2,1,0:T(8,128)(2,1)S(1)}, u32[]{:S(2)}, u32[]{:S(2)}) collective-permute-start(bf16[4,64,128]{2,1,0:T(8,128)(2,1)S(1)} %shard_map.140), channel_id=1, source_target_pairs={{0,8},{8,0},{1,9},{9,1},{2,10},{10,2},{3,11},{11,3},{4,12},{12,4},... | collective-permute-start | bytes 196616 | tf_op jit(solution)/shard_map/ppermute | solution.py:451
  31.1 0.8 copy-done.7
  32.0 1.5 %collective-permute-done.1.rim_ref = bf16[4,64,128]{2,1,0:T(8,128)(2,1)S(1)} collective-permute-done((bf16[4,64,128]{2,1,0:T(8,128)(2,1)S(1)}, bf16[4,64,128]{2,1,0:T(8,128)(2,1)S(1)}, u32[]{:S(2)}, u32[]{:S(2)}) %collective-permute-start.1) | collective-permute-done | bytes 65568 | tf_op jit(solution)/shard_map/ppermute | solution.py:451
  33.5 1.0 shard_map.141
  34.5 6.9 %all-to-all-start.1 = ((bf16[8,2,192,128]{3,2,1,0:T(8,128)(2,1)}), bf16[8,2,192,128]{3,2,1,0:T(8,128)(2,1)S(1)}, u32[]{:S(2)}, u32[]{:S(2)}) async-start(bf16[8,2,192,128]{3,2,1,0:T(8,128)(2,1)} %shard_map.141), calls=%async_computation.1 | async-start | bytes 1572864 | tf_op jit(solution)/shard_map/all_to_all | solution.py:462
  43.9 9.7 %all-to-all-done.1.arrived_ref = bf16[8,2,192,128]{3,2,1,0:T(8,128)(2,1)S(1)} async-done(((bf16[8,2,192,128]{3,2,1,0:T(8,128)(2,1)}), bf16[8,2,192,128]{3,2,1,0:T(8,128)(2,1)S(1)}, u32[]{:S(2)}, u32[]{:S(2)}) %all-to-all-start.1) | async-done | bytes 786464 | tf_op jit(solution)/shard_map/all_to_all | solution.py:462
  53.6 5.9 %shard_map.143 = (bf16[128,128]{1,0:T(8,128)(2,1)}, bf16[1,128,128]{2,1,0:T(8,128)(2,1)S(1)}, bf16[8,48,128]{2,1,0:T(8,128)(2,1)}) custom-call(bf16[8,2,192,128]{3,2,1,0:T(8,128)(2,1)S(1)} %all-to-all-done.1.arrived_ref, bf16[96,1792]{1,0:T(8,128)(2,1)S(1)} %shard_map.142.block_hbm, f32[2,192,1]{2,1,0:T(8,128)S(1)} %copy.23.bias_ref), custom_call_target="tpu_custom_call" | custom-call | flops 10000000000 | bytes 10000000 | tf_op jit(solution)/shard_map/pallas_call | solution.py:338
  59.5 2.8 %collective-permute-start.2 = (bf16[1,128,128]{2,1,0:T(8,128)(2,1)S(1)}, bf16[1,128,128]{2,1,0:T(8,128)(2,1)S(1)}, u32[]{:S(2)}, u32[]{:S(2)}) collective-permute-start(bf16[1,128,128]{2,1,0:T(8,128)(2,1)S(1)} %get-tuple-element.15), channel_id=1, source_target_pairs={{0,1},{1,0},{2,3},{3,2},{4,5},{5,4},{6,7},{7,6},{8,9},{9,8},{10,11... | collective-permute-start | bytes 98312 | tf_op jit(solution)/shard_map/ppermute | solution.py:474
  62.3 3.3 %all-to-all-start.2 = ((bf16[8,48,128]{2,1,0:T(8,128)(2,1)}), bf16[8,48,128]{2,1,0:T(8,128)(2,1)S(1)}, u32[]{:S(2)}, u32[]{:S(2)}) async-start(bf16[8,48,128]{2,1,0:T(8,128)(2,1)} %get-tuple-element.14), calls=%async_computation.2 | async-start | bytes 196608 | tf_op jit(solution)/shard_map/all_to_all | solution.py:465
  65.7 4.9 %all-to-all-done.2.arrived_ref = bf16[8,48,128]{2,1,0:T(8,128)(2,1)S(1)} async-done(((bf16[8,48,128]{2,1,0:T(8,128)(2,1)}), bf16[8,48,128]{2,1,0:T(8,128)(2,1)S(1)}, u32[]{:S(2)}, u32[]{:S(2)}) %all-to-all-start.2) | async-done | bytes 98336 | tf_op jit(solution)/shard_map/all_to_all | solution.py:465
  70.6 0.9 shard_map.144
  71.4 12.7 %all-to-all-start.3 = ((bf16[64,24,128]{2,1,0:T(8,128)(2,1)}), bf16[64,24,128]{2,1,0:T(8,128)(2,1)S(1)}, u32[]{:S(2)}, u32[]{:S(2)}) async-start(bf16[64,24,128]{2,1,0:T(8,128)(2,1)} %shard_map.144), calls=%async_computation.3 | async-start | bytes 786432 | tf_op jit(solution)/shard_map/all_to_all | solution.py:476
  84.1 2.2 %collective-permute-start.3 = (bf16[2,128,128]{2,1,0:T(8,128)(2,1)S(1)}, bf16[2,128,128]{2,1,0:T(8,128)(2,1)S(1)}, u32[]{:S(2)}, u32[]{:S(2)}) collective-permute-start(bf16[2,128,128]{2,1,0:T(8,128)(2,1)S(1)} %pad_maximum_fusion.2), channel_id=1, source_target_pairs={{0,2},{1,3},{2,0},{3,1},{4,6},{5,7},{6,4},{7,5},{8,10},{9,11},{10,... | collective-permute-start | bytes 196616 | tf_op jit(solution)/shard_map/ppermute | solution.py:474
  86.3 3.1 %collective-permute-done.3 = bf16[2,128,128]{2,1,0:T(8,128)(2,1)S(1)} collective-permute-done((bf16[2,128,128]{2,1,0:T(8,128)(2,1)S(1)}, bf16[2,128,128]{2,1,0:T(8,128)(2,1)S(1)}, u32[]{:S(2)}, u32[]{:S(2)}) %collective-permute-start.3) | collective-permute-done | bytes 65568 | tf_op jit(solution)/shard_map/ppermute | solution.py:474
  89.5 2.8 %collective-permute-start.4 = (bf16[4,128,128]{2,1,0:T(8,128)(2,1)S(1)}, bf16[4,128,128]{2,1,0:T(8,128)(2,1)S(1)}, u32[]{:S(2)}, u32[]{:S(2)}) collective-permute-start(bf16[4,128,128]{2,1,0:T(8,128)(2,1)S(1)} %pad_maximum_fusion.1), channel_id=1, source_target_pairs={{0,4},{1,5},{2,6},{3,7},{4,0},{5,1},{6,2},{7,3},{8,12},{9,13},{10,... | collective-permute-start | bytes 393224 | tf_op jit(solution)/shard_map/ppermute | solution.py:474
  92.2 4.9 %collective-permute-done.4 = bf16[4,128,128]{2,1,0:T(8,128)(2,1)S(1)} collective-permute-done((bf16[4,128,128]{2,1,0:T(8,128)(2,1)S(1)}, bf16[4,128,128]{2,1,0:T(8,128)(2,1)S(1)}, u32[]{:S(2)}, u32[]{:S(2)}) %collective-permute-start.4) | collective-permute-done | bytes 131104 | tf_op jit(solution)/shard_map/ppermute | solution.py:474
  97.2 1.6 %shard_map.145 = f32[128,128]{1,0:T(8,128)} custom-call(s32[8,8]{1,0:T(8,128)S(1)} %copy-done.3, s32[8,8]{1,0:T(8,128)S(1)} %copy-done.4, bf16[8,128,128]{2,1,0:T(8,128)(2,1)S(1)} %pad_maximum_fusion.arrived_ref, bf16[8,128,128]{2,1,0:T(8,128)(2,1)S(1)} %copy-done), custom_call_target="tpu_custom_call" | custom-call | flops 100000000 | bytes 1000000 | tf_op jit(solution)/shard_map/pallas_call | solution.py:478
  98.8 0.9 all-to-all-done.3.arrived_ref
  99.8 10.6 %all_to_all.26 = f32[8,24,128]{2,1,0:T(8,128)S(1)} all-to-all(f32[8,24,128]{2,1,0:T(8,128)S(1)} %shard_map.146), channel_id=1, replica_groups=mesh['depth'=32,'height'=2,'view'=8] {'view'}, dimensions={0} | all-to-all | bytes 196608 | tf_op jit(solution)/shard_map/all_to_all | solution.py:493
  110.4 1.1 shard_map.147
  (45 shorter events, 3.1 us)
Async XLA Ops:
  2.8 16.7 %copy-start.2 = (bf16[1,8,16,128]{3,2,1,0:T(8,128)(2,1)S(1)}, bf16[1,8,16,128]{3,2,1,0:T(8,128)(2,1)}, u32[]{:S(2)}) copy-start(bf16[1,8,16,128]{3,2,1,0:T(8,128)(2,1)} %param.20) | copy-start | bytes 98308
  19.5 1.3 %copy-start.6 = (bf16[16,16,3,3,3]{1,0,4,3,2:T(8,128)(2,1)S(1)}, bf16[16,16,3,3,3]{1,0,4,3,2:T(8,128)(2,1)}, u32[]{:S(2)}) copy-start(bf16[16,16,3,3,3]{1,0,4,3,2:T(8,128)(2,1)} %param.15) | copy-start | bytes 41476
  19.6 5.0 %collective-permute-start = (bf16[2,128,128]{2,1,0:T(8,128)(2,1)S(1)}, bf16[2,128,128]{2,1,0:T(8,128)(2,1)S(1)}, u32[]{:S(2)}, u32[]{:S(2)}) collective-permute-start(bf16[2,128,128]{2,1,0:T(8,128)(2,1)S(1)} %shard_map.139.own_ref), channel_id=1, source_target_pairs={{4,20},{5,21},{6,22},{7,23},{16,0},{17,1},{18,2},{19,3},{20,36},{2... | collective-permute-start | bytes 196616 | tf_op jit(solution)/shard_map/ppermute | solution.py:444
  20.9 9.9 %copy-start.5 = (bf16[16,16,3,3,3]{1,0,4,3,2:T(8,128)(2,1)S(1)}, bf16[16,16,3,3,3]{1,0,4,3,2:T(8,128)(2,1)}, u32[]{:S(2)}) copy-start(bf16[16,16,3,3,3]{1,0,4,3,2:T(8,128)(2,1)} %param.16) | copy-start | bytes 41476
  24.6 8.9 %collective-permute-start.1 = (bf16[4,64,128]{2,1,0:T(8,128)(2,1)S(1)}, bf16[4,64,128]{2,1,0:T(8,128)(2,1)S(1)}, u32[]{:S(2)}, u32[]{:S(2)}) collective-permute-start(bf16[4,64,128]{2,1,0:T(8,128)(2,1)S(1)} %shard_map.140), channel_id=1, source_target_pairs={{0,8},{8,0},{1,9},{9,1},{2,10},{10,2},{3,11},{11,3},{4,12},{12,4},... | collective-permute-start | bytes 196616 | tf_op jit(solution)/shard_map/ppermute | solution.py:451
  31.0 0.9 copy-start.7
  34.5 19.2 %all-to-all-start.1 = ((bf16[8,2,192,128]{3,2,1,0:T(8,128)(2,1)}), bf16[8,2,192,128]{3,2,1,0:T(8,128)(2,1)S(1)}, u32[]{:S(2)}, u32[]{:S(2)}) async-start(bf16[8,2,192,128]{3,2,1,0:T(8,128)(2,1)} %shard_map.141), calls=%async_computation.1 | async-start | bytes 1572864 | tf_op jit(solution)/shard_map/all_to_all | solution.py:462
  41.8 0.7 copy-start.8
  41.8 0.7 copy-start.9
  42.4 0.9 copy-start.1
  59.5 6.1 %collective-permute-start.2 = (bf16[1,128,128]{2,1,0:T(8,128)(2,1)S(1)}, bf16[1,128,128]{2,1,0:T(8,128)(2,1)S(1)}, u32[]{:S(2)}, u32[]{:S(2)}) collective-permute-start(bf16[1,128,128]{2,1,0:T(8,128)(2,1)S(1)} %get-tuple-element.15), channel_id=1, source_target_pairs={{0,1},{1,0},{2,3},{3,2},{4,5},{5,4},{6,7},{7,6},{8,9},{9,8},{10,11... | collective-permute-start | bytes 98312 | tf_op jit(solution)/shard_map/ppermute | solution.py:474
  62.3 8.3 %all-to-all-start.2 = ((bf16[8,48,128]{2,1,0:T(8,128)(2,1)}), bf16[8,48,128]{2,1,0:T(8,128)(2,1)S(1)}, u32[]{:S(2)}, u32[]{:S(2)}) async-start(bf16[8,48,128]{2,1,0:T(8,128)(2,1)} %get-tuple-element.14), calls=%async_computation.2 | async-start | bytes 196608 | tf_op jit(solution)/shard_map/all_to_all | solution.py:465
  71.4 28.3 %all-to-all-start.3 = ((bf16[64,24,128]{2,1,0:T(8,128)(2,1)}), bf16[64,24,128]{2,1,0:T(8,128)(2,1)S(1)}, u32[]{:S(2)}, u32[]{:S(2)}) async-start(bf16[64,24,128]{2,1,0:T(8,128)(2,1)} %shard_map.144), calls=%async_computation.3 | async-start | bytes 786432 | tf_op jit(solution)/shard_map/all_to_all | solution.py:476
  84.1 5.3 %collective-permute-start.3 = (bf16[2,128,128]{2,1,0:T(8,128)(2,1)S(1)}, bf16[2,128,128]{2,1,0:T(8,128)(2,1)S(1)}, u32[]{:S(2)}, u32[]{:S(2)}) collective-permute-start(bf16[2,128,128]{2,1,0:T(8,128)(2,1)S(1)} %pad_maximum_fusion.2), channel_id=1, source_target_pairs={{0,2},{1,3},{2,0},{3,1},{4,6},{5,7},{6,4},{7,5},{8,10},{9,11},{10,... | collective-permute-start | bytes 196616 | tf_op jit(solution)/shard_map/ppermute | solution.py:474
  89.4 7.7 %copy-start = (bf16[8,128,128]{2,1,0:T(8,128)(2,1)S(1)}, bf16[8,128,128]{2,1,0:T(8,128)(2,1)}, u32[]{:S(2)}) copy-start(bf16[8,128,128]{2,1,0:T(8,128)(2,1)} %weights_ref.1) | copy-start | bytes 786436
  89.5 7.7 %copy-start.3 = (s32[8,8]{1,0:T(8,128)S(1)}, s32[8,8]{1,0:T(8,128)}, u32[]{:S(2)}) copy-start(s32[8,8]{1,0:T(8,128)} %bricks_ref.1) | copy-start | bytes 772
  89.5 7.7 %copy-start.4 = (s32[8,8]{1,0:T(8,128)S(1)}, s32[8,8]{1,0:T(8,128)}, u32[]{:S(2)}) copy-start(s32[8,8]{1,0:T(8,128)} %rows_ref.1) | copy-start | bytes 772
  89.5 7.6 %collective-permute-start.4 = (bf16[4,128,128]{2,1,0:T(8,128)(2,1)S(1)}, bf16[4,128,128]{2,1,0:T(8,128)(2,1)S(1)}, u32[]{:S(2)}, u32[]{:S(2)}) collective-permute-start(bf16[4,128,128]{2,1,0:T(8,128)(2,1)S(1)} %pad_maximum_fusion.1), channel_id=1, source_target_pairs={{0,4},{1,5},{2,6},{3,7},{4,0},{5,1},{6,2},{7,3},{8,12},{9,13},{10,... | collective-permute-start | bytes 393224 | tf_op jit(solution)/shard_map/ppermute | solution.py:474
